TPU v7x, 32 devices: a whole 2x2x4 slice. The times are simulated.
32 devices in a mesh: dp: 8 (over z, y), mp: 4 (over x, core).
Axes of the slice: x: 2, y: 2, z: 4, core: 2. Of those that a mesh axis runs over, the one named last changes fastest.
Arguments:
- block_input: bfloat16 [8, 2048, 768], P('dp', 'mp'), may hold values from -6 to 6
- out_cotangent: bfloat16 [8, 2048, 768], P('dp', 'mp'), may hold values from -6 to 6
- lengths: int32 [8], P('dp'), may hold values from 1024 to 2048, as said below
- w_qkv: float32 [768, 3, 768], P('dp', None, 'mp'), may hold values from -0.21875 to 0.21875
- w_out: float32 [768, 768], P('mp', 'dp'), may hold values from -1.75 to 1.75
- w_up: float32 [768, 3072], P('dp', 'mp'), may hold values from -0.21875 to 0.21875
- w_down: float32 [3072, 768], P('mp', 'dp'), may hold values from -0.109375 to 0.109375
- pair_bias: float32 [2048, 256], P(('dp', 'mp')), may hold values from -1.5 to 1.5
- norm_gains: float32 [2, 768], replicated, may hold values from 0.5 to 1.5
- first_qkv: float32 [768, 3, 768], P('dp', None, 'mp'), may hold values from -0.625 to 0.625
- first_out: float32 [768, 768], P('mp', 'dp'), may hold values from -0.125 to 0.125
- first_up: float32 [768, 3072], P('dp', 'mp'), may hold values from -0.625 to 0.625
- first_down: float32 [3072, 768], P('mp', 'dp'), may hold values from -0.625 to 0.625
- first_bias: float32 [2048, 256], P(('dp', 'mp')), may hold values from -0.03125 to 0.03125
- first_gains: float32 [2, 768], replicated, may hold values from -0.625 to 0.625
- second_qkv: float32 [768, 3, 768], P('dp', None, 'mp'), may hold values from 0.002 to 0.03
- second_out: float32 [768, 768], P('mp', 'dp'), may hold values from 0.0001 to 0.0015
- second_up: float32 [768, 3072], P('dp', 'mp'), may hold values from 0.002 to 0.03
- second_down: float32 [3072, 768], P('mp', 'dp'), may hold values from 0.002 to 0.03
- second_bias: float32 [2048, 256], P(('dp', 'mp')), may hold values from 5e-05 to 0.00075
- second_gains: float32 [2, 768], replicated, may hold values from 0.002 to 0.03
Outputs:
- block_output: bfloat16 [8, 2048, 768], P('dp', 'mp')
- grad_input: float32 [8, 2048, 768], P('dp', 'mp')
- grad_qkv: float32 [768, 3, 768], P('dp', None, 'mp')
- grad_out: float32 [768, 768], P('mp', 'dp')
- grad_up: float32 [768, 3072], P('dp', 'mp')
- grad_down: float32 [3072, 768], P('mp', 'dp')
- grad_bias: float32 [2048, 256], P(('dp', 'mp'))
- grad_gains: float32 [2, 768], replicated
- newfirst_qkv: float32 [768, 3, 768], P('dp', None, 'mp')
- newfirst_out: float32 [768, 768], P('mp', 'dp')
- newfirst_up: float32 [768, 3072], P('dp', 'mp')
- newfirst_down: float32 [3072, 768], P('mp', 'dp')
- newfirst_bias: float32 [2048, 256], P(('dp', 'mp'))
- newfirst_gains: float32 [2, 768], replicated
- newsecond_qkv: float32 [768, 3, 768], P('dp', None, 'mp')
- newsecond_out: float32 [768, 768], P('mp', 'dp')
- newsecond_up: float32 [768, 3072], P('dp', 'mp')
- newsecond_down: float32 [3072, 768], P('mp', 'dp')
- newsecond_bias: float32 [2048, 256], P(('dp', 'mp'))
- newsecond_gains: float32 [2, 768], replicated
- update_qkv: float32 [768, 3, 768], P('dp', None, 'mp')
- update_out: float32 [768, 768], P('mp', 'dp')
- update_up: float32 [768, 3072], P('dp', 'mp')
- update_down: float32 [3072, 768], P('mp', 'dp')
- update_bias: float32 [2048, 256], P(('dp', 'mp'))
- update_gains: float32 [2, 768], replicated
- rms_stats: float32 [3], replicated
Inputs may be any that keep to these rules, and one draw needn't show every extreme that they name: `lengths`: every length is at least half of 2048, and one of them is exactly 2048.
All inputs are finite; a program needn't handle non-finite values.
Results may differ from a plain program's by a relative error of at most 0.012.
Values may be sent and summed in bfloat16 or wider, within the bound.
A program may use at most 192 MiB of HBM per device.

v0:
```python
import jax
import jax.numpy as jnp
from jax import lax
from jax.sharding import PartitionSpec as P

LEN = 2048
ADAM_STEP = 10


EPS = 1e-06
BETA_ONE = 0.9
BETA_TWO = 0.99
LEARN_RATE = 0.03
WEIGHT_DECAY = 0.1
ADAM_EPS = 1e-08


def skew_band(bias_rows):
    height, width = bias_rows.shape
    padded = jnp.concatenate(
        [
            jnp.zeros((height, 1), bias_rows.dtype),
            bias_rows[:, ::-1],
            jnp.zeros((height, height), bias_rows.dtype),
        ],
        axis=1,
    )
    return padded.reshape(-1)[: height * (height + width)].reshape(height, height + width)


def unskew_band(band_grad, window):
    height, width = band_grad.shape
    flat = jnp.concatenate([band_grad.reshape(-1), jnp.zeros((height,), band_grad.dtype)])
    return flat.reshape(height, width + 1)[:, 1 : window + 1][:, ::-1]


def mix_forward(queries, key_rows, value_rows, bias_low):
    seq_len, channels = queries.shape
    window = bias_low.shape[1]
    block = min(512, seq_len)
    exp_keys = jnp.exp(key_rows)
    front = jnp.zeros((window, channels), jnp.bfloat16)
    keys_pad = jnp.concatenate([front, exp_keys.astype(jnp.bfloat16)], axis=0)
    product_pad = jnp.concatenate([front, (exp_keys * value_rows).astype(jnp.bfloat16)], axis=0)

    def one_block(block_index):
        offset = block_index * block
        band_rows = skew_band(lax.dynamic_slice_in_dim(bias_low, offset, block, 0))
        key_block = lax.dynamic_slice_in_dim(keys_pad, offset, block + window, 0)
        product_block = lax.dynamic_slice_in_dim(product_pad, offset, block + window, 0)
        numerator = jnp.dot(band_rows, product_block, preferred_element_type=jnp.float32)
        denominator = jnp.dot(band_rows, key_block, preferred_element_type=jnp.float32)
        return (numerator, denominator)

    numerator, denominator = lax.map(one_block, jnp.arange(seq_len // block, dtype=jnp.int32))
    return (
        numerator.reshape(seq_len, channels),
        denominator.reshape(seq_len, channels),
        keys_pad,
        product_pad,
    )


def mix_backward(
    queries,
    key_rows,
    value_rows,
    numerator,
    denominator,
    keys_pad,
    product_pad,
    bias_low,
    grad_mixed,
):
    seq_len, channels = queries.shape
    window = bias_low.shape[1]
    block = min(512, seq_len)
    gate_sig = jax.nn.sigmoid(queries)
    mixed_ratio = numerator / denominator
    grad_query = grad_mixed * mixed_ratio * gate_sig * (1.0 - gate_sig)
    grad_numerator = (grad_mixed * gate_sig / denominator).astype(jnp.bfloat16)
    grad_denominator = (-grad_mixed * gate_sig * mixed_ratio / denominator).astype(jnp.bfloat16)

    def one_block(carry, block_index):
        product_sum, key_sum = carry
        offset = block_index * block
        band_rows = skew_band(lax.dynamic_slice_in_dim(bias_low, offset, block, 0))
        key_block = lax.dynamic_slice_in_dim(keys_pad, offset, block + window, 0)
        product_block = lax.dynamic_slice_in_dim(product_pad, offset, block + window, 0)
        upper_block = lax.dynamic_slice_in_dim(grad_numerator, offset, block, 0)
        lower_block = lax.dynamic_slice_in_dim(grad_denominator, offset, block, 0)
        product_part = jnp.einsum(
            "ij,ic->jc", band_rows, upper_block, preferred_element_type=jnp.float32
        )
        key_part = jnp.einsum(
            "ij,ic->jc", band_rows, lower_block, preferred_element_type=jnp.float32
        )
        product_sum = lax.dynamic_update_slice_in_dim(
            product_sum,
            lax.dynamic_slice_in_dim(product_sum, offset, block + window, 0) + product_part,
            offset,
            0,
        )
        key_sum = lax.dynamic_update_slice_in_dim(
            key_sum,
            lax.dynamic_slice_in_dim(key_sum, offset, block + window, 0) + key_part,
            offset,
            0,
        )
        band_grad = jnp.einsum(
            "ic,jc->ij", upper_block, product_block, preferred_element_type=jnp.float32
        )
        band_grad = band_grad + jnp.einsum(
            "ic,jc->ij", lower_block, key_block, preferred_element_type=jnp.float32
        )
        return ((product_sum, key_sum), unskew_band(band_grad, window))

    zeros_pad = jnp.zeros((seq_len + window, channels), jnp.float32)
    sums_pad, bias_blocks = lax.scan(
        one_block, (zeros_pad, zeros_pad), jnp.arange(seq_len // block, dtype=jnp.int32)
    )
    exp_keys = jnp.exp(key_rows)
    grad_product = sums_pad[0][window:]
    grad_keyexp = sums_pad[1][window:] + grad_product * value_rows
    grad_value = grad_product * exp_keys
    grad_key = grad_keyexp * exp_keys
    return (grad_query, grad_key, grad_value, bias_blocks.reshape(seq_len, window))


def rms_rescale(inputs):
    return lax.rsqrt(jnp.mean(inputs * inputs, axis=-1, keepdims=True) + EPS)


def norm_back(inputs, rescale, gain, grad_normed):
    scaled = grad_normed * gain
    grad_inputs = rescale * scaled - inputs * rescale * rescale * rescale * jnp.mean(
        scaled * inputs, axis=-1, keepdims=True
    )
    grad_gain = jnp.sum(grad_normed * inputs * rescale, axis=(0, 1))
    return (grad_inputs, grad_gain)


def gelu_tanh(pre_act):
    return jax.nn.gelu(pre_act, approximate=True)


def adam_step(param, grad, first, second, step_value, decay):
    new_first = BETA_ONE * first + (1.0 - BETA_ONE) * grad
    new_second = BETA_TWO * second + (1.0 - BETA_TWO) * grad * grad
    first_hat = new_first / (1.0 - jnp.power(jnp.float32(BETA_ONE), step_value))
    second_hat = new_second / (1.0 - jnp.power(jnp.float32(BETA_TWO), step_value))
    update = -LEARN_RATE * (first_hat / (jnp.sqrt(second_hat) + ADAM_EPS) + decay * param)
    return (new_first, new_second, update)


def shards(
    block_input,
    out_cotangent,
    lengths,
    w_qkv,
    w_out,
    w_up,
    w_down,
    pair_bias,
    norm_gains,
    first_qkv,
    first_out,
    first_up,
    first_down,
    first_bias,
    first_gains,
    second_qkv,
    second_out,
    second_up,
    second_down,
    second_bias,
    second_gains,
):
    query_weights, mixer_weights, hidden_weights, back_weights = (
        lax.all_gather(w_qkv.astype(jnp.bfloat16), "dp", axis=0, tiled=True),
        lax.all_gather(w_out.astype(jnp.bfloat16), "dp", axis=1, tiled=True),
        lax.all_gather(w_up.astype(jnp.bfloat16), "dp", axis=0, tiled=True),
        lax.all_gather(w_down.astype(jnp.bfloat16), "dp", axis=1, tiled=True),
    )
    bias_full = lax.all_gather(pair_bias, ("dp", "mp"), axis=0, tiled=True)
    exp_bias = jnp.exp(bias_full)
    bias_low = exp_bias.astype(jnp.bfloat16)
    seqs, quarter, width = block_input.shape
    dp_count = lax.axis_size("dp")
    positions = lax.axis_index("mp") * quarter + jnp.arange(quarter, dtype=jnp.int32)
    valid_mask = (positions[None, :] < lengths[:, None]).astype(jnp.float32)
    input_float = block_input.astype(jnp.float32)
    rescale_one = rms_rescale(input_float)
    normed_one = (input_float * rescale_one * norm_gains[0]).astype(jnp.bfloat16)
    full_one = lax.all_gather(normed_one, "mp", axis=1, tiled=True)
    projected = jnp.einsum(
        "std,dkc->stkc", full_one, query_weights, preferred_element_type=jnp.float32
    )
    queries = projected[:, :, 0]
    key_rows = projected[:, :, 1]
    value_rows = projected[:, :, 2]
    numerator, denominator, keys_pad, product_pad = jax.vmap(mix_forward, in_axes=(0, 0, 0, None))(
        queries, key_rows, value_rows, bias_low
    )
    mixed_low = (jax.nn.sigmoid(queries) * numerator / denominator).astype(jnp.bfloat16)
    attn_terms = jnp.einsum(
        "stc,cd->std", mixed_low, mixer_weights, preferred_element_type=jnp.float32
    )
    attn_rows = lax.psum_scatter(attn_terms, "mp", scatter_dimension=1, tiled=True)
    resid = input_float + attn_rows
    rescale_two = rms_rescale(resid)
    normed_two = (resid * rescale_two * norm_gains[1]).astype(jnp.bfloat16)
    full_two = lax.all_gather(normed_two, "mp", axis=1, tiled=True)
    pre_act = jnp.einsum(
        "std,df->stf", full_two, hidden_weights, preferred_element_type=jnp.float32
    )
    act_low = gelu_tanh(pre_act).astype(jnp.bfloat16)
    ffn_terms = jnp.einsum("stf,fd->std", act_low, back_weights, preferred_element_type=jnp.float32)
    ffn_rows = lax.psum_scatter(
        ffn_terms.astype(jnp.bfloat16), "mp", scatter_dimension=1, tiled=True
    ).astype(jnp.float32)
    block_output = (resid + ffn_rows).astype(jnp.bfloat16)
    cotangent = out_cotangent.astype(jnp.float32) * valid_mask[:, :, None]
    cot_low = cotangent.astype(jnp.bfloat16)
    grad_full = lax.all_gather(cot_low, "mp", axis=1, tiled=True)
    grad_act = jnp.einsum(
        "std,fd->stf", grad_full, back_weights, preferred_element_type=jnp.float32
    )
    grad_pre = jax.vjp(gelu_tanh, pre_act)[1](grad_act)[0].astype(jnp.bfloat16)
    normed_terms = jnp.einsum(
        "stf,df->std", grad_pre, hidden_weights, preferred_element_type=jnp.float32
    )
    grad_normed_two = lax.psum_scatter(normed_terms, "mp", scatter_dimension=1, tiled=True)
    grad_up_local = jnp.einsum(
        "std,stf->df", full_two, grad_pre, preferred_element_type=jnp.float32
    )
    grad_down_local = jnp.einsum(
        "stf,std->fd", act_low, grad_full, preferred_element_type=jnp.float32
    )
    grad_resid_norm, gain_two_grad = norm_back(resid, rescale_two, norm_gains[1], grad_normed_two)
    grad_resid = cotangent + grad_resid_norm
    resid_full = lax.all_gather(grad_resid.astype(jnp.bfloat16), "mp", axis=1, tiled=True)
    grad_mixed = jnp.einsum(
        "std,cd->stc", resid_full, mixer_weights, preferred_element_type=jnp.float32
    )
    grad_mixer = jnp.einsum(
        "stc,std->cd", mixed_low, resid_full, preferred_element_type=jnp.float32
    )
    grad_query, grad_key, grad_value, bias_parts = jax.vmap(
        mix_backward, in_axes=(0, 0, 0, 0, 0, 0, 0, None, 0)
    )(
        queries,
        key_rows,
        value_rows,
        numerator,
        denominator,
        keys_pad,
        product_pad,
        bias_low,
        grad_mixed,
    )
    grad_bias_local = jnp.sum(bias_parts, axis=0) * exp_bias
    grad_proj = jnp.stack([grad_query, grad_key, grad_value], axis=2).astype(jnp.bfloat16)
    input_terms = jnp.einsum(
        "stkc,dkc->std", grad_proj, query_weights, preferred_element_type=jnp.float32
    )
    grad_normed_one = lax.psum_scatter(
        input_terms.astype(jnp.bfloat16), "mp", scatter_dimension=1, tiled=True
    ).astype(jnp.float32)
    grad_projection = jnp.einsum(
        "std,stkc->dkc", full_one, grad_proj, preferred_element_type=jnp.float32
    )
    grad_input_norm, gain_one_grad = norm_back(
        input_float, rescale_one, norm_gains[0], grad_normed_one
    )
    grad_input = grad_resid + grad_input_norm
    owned_qkv, owned_out, owned_up, owned_down = (
        lax.psum_scatter(grad_projection, "dp", scatter_dimension=0, tiled=True),
        lax.psum_scatter(grad_mixer, "dp", scatter_dimension=1, tiled=True),
        lax.psum_scatter(grad_up_local, "dp", scatter_dimension=0, tiled=True),
        lax.psum_scatter(grad_down_local, "dp", scatter_dimension=1, tiled=True),
    )
    owned_bias = lax.psum_scatter(grad_bias_local, ("dp", "mp"), scatter_dimension=0, tiled=True)
    mask_cols = valid_mask[:, :, None]
    local_sums = jnp.stack(
        [
            jnp.sum(mask_cols * input_float * input_float),
            jnp.sum(mask_cols * attn_rows * attn_rows),
            jnp.sum(mask_cols * ffn_rows * ffn_rows),
            jnp.sum(valid_mask),
        ]
    )
    gain_grads, global_sums = lax.psum(
        (jnp.stack([gain_one_grad, gain_two_grad]), local_sums), ("dp", "mp")
    )
    grad_scale = float(seqs * dp_count * LEN) ** (-0.5)
    scaled = [
        owned_qkv * grad_scale,
        owned_out * grad_scale,
        owned_up * grad_scale,
        owned_down * grad_scale,
        owned_bias * grad_scale,
        gain_grads * grad_scale,
    ]
    params = (w_qkv, w_out, w_up, w_down, pair_bias, norm_gains)
    firsts = (first_qkv, first_out, first_up, first_down, first_bias, first_gains)
    seconds = (second_qkv, second_out, second_up, second_down, second_bias, second_gains)
    decays = (WEIGHT_DECAY, WEIGHT_DECAY, WEIGHT_DECAY, WEIGHT_DECAY, 0.0, 0.0)
    step_value = jnp.float32(ADAM_STEP)
    states = [
        adam_step(
            params[place], scaled[place], firsts[place], seconds[place], step_value, decays[place]
        )
        for place in range(6)
    ]
    rms_stats = jnp.sqrt(global_sums[:3] / (global_sums[3] * width))
    return (
        block_output,
        grad_input,
        scaled[0],
        scaled[1],
        scaled[2],
        scaled[3],
        scaled[4],
        scaled[5],
        states[0][0],
        states[1][0],
        states[2][0],
        states[3][0],
        states[4][0],
        states[5][0],
        states[0][1],
        states[1][1],
        states[2][1],
        states[3][1],
        states[4][1],
        states[5][1],
        states[0][2],
        states[1][2],
        states[2][2],
        states[3][2],
        states[4][2],
        states[5][2],
        rms_stats,
    )


def solution(mesh):
    placed = (
        P("dp", "mp", None),
        P("dp", "mp", None),
        P("dp"),
        P("dp", None, "mp"),
        P("mp", "dp"),
        P("dp", "mp"),
        P("mp", "dp"),
        P(("dp", "mp"), None),
        P(),
        P("dp", None, "mp"),
        P("mp", "dp"),
        P("dp", "mp"),
        P("mp", "dp"),
        P(("dp", "mp"), None),
        P(),
        P("dp", None, "mp"),
        P("mp", "dp"),
        P("dp", "mp"),
        P("mp", "dp"),
        P(("dp", "mp"), None),
        P(),
    )
    return jax.shard_map(
        shards,
        mesh=mesh,
        in_specs=placed,
        out_specs=(
            P("dp", "mp", None),
            P("dp", "mp", None),
            P("dp", None, "mp"),
            P("mp", "dp"),
            P("dp", "mp"),
            P("mp", "dp"),
            P(("dp", "mp"), None),
            P(),
            P("dp", None, "mp"),
            P("mp", "dp"),
            P("dp", "mp"),
            P("mp", "dp"),
            P(("dp", "mp"), None),
            P(),
            P("dp", None, "mp"),
            P("mp", "dp"),
            P("dp", "mp"),
            P("mp", "dp"),
            P(("dp", "mp"), None),
            P(),
            P("dp", None, "mp"),
            P("mp", "dp"),
            P("dp", "mp"),
            P("mp", "dp"),
            P(("dp", "mp"), None),
            P(),
            P(),
        ),
        check_vma=False,
    )
```

profile of v0, /device:TPU:4, one launch (start us, length us, event | category | flops | bytes accessed | tf_op | source)
XLA Modules:
  0.0 1116.9 jit_solution(440134953824008164)
XLA Ops:
  13.6 38.0 %all_gather.28 = bf16[768,3,192]{2,1,0:T(4,128)(2,1)S(1)} all-gather(bf16[96,3,192]{2,1,0:T(4,128)(2,1)S(1)} %copy.88), channel_id=1, replica_groups=mesh['dp'=8,'mp'=4] {'dp'}, dimensions={0}, use_global_device_ids=true | all-gather | bytes 995328 | tf_op jit(solution)/shard_map/all_gather | solution.py:180
  52.6 31.4 %all_gather.30 = bf16[192,768]{0,1:T(8,128)(2,1)S(1)} all-gather(bf16[192,96]{0,1:T(8,128)(2,1)S(1)} %copy.94), channel_id=1, replica_groups=mesh['dp'=8,'mp'=4] {'dp'}, dimensions={1}, use_global_device_ids=true | all-gather | bytes 331776 | tf_op jit(solution)/shard_map/all_gather | solution.py:181
  87.0 16.9 %all-gather.8.cloned.1.call-done = bf16[1,2048,768]{2,1,0:T(8,128)(2,1)} async-done(((bf16[1,512,768]{2,1,0:T(8,128)(2,1)}), bf16[1,2048,768]{2,1,0:T(8,128)(2,1)}) %all-gather.8.cloned.1.call-update) | async-done | bytes 3145744 | tf_op jit(solution)/shard_map/all_gather | solution.py:195
  114.1 40.1 %while.36 = (s32[]{:T(128)}, f32[4,1,512,192]{2,3,1,0:T(8,128)}, f32[4,1,512,192]{2,3,1,0:T(8,128)}, s32[4]{0:T(128)S(1)}, bf16[2048,256]{1,0:T(8,128)(2,1)}, /*...) while((s32[]{:T(128)}, f32[4,1,512,192]{2,3,1,0:T(8,128)}, ...), condition=%wide.region_2.3_spmd, body=%wide.region_1.2_spmd.sunk | while | flops 304352256 | bytes 9974028 | solution.py:55
  168.7 56.4 %reduce-scatter.12.cloned.1.call-done = f32[1,512,768]{2,1,0:T(8,128)} async-done(((f32[1,2048,768]{2,1,0:T(8,128)}), f32[1,512,768]{2,1,0:T(8,128)}) %reduce-scatter.12.cloned.1.call-update) | async-done | bytes 1572880 | tf_op jit(solution)/shard_map/reduce_scatter | solution.py:209
  229.9 26.6 %all-gather.12.cloned.1.call-done = bf16[1,2048,768]{2,1,0:T(8,128)(2,1)} async-done(((bf16[1,512,768]{2,1,0:T(8,128)(2,1)}), bf16[1,2048,768]{2,1,0:T(8,128)(2,1)}) %all-gather.12.cloned.1.call-update) | async-done | bytes 3145744 | tf_op jit(solution)/shard_map/all_gather | solution.py:213
  263.9 22.4 %all-gather.18.cloned.1.call-done = bf16[1,2048,768]{2,1,0:T(8,128)(2,1)} async-done(((bf16[1,512,768]{2,1,0:T(8,128)(2,1)}), bf16[1,2048,768]{2,1,0:T(8,128)(2,1)}) %all-gather.18.cloned.1.call-update) | async-done | bytes 3145744 | tf_op jit(solution)/shard_map/all_gather | solution.py:225
  294.6 68.3 %reduce-scatter.24.cloned.1.call-done = f32[768,96]{0,1:T(8,128)} async-done(((f32[768,768]{0,1:T(8,128)}), f32[768,96]{0,1:T(8,128)}) %reduce-scatter.24.cloned.1.call-update) | async-done | bytes 294928 | tf_op jit(solution)/shard_map/reduce_scatter | solution.py:281
  365.2 41.3 %all-gather.16.cloned.1.call-done = bf16[768,768]{0,1:T(8,128)(2,1)} async-done(((bf16[768,96]{0,1:T(8,128)(2,1)}), bf16[768,768]{0,1:T(8,128)(2,1)}) %all-gather.16.cloned.1.call-update) | async-done | bytes 1179664 | tf_op jit(solution)/shard_map/all_gather | solution.py:183
  406.5 8.2 fusion.37
  422.3 8.6 fusion.54
  431.0 47.8 %reduce-scatter.16.cloned.1.call-done = f32[1,512,768]{2,1,0:T(8,128)} async-done(((f32[1,2048,768]{2,1,0:T(8,128)}), f32[1,512,768]{2,1,0:T(8,128)}) %reduce-scatter.16.cloned.1.call-update) | async-done | bytes 1572880 | tf_op jit(solution)/shard_map/reduce_scatter | solution.py:233
  481.2 37.8 %reduce-scatter.14.cloned.1.call-done = bf16[1,512,768]{2,1,0:T(8,128)(2,1)} async-done(((bf16[1,2048,768]{2,1,0:T(8,128)(2,1)}), bf16[1,512,768]{2,1,0:T(8,128)(2,1)}) %reduce-scatter.14.cloned.1.call-update) | async-done | bytes 786448 | tf_op jit(solution)/shard_map/reduce_scatter | solution.py:219
  536.8 16.3 %all-gather.20.cloned.1.call-done = bf16[1,2048,768]{2,1,0:T(8,128)(2,1)} async-done(((bf16[1,512,768]{2,1,0:T(8,128)(2,1)}), bf16[1,2048,768]{2,1,0:T(8,128)(2,1)}) %all-gather.20.cloned.1.call-update) | async-done | bytes 3145744 | tf_op jit(solution)/shard_map/all_gather | solution.py:242
  564.0 186.5 %while.37 = (s32[]{:T(128)}, f32[1,2304,192]{1,2,0:T(8,128)}, f32[1,2304,192]{1,2,0:T(8,128)}, f32[4,1,512,256]{3,2,1,0:T(8,128)}, s32[4]{0:T(128)S(1)}, /*index...) while((s32[]{:T(128)}, f32[1,2304,192]{1,2,0:T(8,128)}, ...), condition=%wide.region_10.11_spmd, body=%wide.region_8.10_spmd.sunk | while | flops 607325184 | bytes 47336400 | solution.py:119
  570.7 16.3 %pad_reduce_fusion.2 = f32[393728]{0:T(1024)S(1)} fusion(f32[1,393216]{1,0:T(1,128)S(1)} %bitcast.305), kind=kLoop, calls=%fused_computation.13.clone.1 | loop fusion | bytes 3147776 | tf_op jit(solution)/shard_map/vmap()/while/body/eval_jaxpr/concatenate | solution.py:33
  618.1 16.3 %pad_reduce_fusion.2 = f32[393728]{0:T(1024)S(1)} fusion(f32[1,393216]{1,0:T(1,128)S(1)} %bitcast.305), kind=kLoop, calls=%fused_computation.13.clone.1 | loop fusion | bytes 3147776 | tf_op jit(solution)/shard_map/vmap()/while/body/eval_jaxpr/concatenate | solution.py:33
  665.5 16.3 %pad_reduce_fusion.2 = f32[393728]{0:T(1024)S(1)} fusion(f32[1,393216]{1,0:T(1,128)S(1)} %bitcast.305), kind=kLoop, calls=%fused_computation.13.clone.1 | loop fusion | bytes 3147776 | tf_op jit(solution)/shard_map/vmap()/while/body/eval_jaxpr/concatenate | solution.py:33
  712.1 16.3 %pad_reduce_fusion.2 = f32[393728]{0:T(1024)S(1)} fusion(f32[1,393216]{1,0:T(1,128)S(1)} %bitcast.305), kind=kLoop, calls=%fused_computation.13.clone.1 | loop fusion | bytes 3147776 | tf_op jit(solution)/shard_map/vmap()/while/body/eval_jaxpr/concatenate | solution.py:33
  774.3 38.6 %reduce-scatter.28.cloned.1.call-done = f32[96,192]{1,0:T(8,128)} async-done(((f32[768,192]{1,0:T(8,128)}), f32[96,192]{1,0:T(8,128)}) %reduce-scatter.28.cloned.1.call-update) | async-done | bytes 73744
  814.8 69.3 %reduce-scatter.20.cloned.1.call-done = f32[96,3,192]{2,0,1:T(8,128)} async-done(((f32[768,3,192]{2,0,1:T(8,128)}), f32[96,3,192]{2,0,1:T(8,128)}) %reduce-scatter.20.cloned.1.call-update) | async-done | bytes 221200 | tf_op jit(solution)/shard_map/reduce_scatter | solution.py:278
  886.2 126.3 %reduce-scatter.26.cloned.1.call-done = f32[64,256]{1,0:T(8,128)} async-done(((f32[2048,256]{1,0:T(8,128)}), f32[64,256]{1,0:T(8,128)}) %reduce-scatter.26.cloned.1.call-update) | async-done | bytes 65552 | tf_op jit(solution)/shard_map/reduce_scatter | solution.py:283
  1014.1 44.7 %reduce-scatter.18.cloned.1.call-done = bf16[1,512,768]{2,1,0:T(8,128)(2,1)} async-done(((bf16[1,2048,768]{2,1,0:T(8,128)(2,1)}), bf16[1,512,768]{2,1,0:T(8,128)(2,1)}) %reduce-scatter.18.cloned.1.call-update) | async-done | bytes 786448 | tf_op jit(solution)/shard_map/reduce_scatter | solution.py:267
  1064.2 40.2 %all-reduce.3 = (f32[2,768]{1,0:T(2,128)S(1)}, f32[4]{0:T(128)S(1)}) all-reduce(f32[2,768]{1,0:T(2,128)S(1)} %pad_maximum_fusion.3, f32[4]{0:T(128)S(1)} %pad_maximum_fusion.4), channel_id=1, replica_groups=mesh['dp'=8,'mp'=4] {'dp','mp'}, use_global_device_ids=true, to_apply=%region_20.21 | all-reduce | flops 1540 | bytes 12320 | tf_op jit(solution)/shard_map/psum | solution.py:293
  (375 shorter events, 288.7 us)
Async XLA Ops:
  8.0 76.0 %all-gather.10.cloned.1.call-start = ((), (), s32[]{:S(2)}) async-start(), calls=%async_computation.10 | async-start | bytes 2162688 | tf_op jit(solution)/shard_map/all_gather | solution.py:185
  8.8 95.1 %all-gather.8.cloned.1.call-start = ((), (), s32[]{:S(2)}) async-start(), calls=%async_computation.9 | async-start | bytes 3932160 | tf_op jit(solution)/shard_map/all_gather | solution.py:195
  13.4 211.8 %reduce-scatter.12.cloned.1.call-start = ((), (), s32[]{:S(2)}) async-start(), calls=%async_computation.11 | async-start | bytes 7864320 | tf_op jit(solution)/shard_map/reduce_scatter | solution.py:209
  166.5 63.3 %all-gather.14.cloned.1.call-start = ((), (), s32[]{:S(2)}) async-start(), calls=%async_computation.13 | async-start | bytes 1327104 | tf_op jit(solution)/shard_map/all_gather | solution.py:182
  168.2 88.2 %all-gather.12.cloned.1.call-start = ((), (), s32[]{:S(2)}) async-start(), calls=%async_computation.12 | async-start | bytes 3932160 | tf_op jit(solution)/shard_map/all_gather | solution.py:213
  227.9 58.4 %all-gather.18.cloned.1.call-start = ((), (), s32[]{:S(2)}) async-start(), calls=%async_computation.16 | async-start | bytes 3932160 | tf_op jit(solution)/shard_map/all_gather | solution.py:225
  229.8 133.1 %reduce-scatter.24.cloned.1.call-start = ((), (), s32[]{:S(2)}) async-start(), calls=%async_computation.22 | async-start | bytes 2654208 | tf_op jit(solution)/shard_map/reduce_scatter | solution.py:281
  294.6 111.9 %all-gather.16.cloned.1.call-start = ((), (), s32[]{:S(2)}) async-start(), calls=%async_computation.14 | async-start | bytes 1327104 | tf_op jit(solution)/shard_map/all_gather | solution.py:183
  365.1 113.7 %reduce-scatter.16.cloned.1.call-start = ((), (), s32[]{:S(2)}) async-start(), calls=%async_computation.17 | async-start | bytes 7864320 | tf_op jit(solution)/shard_map/reduce_scatter | solution.py:233
  421.1 98.0 %reduce-scatter.14.cloned.1.call-start = ((), (), s32[]{:S(2)}) async-start(), calls=%async_computation.15 | async-start | bytes 3932160 | tf_op jit(solution)/shard_map/reduce_scatter | solution.py:219
  430.9 122.2 %all-gather.20.cloned.1.call-start = ((), (), s32[]{:S(2)}) async-start(), calls=%async_computation.18 | async-start | bytes 3932160 | tf_op jit(solution)/shard_map/all_gather | solution.py:242
  524.4 247.4 %reduce-scatter.22.cloned.1.call-start = ((), (), s32[]{:S(2)}) async-start(), calls=%async_computation.21 | async-start | bytes 2654208 | tf_op jit(solution)/shard_map/reduce_scatter | solution.py:280
  536.7 276.2 %reduce-scatter.28.cloned.1.call-start = ((), (), s32[]{:S(2)}) async-start(), calls=%async_computation.24 | async-start | bytes 884736
  750.5 133.5 %reduce-scatter.20.cloned.1.call-start = ((), (), s32[]{:S(2)}) async-start(), calls=%async_computation.20 | async-start | bytes 2654208 | tf_op jit(solution)/shard_map/reduce_scatter | solution.py:278
  759.4 253.1 %reduce-scatter.26.cloned.1.call-start = ((), (), s32[]{:S(2)}) async-start(), calls=%async_computation.23 | async-start | bytes 2162688 | tf_op jit(solution)/shard_map/reduce_scatter | solution.py:283
  764.3 294.6 %reduce-scatter.18.cloned.1.call-start = ((), (), s32[]{:S(2)}) async-start(), calls=%async_computation.19 | async-start | bytes 3932160 | tf_op jit(solution)/shard_map/reduce_scatter | solution.py:267
  814.0 198.6 %copy-start.34 = (f32[64,256]{1,0:T(8,128)S(1)}, f32[64,256]{1,0:T(8,128)}, u32[]{:S(2)}) copy-start(f32[64,256]{1,0:T(8,128)} %param.36) | copy-start | bytes 196612
  814.8 244.1 %copy-start.3 = (bf16[1,512,768]{2,1,0:T(8,128)(2,1)S(1)}, bf16[1,512,768]{2,1,0:T(8,128)(2,1)}, u32[]{:S(2)}) copy-start(bf16[1,512,768]{2,1,0:T(8,128)(2,1)} %param.29) | copy-start | bytes 2359300
  814.8 244.1 %copy-start.38 = (f32[768]{0:T(1024)S(1)}, f32[768]{0:T(1024)}, u32[]{:S(2)}) copy-start(f32[768]{0:T(1024)} %copy-done.37) | copy-start | bytes 9220
  814.8 244.1 %copy-start.42 = (f32[512]{0:T(512)S(1)}, f32[512]{0:T(512)}, u32[]{:S(2)}) copy-start(f32[512]{0:T(512)} %copy-done.41) | copy-start | bytes 6148
  886.2 219.9 %copy-start.43 = (f32[2,768]{1,0:T(2,128)S(1)}, f32[2,768]{1,0:T(2,128)}, u32[]{:S(2)}) copy-start(f32[2,768]{1,0:T(2,128)} %param.37) | copy-start | bytes 18436
  886.2 219.9 %copy-start.46 = (f32[2,768]{1,0:T(2,128)S(1)}, f32[2,768]{1,0:T(2,128)}, u32[]{:S(2)}) copy-start(f32[2,768]{1,0:T(2,128)} %param.49) | copy-start | bytes 18436
  886.2 219.9 %copy-start.47 = (f32[2,768]{1,0:T(2,128)S(1)}, f32[2,768]{1,0:T(2,128)}, u32[]{:S(2)}) copy-start(f32[2,768]{1,0:T(2,128)} %param.43) | copy-start | bytes 18436
  886.2 220.6 %copy-start.7 = (f32[1,512,768]{2,1,0:T(8,128)S(1)}, f32[1,512,768]{2,1,0:T(8,128)}, u32[]{:S(2)}) copy-start(f32[1,512,768]{2,1,0:T(8,128)} %get-tuple-element.374) | copy-start | bytes 4718596
  (54 other events, 1457.0 us)
Sparse Core Ops, SparseCore 0:
  11.7 61.6 all-gather.9
  75.6 28.2 all-gather.7
  166.7 58.4 reduce-scatter.11
  524.5 28.5 all-gather.19
Sparse Core Ops, SparseCore 1:
  169.8 40.6 all-gather.13
  228.0 28.4 all-gather.11
  257.9 28.3 all-gather.17
  294.7 68.2 reduce-scatter.23
  365.9 40.5 all-gather.15
  421.1 57.6 reduce-scatter.15
  481.2 37.8 reduce-scatter.13
  536.8 68.3 reduce-scatter.21
  750.6 62.3 reduce-scatter.27
  816.5 67.5 reduce-scatter.19
  886.2 126.3 reduce-scatter.25
  1015.3 43.5 reduce-scatter.17
where the time goes:
time: 1130 us; the launch traced here: 1120 us
  waiting for transfers between devices  614 us (54%)
  local copies, waits for them, and re-layouts  194 us (17%)
  matrix products  119 us (11%)
  blocking collectives  110 us (10%)
  other arithmetic  55 us (5%)
  between operations  17.4 us (2%)
    reduce_scatter x1, waiting for transfers between devices, shards(): lax.psum_scatter(grad_bias_local, ('dp', 'mp'), scatter_dimension=0, tile...  126 us
    reduce_scatter x1, waiting for transfers between devices, shards(): lax.psum_scatter(grad_projection, 'dp', scatter_dimension=0, tiled=True)  69.3 us
    reduce_scatter x1, waiting for transfers between devices, shards(): lax.psum_scatter(grad_down_local, 'dp', scatter_dimension=1, tiled=True)  68.3 us
    concatenate x4, local copies, waits for them, and re-layouts, unskew_band(): jnp.concatenate([band_grad.reshape(-1), jnp.zeros((height,), band_grad.dt...  65 us
    reduce_scatter x1, waiting for transfers between devices, shards(): lax.psum_scatter(attn_terms, 'mp', scatter_dimension=1, tiled=True)  56.4 us
    reduce_scatter x1, waiting for transfers between devices, shards(): lax.psum_scatter(normed_terms, 'mp', scatter_dimension=1, tiled=True)  47.8 us
    reduce_scatter x1, waiting for transfers between devices, shards(): lax.psum_scatter(input_terms.astype(jnp.bfloat16), 'mp', scatter_dimensio...  44.7 us
    all_gather x1, waiting for transfers between devices, shards(): lax.all_gather(w_down.astype(jnp.bfloat16), 'dp', axis=1, tiled=True)  41.3 us
  transfers between devices with their start and end apart: 16, of which 13 were waited for; matrix products, arithmetic and copies ran while one was open for 23% of the time, Pallas kernels for 0%

commit v1 on v0

v1 whole, which is shorter than its diff:
```python
import functools

import jax
import jax.numpy as jnp
from jax import lax
from jax.experimental import pallas as pl
from jax.experimental.pallas import tpu as pltpu
from jax.sharding import Mesh
from jax.sharding import PartitionSpec as P

LEN = 2048
ADAM_STEP = 10
EPS = 1e-06
BETA_ONE = 0.9
BETA_TWO = 0.99
LEARN_RATE = 0.03
WEIGHT_DECAY = 0.1
ADAM_EPS = 1e-08

F32 = jnp.float32
BF = jnp.bfloat16
ZN, YN = 4, 2
GROUPS = ZN * YN
CHUNK = 128
GELU_C = 0.7978845608028654
GELU_A = 0.044715


def dot_nn(a, b):
    return jnp.dot(a, b, preferred_element_type=F32)


def dot_nt(a, b):
    return lax.dot_general(a, b, (((1,), (1,)), ((), ())), preferred_element_type=F32)


def dot_tn(a, b):
    return lax.dot_general(a, b, (((0,), (0,)), ((), ())), preferred_element_type=F32)


def loop_rows(count, step, body, unroll=False):
    @pl.loop(0, count // step, unroll=unroll)
    def _(index):
        body(pl.multiple_of(index * step, step))


class Copies:
    def __init__(self):
        self.started = []

    def go(self, copy):
        copy.start()
        self.started.append(copy)

    def drain(self):
        for copy in self.started:
            copy.wait_send()
        self.started = []


def block_kernel(
    x_ref,
    cot_ref,
    valid_ref,
    gains_ref,
    wa_ref,
    wu_ref,
    wd_ref,
    eb_ref,
    blk_ref,
    gin_ref,
    ga_ref,
    gu_ref,
    gd_ref,
    gb_ref,
    stat_ref,
    mix_w,
    up_w,
    down_w,
    band_rows,
    x_halo,
    full_w,
    normed,
    sig,
    expk,
    val,
    ratio,
    rden,
    resid,
    exp_low,
    kv_low,
    bands,
    mixed,
    normed_two,
    cot_low,
    act,
    dpre,
    ffn,
    dn_two,
    dnum,
    dden,
    bias_part,
    bias_recv_y,
    bias_recv_z,
    stats,
    stats_recv,
    recv_core,
    recv_one,
    recv_two,
    recv_z,
    ag_send,
    ag_recv,
    rs_send,
    rs_recv,
    halo_send,
    halo_recv,
    bias_send,
    bias_recv,
    stat_send,
    stat_recv,
):
    tokens, width = x_ref.shape
    window = x_halo.shape[0]
    rows = wa_ref.shape[0]
    chan = width // 4
    group = lax.axis_index("dph")
    inner = lax.axis_index("dpl")
    mp = lax.axis_index("mp")
    z, y = group // YN, group % YN
    x, c = mp // 2, mp % 2

    def device(zs, ys, xs, cs):
        return (zs * YN + ys, inner, xs * 2 + cs)

    def z_at(k):
        return (z + k) % ZN

    core_peer = device(z, y, x, 1 - c)
    x_peer = device(z, y, 1 - x, c)
    y_peer = device(z, 1 - y, x, c)
    diag_peer = device(z, y, 1 - x, 1 - c)
    z_peers = [device(z_at(k), y, x, c) for k in range(1, ZN)]

    barrier = pltpu.get_barrier_semaphore()
    friends = [core_peer, x_peer, y_peer, diag_peer] + z_peers
    for friend in friends:
        pl.semaphore_signal(barrier, inc=1, device_id=friend, device_id_type=MESH)
    pl.semaphore_wait(barrier, len(friends))

    out = Copies()

    half = 2 * chan
    gather_pieces = [
        (mix_w, 0, half, True),
        (mix_w, half, half, False),
        (None, 0, 0, True),
        (up_w, 0, up_w.shape[2], True),
        (down_w, 0, down_w.shape[2], False),
    ]

    def place(piece, zs, ys, xs, cs):
        buf, start, size, _ = gather_pieces[piece]
        if buf is None:
            return band_rows.at[(zs * YN + ys) * 4 + xs * 2 + cs]
        at = pl.multiple_of((zs * YN + ys) * rows, 32)
        return buf.at[xs * 2 + cs, pl.ds(at, rows), pl.ds(start, size)]

    def ag(piece, loc, peer, slot):
        ref = place(piece, *loc)
        return pltpu.make_async_remote_copy(
            src_ref=ref,
            dst_ref=ref,
            send_sem=ag_send.at[piece, slot],
            recv_sem=ag_recv.at[piece, slot],
            device_id=peer,
            device_id_type=MESH,
        )

    own = (z, y, x, c)

    def behind(k):
        return (z + ZN - k) % ZN

    def spot(kind, k):
        return (behind(k), y if kind in (0, 2) else 1 - y, x if kind in (0, 1) else 1 - x, c)

    def to_core(piece, kind, k):
        out.go(ag(piece, spot(kind, k), core_peer, 15 + kind * 4 + k))

    def arrived(piece, slot):
        ag(piece, own, core_peer, slot).wait_recv()

    def gather_start(pieces):
        for p in pieces:
            for k in range(1, ZN):
                out.go(ag(p, own, device(z_at(k), y, x, c), k - 1))
        for p in pieces:
            out.go(ag(p, own, y_peer, 3))
            out.go(ag(p, own, x_peer, 7))
            to_core(p, 0, 0)

    def gather_z(pieces, k):
        for p in pieces:
            arrived(p, k - 1)
            out.go(ag(p, spot(0, k), y_peer, 3 + k))
            out.go(ag(p, spot(0, k), x_peer, 7 + k))
            to_core(p, 0, k)

    def gather_turn(pieces, k):
        for p in pieces:
            if gather_pieces[p][3]:
                arrived(p, 3 + k)
                out.go(ag(p, spot(1, k), x_peer, 11 + k))
                to_core(p, 1, k)
            else:
                arrived(p, 7 + k)
                out.go(ag(p, spot(2, k), y_peer, 11 + k))
                to_core(p, 2, k)

    def gather_side(pieces, k):
        for p in pieces:
            if gather_pieces[p][3]:
                arrived(p, 7 + k)
                to_core(p, 2, k)
            else:
                arrived(p, 3 + k)
                to_core(p, 1, k)

    def gather_last(pieces, k):
        for p in pieces:
            arrived(p, 11 + k)
            to_core(p, 3, k)

    def gather_core(pieces):
        for p in pieces:
            for slot in range(15, 31):
                arrived(p, slot)

    mix_w[mp, pl.ds(pl.multiple_of(group * rows, 32), rows), :] = wa_ref[...]
    up_w[mp, pl.ds(pl.multiple_of(group * rows, 32), rows), :] = wu_ref[...]
    down_w[mp, pl.ds(pl.multiple_of(group * rows, 32), rows), :] = wd_ref[...]
    band_rows[group * 4 + mp] = eb_ref[...]
    band_rows[4 * GROUPS : 4 * GROUPS + 4] = jnp.zeros((4,) + eb_ref.shape, BF)

    halo_copy = pltpu.make_async_remote_copy(
        src_ref=x_ref.at[pl.ds(tokens - window, window)],
        dst_ref=x_halo,
        send_sem=halo_send.at[0],
        recv_sem=halo_recv.at[0],
        device_id=(group, inner, (mp + 1) % 4),
        device_id_type=MESH,
    )

    @pl.when(mp < 3)
    def _():
        halo_copy.start()

    def gather(pieces):
        gather_start(pieces)
        for k in range(1, ZN):
            gather_z(pieces, k)
        for k in range(ZN):
            gather_turn(pieces, k)
        for k in range(ZN):
            gather_side(pieces, k)
        for k in range(ZN):
            gather_last(pieces, k)
        gather_core(pieces)

    stats[0] = jnp.zeros(stats.shape[1:], F32)

    def add_stat(row, value):
        stats[0, row : row + 1, :] += jnp.sum(value, axis=0, keepdims=True)

    def rms(value):
        return lax.rsqrt(jnp.mean(value * value, axis=-1, keepdims=True) + EPS)

    def norm_own(at):
        part = pl.ds(at, CHUNK)
        xf = x_ref[part].astype(F32)
        normed[pl.ds(at + window, CHUNK)] = (xf * rms(xf) * gains_ref[0:1]).astype(BF)
        mask = valid_ref[part]
        add_stat(2, mask * xf * xf)
        add_stat(5, mask + jnp.zeros_like(xf))
        cot_low[part] = (cot_ref[part].astype(F32) * mask).astype(BF)

    def norm_halo(at):
        part = pl.ds(at, CHUNK)
        xf = x_halo[part].astype(F32)
        normed[part] = (xf * rms(xf) * gains_ref[0:1]).astype(BF)

    def repack(at):
        part = pl.ds(at, rows)
        for kind in range(4):
            full_w[kind, part] = jnp.concatenate(
                [mix_w[m, part, kind * chan : (kind + 1) * chan] for m in range(4)], axis=1
            )

    def project_halo(at):
        part = pl.ds(at, CHUNK)
        a = normed[part]
        ek = jnp.where(mp > 0, jnp.exp(dot_nn(a, full_w[1])), 0.0)
        exp_low[part] = ek.astype(BF)
        kv_low[part] = (ek * dot_nn(a, full_w[2])).astype(BF)

    def project_own(at):
        part = pl.ds(at, CHUNK)
        shifted = pl.ds(at + window, CHUNK)
        a = normed[shifted]
        ek = jnp.exp(dot_nn(a, full_w[1]))
        v = dot_nn(a, full_w[2])
        exp_low[shifted] = ek.astype(BF)
        kv_low[shifted] = (ek * v).astype(BF)
        expk[part] = ek
        val[part] = v
        sig[part] = jax.nn.sigmoid(dot_nn(a, full_w[0]))

    def build_bands():
        for i in range(3):
            raw = band_rows[pl.ds(mp * 8 + i * 4, 4)].reshape(window, window).astype(F32)
            wide = jnp.concatenate([raw, jnp.zeros_like(raw)], axis=1)
            bands[i] = pltpu.roll(wide, 1, 1, stride=1, stride_axis=0).astype(BF)

    def mix_rows(i):
        part = slice(i * window, (i + 1) * window)
        near = slice(i * window, (i + 2) * window)
        num = dot_nn(bands[i], kv_low[near])
        den = dot_nn(bands[i], exp_low[near])
        ratio[part] = num / den
        rden[part] = 1.0 / den

    def attend(at):
        part = pl.ds(at, CHUNK)
        low = (sig[part] * ratio[part]).astype(BF)
        mixed[part] = low
        attn = dot_nt(low, full_w[3])
        add_stat(3, valid_ref[part] * attn * attn)
        total = x_ref[part].astype(F32) + attn
        resid[part] = total
        normed_two[part] = (total * rms(total) * gains_ref[1:2]).astype(BF)

    def hidden_rows(m, first):
        def body(at):
            part = pl.ds(at, CHUNK)
            p = dot_nn(normed_two[part], up_w[m])
            da = dot_nn(cot_low[part], down_w[m])
            t = jnp.tanh(GELU_C * (p + GELU_A * (p * p * p)))
            low = (0.5 * p * (1.0 + t)).astype(BF)
            slope = 0.5 * (1.0 + t) + 0.5 * p * (1.0 - t * t) * (
                GELU_C * (1.0 + 3.0 * GELU_A * (p * p))
            )
            dlow = (da * slope).astype(BF)
            act[part] = low
            dpre[part] = dlow
            f = dot_nt(low, down_w[m])
            d = dot_nt(dlow, up_w[m])
            if first:
                ffn[part] = f
                dn_two[part] = d
            else:
                ffn[part] += f
                dn_two[part] += d

        return body

    def weight_grad(result, left, right):
        for at in range(0, result.shape[1], 256):
            part = slice(at, at + 256)
            result[:, part] = dot_tn(left[...], right[:, part]).astype(BF)

    def hidden_slab(m, first):
        loop_rows(tokens, CHUNK, hidden_rows(m, first))
        weight_grad(up_w.at[m], normed_two, dpre)
        weight_grad(down_w.at[m], cot_low, act)

    def close_hidden(at):
        part = pl.ds(at, CHUNK)
        mask = valid_ref[part]
        f = ffn[part]
        res = resid[part]
        add_stat(4, mask * f * f)
        blk_ref[part] = (res + f).astype(BF)
        d = dn_two[part]
        r = rms(res)
        u = gains_ref[1:2] * d
        grad = (
            cot_ref[part].astype(F32) * mask
            + r * u
            - res * (r * r * r) * jnp.mean(u * res, axis=-1, keepdims=True)
        )
        add_stat(1, d * res * r)
        ffn[part] = grad
        act[part] = grad.astype(BF)

    def back_attend(at):
        part = pl.ds(at, CHUNK)
        dm = dot_nn(act[part], full_w[3])
        sg = sig[part]
        rt = ratio[part]
        scaled = dm * sg
        normed_two[part] = (scaled * rt * (1.0 - sg)).astype(BF)
        dn = scaled * rden[part]
        dnum[part] = dn.astype(BF)
        dden[part] = (-dn * rt).astype(BF)

    def halo_back(slot, buf):
        return pltpu.make_async_remote_copy(
            src_ref=buf.at[pl.ds(0, window)],
            dst_ref=buf.at[pl.ds(tokens, window)],
            send_sem=halo_send.at[slot],
            recv_sem=halo_recv.at[slot],
            device_id=(group, inner, (mp + 3) % 4),
            device_id_type=MESH,
        )

    def band_grad(i):
        part = slice(i * window, (i + 1) * window)
        near = slice(i * window, (i + 2) * window)
        dn_two[part, 0 : 2 * window] = dot_nt(dnum[part], kv_low[near]) + dot_nt(dden[part], exp_low[near])

    def unskew():
        wide = 2 * window
        line = lax.broadcasted_iota(jnp.int32, (8, wide), 0)

        @pl.loop(0, tokens // 8, unroll=8)
        def _(index):
            at = pl.multiple_of(index * 8, 8)
            v = pltpu.roll(dn_two[pl.ds(at, 8), 0:wide], wide - 1 - at % window, 1)
            for bit in (1, 2, 4):
                v = jnp.where((line & bit) != 0, pltpu.roll(v, wide - bit, 1), v)
            dn_two[pl.ds(at, 8), 0:window] = v[:, 0:window]

        for j in range(GROUPS):
            bias_part[j] = dn_two[j * 64 : (j + 1) * 64, 0:window].astype(BF)

    def back_keys(j):
        here = slice(j * window, (j + 1) * window)
        then = slice((j + 1) * window, (j + 2) * window)
        right = bands[j, :, window:]
        left = bands[j + 1, :, :window]
        dkv = dot_tn(right, dnum[here]) + dot_tn(left, dnum[then])
        de = dot_tn(right, dden[here]) + dot_tn(left, dden[then])
        ek = expk[here]
        cot_low[here] = (dkv * ek).astype(BF)
        dpre[here] = ((de + dkv * val[here]) * ek).astype(BF)

    def back_input(at):
        part = pl.ds(at, CHUNK)
        d = (
            dot_nt(normed_two[part], full_w[0])
            + dot_nt(dpre[part], full_w[1])
            + dot_nt(cot_low[part], full_w[2])
        )
        xf = x_ref[part].astype(F32)
        r = rms(xf)
        u = gains_ref[0:1] * d
        gin_ref[part] = (
            ffn[part] + r * u - xf * (r * r * r) * jnp.mean(u * xf, axis=-1, keepdims=True)
        )
        add_stat(0, d * xf * r)

    def unpack(at):
        part = pl.ds(at, rows)
        for m in range(4):
            mix_w[m, part] = jnp.concatenate(
                [full_w[kind, part, m * chan : (m + 1) * chan] for kind in range(4)], axis=1
            )

    scatter_pieces = [
        (mix_w, 0, half, True, ga_ref, 0),
        (mix_w, half, half, False, ga_ref, half),
        (up_w, 0, up_w.shape[2], True, gu_ref, 2 * half),
        (down_w, 0, down_w.shape[2], False, gd_ref, 2 * half + up_w.shape[2]),
    ]

    def rs(piece, src, dst, peer, slot):
        return pltpu.make_async_remote_copy(
            src_ref=src,
            dst_ref=dst,
            send_sem=rs_send.at[piece, slot],
            recv_sem=rs_recv.at[piece, slot],
            device_id=peer,
            device_id_type=MESH,
        )

    def block(piece, xs, zs, ys, count=1):
        buf, start, size = scatter_pieces[piece][:3]
        at = pl.multiple_of((zs * YN + ys) * rows, 32)
        return buf.at[xs * 2 + c, pl.ds(at, rows * count), pl.ds(start, size)]

    def lanes(piece):
        return pl.ds(scatter_pieces[piece][5], scatter_pieces[piece][2])

    def core_copies(p):
        buf, start, size = scatter_pieces[p][:3]
        return [
            rs(
                p,
                buf.at[xs * 2 + 1 - c, :, pl.ds(start, size)],
                recv_core.at[xs, :, lanes(p)],
                core_peer,
                xs,
            )
            for xs in range(2)
        ]

    def one_copies(p):
        if scatter_pieces[p][3]:
            return [
                rs(p, block(p, 1 - x, k // YN, k % YN), recv_one.at[k, :, lanes(p)], x_peer, 2 + k)
                for k in range(GROUPS)
            ]
        return [
            rs(
                p,
                block(p, k // ZN, k % ZN, 1 - y),
                recv_one.at[k, :, lanes(p)],
                y_peer,
                2 + k,
            )
            for k in range(GROUPS)
        ]

    def one_home(p, k):
        if scatter_pieces[p][3]:
            return block(p, x, k // YN, k % YN)
        return block(p, k // ZN, k % ZN, y)

    def two_copies(p):
        if scatter_pieces[p][3]:
            return [
                rs(p, block(p, x, zs, 1 - y), recv_two.at[zs, :, lanes(p)], y_peer, 10 + zs)
                for zs in range(ZN)
            ]
        return [
            rs(p, block(p, 1 - x, zs, y), recv_two.at[zs, :, lanes(p)], x_peer, 10 + zs)
            for zs in range(ZN)
        ]

    def z_copies(p):
        return [
            rs(
                p,
                block(p, x, z_at(k), y),
                recv_z.at[k - 1, :, lanes(p)],
                z_peers[k - 1],
                13 + k,
            )
            for k in range(1, ZN)
        ]

    def scatter(pieces):
        core = {p: core_copies(p) for p in pieces}
        for p in pieces:
            for copy in core[p]:
                out.go(copy)
        ones = {p: one_copies(p) for p in pieces}
        for p in pieces:
            buf, start, size = scatter_pieces[p][:3]
            for xs in range(2):
                core[p][xs].wait_recv()

                def body(at):
                    part = pl.ds(at, rows)
                    buf[xs * 2 + c, part, pl.ds(start, size)] += recv_core[xs, part, lanes(p)]

                loop_rows(GROUPS * rows, rows, body)
            for copy in ones[p]:
                out.go(copy)
        twos = {p: two_copies(p) for p in pieces}
        for p in pieces:
            for k in range(GROUPS):
                ones[p][k].wait_recv()
                home = one_home(p, k)
                home[...] += recv_one[k, :, lanes(p)]
            for copy in twos[p]:
                out.go(copy)
        zs_all = {p: z_copies(p) for p in pieces}
        for p in pieces:
            for zs in range(ZN):
                twos[p][zs].wait_recv()
                home = block(p, x, zs, y)
                home[...] += recv_two[zs, :, lanes(p)]
            for copy in zs_all[p]:
                out.go(copy)
        for p in pieces:
            total = block(p, x, z, y)[...].astype(F32)
            for k in range(1, ZN):
                zs_all[p][k - 1].wait_recv()
                total = total + recv_z[k - 1, :, lanes(p)].astype(F32)
            result, start, size = (
                scatter_pieces[p][4],
                scatter_pieces[p][1],
                scatter_pieces[p][2],
            )
            result[:, pl.ds(start, size)] = total

    def scatter_bias():
        def copy(src, dst, peer, slot):
            return pltpu.make_async_remote_copy(
                src_ref=src,
                dst_ref=dst,
                send_sem=bias_send.at[slot],
                recv_sem=bias_recv.at[slot],
                device_id=peer,
                device_id_type=MESH,
            )

        first = [
            copy(bias_part.at[zs * YN + 1 - y], bias_recv_y.at[zs], y_peer, zs)
            for zs in range(ZN)
        ]
        for item in first:
            out.go(item)
        for zs in range(ZN):
            first[zs].wait_recv()
            bias_part[zs * YN + y] += bias_recv_y[zs]
        second = [
            copy(bias_part.at[z_at(k) * YN + y], bias_recv_z.at[k - 1], z_peers[k - 1], 3 + k)
            for k in range(1, ZN)
        ]
        for item in second:
            out.go(item)
        total = bias_part[z * YN + y].astype(F32)
        for k in range(1, ZN):
            second[k - 1].wait_recv()
            total = total + bias_recv_z[k - 1].astype(F32)
        gb_ref[...] = total

    def reduce_stats():
        def copy(step, slot, peer):
            return pltpu.make_async_remote_copy(
                src_ref=stats.at[step],
                dst_ref=stats_recv.at[slot],
                send_sem=stat_send.at[slot],
                recv_sem=stat_recv.at[slot],
                device_id=peer,
                device_id_type=MESH,
            )

        for step, peer in enumerate((core_peer, x_peer, y_peer)):
            item = copy(step, step, peer)
            out.go(item)
            item.wait_recv()
            stats[step + 1] = stats[step] + stats_recv[step]
        items = [copy(3, 2 + k, z_peers[k - 1]) for k in range(1, ZN)]
        for item in items:
            out.go(item)
        total = stats[3]
        for k, item in enumerate(items):
            item.wait_recv()
            total = total + stats_recv[3 + k]
        stat_ref[...] = total

    gather([0, 1, 2])
    gather([3, 4])
    loop_rows(tokens, CHUNK, norm_own)

    @pl.when(mp > 0)
    def _():
        halo_copy.wait_recv()

    @pl.when(mp == 0)
    def _():
        x_halo[...] = jnp.zeros_like(x_halo)

    loop_rows(window, CHUNK, norm_halo)
    loop_rows(GROUPS * rows, rows, repack)
    loop_rows(window, CHUNK, project_halo)
    loop_rows(tokens, CHUNK, project_own)
    build_bands()
    for i in range(2):
        mix_rows(i)
    loop_rows(tokens, CHUNK, attend)
    out.drain()
    for r in range(4):
        slab = (x ^ (r // 2)) * 2 + (c ^ (r % 2))
        hidden_slab(slab, r == 0)
    loop_rows(tokens, CHUNK, close_hidden)
    loop_rows(tokens, CHUNK, back_attend)

    backs = [halo_back(1, dnum), halo_back(2, dden)]

    @pl.when(mp > 0)
    def _():
        for item in backs:
            item.start()

    weight_grad(full_w.at[3], act, mixed)
    for i in range(2):
        band_grad(i)
    unskew()

    @pl.when(mp < 3)
    def _():
        for item in backs:
            item.wait_recv()

    @pl.when(mp == 3)
    def _():
        dnum[pl.ds(tokens, window)] = jnp.zeros((window, width), BF)
        dden[pl.ds(tokens, window)] = jnp.zeros((window, width), BF)

    for j in range(2):
        back_keys(j)
    loop_rows(tokens, CHUNK, back_input)
    for kind, grad in enumerate((normed_two, dpre, cot_low)):
        weight_grad(full_w.at[kind], normed.at[pl.ds(window, tokens)], grad)
    loop_rows(GROUPS * rows, rows, unpack)
    scatter([2, 3, 0, 1])
    scatter_bias()
    reduce_stats()

    @pl.when(mp < 3)
    def _():
        halo_copy.wait_send()

    @pl.when(mp > 0)
    def _():
        for item in backs:
            item.wait_send()

    out.drain()


def run_block(x, cot, valid, gains, wa, wu, wd, eb):
    tokens, width = x.shape
    window = eb.shape[1]
    rows = wa.shape[0]
    full = rows * GROUPS
    vmem = pl.BlockSpec(memory_space=pltpu.VMEM)
    lanes = wa.shape[1] + wu.shape[1] + wd.shape[1]

    def shape(*dims, kind=F32):
        return jax.ShapeDtypeStruct(dims, kind)

    def buf(*dims, kind=F32):
        return pltpu.VMEM(dims, kind)

    def low(*dims):
        return pltpu.VMEM(dims, BF)

    dma = pltpu.SemaphoreType.DMA
    return pl.pallas_call(
        block_kernel,
        out_shape=(
            shape(tokens, width, kind=BF),
            shape(tokens, width),
            shape(*wa.shape),
            shape(*wu.shape),
            shape(*wd.shape),
            shape(*eb.shape),
            shape(8, width),
        ),
        in_specs=[vmem] * 8,
        out_specs=(vmem,) * 7,
        scratch_shapes=[
            low(4, full, wa.shape[1]),
            low(4, full, wu.shape[1]),
            low(4, full, wd.shape[1]),
            low(4 * GROUPS + 4, *eb.shape),
            low(window, width),
            low(4, full, width),
            low(window + tokens, width),
            buf(tokens, width),
            buf(tokens, width),
            buf(tokens, width),
            buf(tokens, width),
            buf(tokens, width),
            buf(tokens, width),
            low(window + tokens, width),
            low(window + tokens, width),
            low(3, window, 2 * window),
            low(tokens, width),
            low(tokens, width),
            low(tokens, width),
            low(tokens, wu.shape[1]),
            low(tokens, wu.shape[1]),
            buf(tokens, width),
            buf(tokens, width),
            low(tokens + window, width),
            low(tokens + window, width),
            low(GROUPS, *eb.shape),
            low(ZN, *eb.shape),
            low(ZN - 1, *eb.shape),
            buf(4, 8, width),
            buf(6, 8, width),
            low(2, full, lanes),
            low(GROUPS, rows, lanes),
            low(ZN, rows, lanes),
            low(ZN - 1, rows, lanes),
            dma((5, 31)),
            dma((5, 31)),
            dma((4, 17)),
            dma((4, 17)),
            dma((3,)),
            dma((3,)),
            dma((7,)),
            dma((7,)),
            dma((6,)),
            dma((6,)),
        ],
        compiler_params=pltpu.CompilerParams(
            collective_id=0, has_side_effects=True, vmem_limit_bytes=63 * 1024 * 1024
        ),
    )(x, cot, valid, gains, wa, wu, wd, eb)


MESH = pl.DeviceIdType.MESH


def adam_step(param, grad, first, second, step_value, decay):
    new_first = BETA_ONE * first + (1.0 - BETA_ONE) * grad
    new_second = BETA_TWO * second + (1.0 - BETA_TWO) * grad * grad
    first_hat = new_first / (1.0 - jnp.power(jnp.float32(BETA_ONE), step_value))
    second_hat = new_second / (1.0 - jnp.power(jnp.float32(BETA_TWO), step_value))
    update = -LEARN_RATE * (first_hat / (jnp.sqrt(second_hat) + ADAM_EPS) + decay * param)
    return (new_first, new_second, update)


def shards(inner, block_input, out_cotangent, lengths, *rest):
    params, firsts, seconds = rest[:6], rest[6:12], rest[12:18]
    w_qkv, w_out, w_up, w_down, pair_bias, norm_gains = params
    _, tokens, width = block_input.shape
    chan = w_qkv.shape[2]
    positions = lax.axis_index("mp") * tokens + jnp.arange(tokens, dtype=jnp.int32)
    valid = (positions < lengths[0]).astype(F32)[:, None]
    own_a = jnp.concatenate(
        [w_qkv.reshape(w_qkv.shape[0], 3 * chan).astype(BF), w_out.astype(BF).T], axis=1
    )
    own_u = w_up.astype(BF)
    own_d = w_down.astype(BF).T
    own_e = jnp.exp(pair_bias).astype(BF)[:, ::-1]
    if inner > 1:
        own_a, own_u, own_d = (
            lax.all_gather(item, "dpl", axis=0, tiled=True) for item in (own_a, own_u, own_d)
        )
        count = own_e.shape[0]
        every = lax.all_gather(own_e, ("dpl", "mp"), axis=0, tiled=True)
        own_e = lax.dynamic_slice_in_dim(
            every, lax.axis_index("mp") * inner * count, inner * count, 0
        )
    block_low, grad_input, part_a, part_u, part_d, part_b, stats = run_block(
        block_input[0], out_cotangent[0], valid, norm_gains, own_a, own_u, own_d, own_e
    )
    if inner > 1:
        part_a, part_u, part_d = (
            lax.psum_scatter(item, "dpl", scatter_dimension=0, tiled=True)
            for item in (part_a, part_u, part_d)
        )
        part_b, stats = lax.psum((part_b, stats), "dpl")
        every = lax.all_gather(part_b, ("mp", "dph"), axis=0, tiled=True)
        count = pair_bias.shape[0]
        place = lax.axis_index(("dph", "dpl", "mp"))
        owned_b = lax.dynamic_slice_in_dim(every, place * count, count, 0)
    else:
        moves = []
        for group in range(GROUPS):
            for m in range(4):
                moves.append((group * 4 + m, m * GROUPS + group))
        owned_b = lax.ppermute(part_b, ("dph", "mp"), moves)
    grad_scale = float(lax.axis_size("dph") * inner * LEN) ** (-0.5)
    grads = [
        part_a[:, : 3 * chan].reshape(w_qkv.shape) * grad_scale,
        part_a[:, 3 * chan :].T * grad_scale,
        part_u * grad_scale,
        part_d.T * grad_scale,
        owned_b[:, ::-1] * jnp.exp(pair_bias) * grad_scale,
        stats[0:2] * grad_scale,
    ]
    decays = (WEIGHT_DECAY, WEIGHT_DECAY, WEIGHT_DECAY, WEIGHT_DECAY, 0.0, 0.0)
    step_value = jnp.float32(ADAM_STEP)
    states = [
        adam_step(params[i], grads[i], firsts[i], seconds[i], step_value, decays[i])
        for i in range(6)
    ]
    sums = jnp.sum(stats, axis=1)
    rms_stats = jnp.sqrt(sums[2:5] / sums[5])
    return (
        block_low[None],
        grad_input[None],
        *grads,
        *(state[0] for state in states),
        *(state[1] for state in states),
        *(state[2] for state in states),
        rms_stats,
    )


def solution(mesh):
    inner = mesh.shape["dp"] // GROUPS
    fine = Mesh(
        mesh.devices.reshape(GROUPS, inner, mesh.shape["mp"]),
        ("dph", "dpl", "mp"),
    )
    dp = ("dph", "dpl")
    weights = (
        P(dp, None, "mp"),
        P("mp", dp),
        P(dp, "mp"),
        P("mp", dp),
        P((*dp, "mp"), None),
        P(),
    )
    acts = P(dp, "mp", None)
    return jax.shard_map(
        functools.partial(shards, inner),
        mesh=fine,
        in_specs=(acts, acts, P(dp), *weights, *weights, *weights),
        out_specs=(acts, acts, *weights, *weights, *weights, *weights, P()),
        check_vma=False,
    )
```

time: 1130 us -> 319 us (0.28)
  waiting for transfers between devices: 614 us -> 0.01 us
  Pallas kernels: 0 us -> 282 us
  local copies, waits for them, and re-layouts: 194 us -> 13.7 us
  matrix products: 119 us -> 0 us
  blocking collectives: 110 us -> 0 us
  other arithmetic: 55 us -> 16.1 us
  between operations: 17.4 us -> 1.67 us
    reduce_scatter x8 -> x0, waiting for transfers between devices: 451 us -> none  [the longest x1 126 us: shards(): lax.psum_scatter(grad_bias_local, ('dp', 'mp'), scatter_dimension=0, tile...]
    pallas_call x0 -> x1, Pallas kernels: none -> 282 us  [run_block(): pl.pallas_call(block_kernel, out_shape=(shape(tokens, width, kind=BF), sh...]
    all_gather x7 -> x0, waiting for transfers between devices: 123 us -> none  [the longest x1 41.3 us: shards(): lax.all_gather(w_down.astype(jnp.bfloat16), 'dp', axis=1, tiled=True)]
    dot_general x34 -> x0, matrix products: 113 us -> none  [the longest x4 10.8 us: one_block(): jnp.einsum('ij,ic->jc', band_rows, lower_block, preferred_element_type=jn...]
    all_gather x2 -> x0, blocking collectives: 69.4 us -> none  [the longest x1 38 us: shards(): lax.all_gather(w_qkv.astype(jnp.bfloat16), 'dp', axis=0, tiled=True)]
    concatenate x22 -> x0, local copies, waits for them, and re-layouts: 68.1 us -> none  [the longest x4 65 us: unskew_band(): jnp.concatenate([band_grad.reshape(-1), jnp.zeros((height,), band_grad.dt...]
    psum x1 -> x0, blocking collectives: 40.2 us -> none  [shards(): lax.psum((jnp.stack([gain_one_grad, gain_two_grad]), local_sums), ('dp',...]
    unnamed x17 -> x0, waiting for transfers between devices: 39.6 us -> none
  transfers between devices with their start and end apart: 16 -> 1, of which waited for: 13 -> 0; matrix products, arithmetic and copies ran while one was open for 23% -> 6% of each run, Pallas kernels for 0% -> 0%
where the time goes in v1:
time: 319 us; the launch traced here: 315 us
  Pallas kernels  282 us (88%)
  other arithmetic  16.1 us (5%)
  local copies, waits for them, and re-layouts  13.7 us (4%)
    pallas_call x1, Pallas kernels, run_block(): pl.pallas_call(block_kernel, out_shape=(shape(tokens, width, kind=BF), sh...  282 us
    unnamed x64, local copies, waits for them, and re-layouts  10.6 us
    mul x6, other arithmetic, adam_step(): -LEARN_RATE  7.43 us
  transfers between devices with their start and end apart: 1, of which 0 were waited for; matrix products, arithmetic and copies ran while one was open for 6% of the time, Pallas kernels for 0%

profile of v1, /device:TPU:4, one launch (start us, length us, event | category | flops | bytes accessed | tf_op | source)
XLA Modules:
  0.0 315.4 jit_solution(5097401323946035139)
XLA Ops:
  1.4 0.9 exponential_convert_fusion
  2.3 0.8 rev.6.eb_ref
  3.1 1.0 copy.83
  4.1 1.0 convert_element_type.29
  6.7 0.7 pad_maximum_fusion.wa_ref
  8.2 282.0 %shard_map.412 = (bf16[512,768]{1,0:T(8,128)(2,1)}, f32[512,768]{1,0:T(8,128)}, f32[96,768]{1,0:T(8,128)}, f32[96,768]{1,0:T(8,128)}, f32[96,768]{1,0:T(8,128)}, /*index=5*/f32[64,256]{1,0:T(8,128)}, f32[8,768]{1,0:T(8,128)}) custom-call(bf16[512,768]{1,0:T(8,128)(2,1)} %bitcast.45, bf16[512,768]{1,0:T(8,128)(2,1)} %bitcast.46, f32[512,1]{1,0:T(8,128)} %fusion.1.valid_ref, ...), custom_call_target="tpu_custom_call" | custom-call | tf_op jit(solution)/shard_map/pallas_call | solution.py:744
  290.2 2.1 collective-permute-start
  292.5 1.6 multiply_bitcast_fusion.1
  294.1 1.0 slice_multiply_fusion.1
  296.9 1.8 add_multiply_fusion.3
  298.7 1.4 add_multiply_fusion.5
  300.0 2.2 add_multiply_fusion.1
  302.2 1.2 add_multiply_fusion
  304.1 1.2 divide_sqrt_fusion
  305.3 0.9 copy.94
  306.2 0.7 copy.101
  306.9 0.7 copy.99
  308.4 0.7 copy.95
  309.1 0.9 copy.100
  310.0 0.9 copy.98
  310.9 0.9 copy.96
  311.8 0.9 rev.7
  313.4 0.9 copy.105
  314.3 1.1 copy.106
  (68 shorter events, 6.4 us)
Async XLA Ops:
  0.7 4.7 %copy-start.1 = (f32[96,768]{1,0:T(8,128)S(1)}, f32[96,768]{1,0:T(8,128)}, u32[]{:S(2)}) copy-start(f32[96,768]{1,0:T(8,128)} %param.26) | copy-start | bytes 884740
  0.7 5.4 %copy-start.2 = (f32[768,96]{0,1:T(8,128)S(1)}, f32[768,96]{0,1:T(8,128)}, u32[]{:S(2)}) copy-start(f32[768,96]{0,1:T(8,128)} %param.27) | copy-start | bytes 884740
  6.0 286.2 %copy-start.3 = (f32[96,3,192]{2,0,1:T(8,128)S(1)}, f32[96,3,192]{2,0,1:T(8,128)}, u32[]{:S(2)}) copy-start(f32[96,3,192]{2,0,1:T(8,128)} %param.24) | copy-start | bytes 663556
  290.2 4.9 %copy-start.14 = (f32[192,96]{1,0:T(8,128)S(1)}, f32[192,96]{1,0:T(8,128)}, u32[]{:S(2)}) copy-start(f32[192,96]{1,0:T(8,128)} %param.31) | copy-start | bytes 221188
  290.2 5.0 %copy-start.15 = (f32[192,96]{1,0:T(8,128)S(1)}, f32[192,96]{1,0:T(8,128)}, u32[]{:S(2)}) copy-start(f32[192,96]{1,0:T(8,128)} %param.37) | copy-start | bytes 221188
  290.2 5.1 %copy-start.11 = (f32[96,3,192]{2,0,1:T(8,128)S(1)}, f32[96,3,192]{2,0,1:T(8,128)}, u32[]{:S(2)}) copy-start(f32[96,3,192]{2,0,1:T(8,128)} %param.30) | copy-start | bytes 663556
  290.2 5.2 %copy-start.12 = (f32[96,3,192]{2,0,1:T(8,128)S(1)}, f32[96,3,192]{2,0,1:T(8,128)}, u32[]{:S(2)}) copy-start(f32[96,3,192]{2,0,1:T(8,128)} %param.36) | copy-start | bytes 663556
  290.2 5.4 %copy-start.18 = (f32[8,768]{1,0:T(8,128)S(1)}, f32[8,768]{1,0:T(8,128)}, u32[]{:S(2)}) copy-start(f32[8,768]{1,0:T(8,128)} %get-tuple-element.40) | copy-start | bytes 73732
  290.2 21.5 %collective-permute-start = (f32[64,256]{1,0:T(8,128)}, f32[64,256]{1,0:T(8,128)}, u32[]{:S(2)}, u32[]{:S(2)}) collective-permute-start(f32[64,256]{1,0:T(8,128)} %get-tuple-element.39), channel_id=1, source_target_pairs={{0,0},{1,8},{2,16},{3,24},{4,1},{5,9},{6,17},{7,25},{8,2},{9,10},{... | collective-permute-start | bytes 196616 | tf_op jit(solution)/shard_map/ppermute | solution.py:861
  295.5 3.2 %copy-start.19 = (f32[2,768]{1,0:T(2,128)S(1)}, f32[2,768]{1,0:T(2,128)}, u32[]{:S(2)}) copy-start(f32[2,768]{1,0:T(2,128)} %gains_ref.1) | copy-start | bytes 18436
  295.5 3.2 %copy-start.20 = (f32[2,768]{1,0:T(2,128)S(1)}, f32[2,768]{1,0:T(2,128)}, u32[]{:S(2)}) copy-start(f32[2,768]{1,0:T(2,128)} %param.41) | copy-start | bytes 18436
  295.5 4.5 %copy-start.7 = (f32[96,768]{1,0:T(8,128)S(1)}, f32[96,768]{1,0:T(8,128)}, u32[]{:S(2)}) copy-start(f32[96,768]{1,0:T(8,128)} %param.38) | copy-start | bytes 884740
  295.6 3.0 copy-start.21
  295.8 0.9 copy-start.22
  296.8 5.4 %copy-start.8 = (f32[768,96]{0,1:T(8,128)S(1)}, f32[768,96]{0,1:T(8,128)}, u32[]{:S(2)}) copy-start(f32[768,96]{0,1:T(8,128)} %param.39) | copy-start | bytes 884740
  296.9 5.4 %copy-start.9 = (f32[768,96]{0,1:T(8,128)S(1)}, f32[768,96]{0,1:T(8,128)}, u32[]{:S(2)}) copy-start(f32[768,96]{0,1:T(8,128)} %param.33) | copy-start | bytes 884740
  296.9 5.4 %copy-start.10 = (f32[96,768]{1,0:T(8,128)S(1)}, f32[96,768]{1,0:T(8,128)}, u32[]{:S(2)}) copy-start(f32[96,768]{1,0:T(8,128)} %get-tuple-element.38) | copy-start | bytes 884740
  303.4 2.8 copy-start.6
  303.4 5.0 %copy-start.5 = (f32[192,96]{0,1:T(8,128)S(1)}, f32[192,96]{0,1:T(8,128)}, u32[]{:S(2)}) copy-start(f32[192,96]{0,1:T(8,128)} %multiply_bitcast_fusion.1) | copy-start | bytes 221188
  305.3 7.4 %copy-start.13 = (f32[64,256]{1,0:T(8,128)S(1)}, f32[64,256]{1,0:T(8,128)}, u32[]{:S(2)}) copy-start(f32[64,256]{1,0:T(8,128)} %param.28) | copy-start | bytes 196612
  305.3 7.4 %copy-start.16 = (f32[64,256]{1,0:T(8,128)S(1)}, f32[64,256]{1,0:T(8,128)}, u32[]{:S(2)}) copy-start(f32[64,256]{1,0:T(8,128)} %param.40) | copy-start | bytes 196612
  305.3 7.4 %copy-start.17 = (f32[64,256]{1,0:T(8,128)S(1)}, f32[64,256]{1,0:T(8,128)}, u32[]{:S(2)}) copy-start(f32[64,256]{1,0:T(8,128)} %param.34) | copy-start | bytes 196612
  306.9 6.5 %copy-start.4 = (bf16[512,768]{1,0:T(8,128)(2,1)S(1)}, bf16[512,768]{1,0:T(8,128)(2,1)}, u32[]{:S(2)}) copy-start(bf16[512,768]{1,0:T(8,128)(2,1)} %get-tuple-element.34) | copy-start | bytes 2359300
  310.9 3.4 %copy-start = (f32[512,768]{1,0:T(8,128)S(1)}, f32[512,768]{1,0:T(8,128)}, u32[]{:S(2)}) copy-start(f32[512,768]{1,0:T(8,128)} %get-tuple-element.35) | copy-start | bytes 4718596
  (1 other events, 0.7 us)

commit v2 on v1

v2 whole, which is shorter than its diff:
```python
import functools

import jax
import jax.numpy as jnp
from jax import lax
from jax.experimental import pallas as pl
from jax.experimental.pallas import tpu as pltpu
from jax.sharding import Mesh
from jax.sharding import PartitionSpec as P

LEN = 2048
ADAM_STEP = 10
EPS = 1e-06
BETA_ONE = 0.9
BETA_TWO = 0.99
LEARN_RATE = 0.03
WEIGHT_DECAY = 0.1
ADAM_EPS = 1e-08

F32 = jnp.float32
BF = jnp.bfloat16
ZN, YN = 4, 2
GROUPS = ZN * YN
CHUNK = 128
GELU_C = 0.7978845608028654
GELU_A = 0.044715


def dot_nn(a, b):
    return jnp.dot(a, b, preferred_element_type=F32)


def dot_nt(a, b):
    return lax.dot_general(a, b, (((1,), (1,)), ((), ())), preferred_element_type=F32)


def dot_tn(a, b):
    return lax.dot_general(a, b, (((0,), (0,)), ((), ())), preferred_element_type=F32)


def loop_rows(count, step, body, unroll=False):
    @pl.loop(0, count // step, unroll=unroll)
    def _(index):
        body(pl.multiple_of(index * step, step))


class Copies:
    def __init__(self):
        self.started = {}

    def go(self, copy, tag=None):
        copy.start()
        self.started.setdefault(tag, []).append(copy)

    def drain(self, *tags):
        for tag in tags or list(self.started):
            for copy in self.started.pop(tag, []):
                copy.wait_send()


def block_kernel(
    last_hop,
    len_ref,
    x_ref,
    cot_ref,
    gains_ref,
    wq_ref,
    wo_ref,
    wu_ref,
    wd_ref,
    bias_ref,
    blk_ref,
    gin_ref,
    gq_ref,
    go_ref,
    gu_ref,
    gd_ref,
    gb_ref,
    stat_ref,
    mix_w,
    up_w,
    down_w,
    band_rows,
    x_halo,
    full_w,
    normed,
    wide_rows,
    resid,
    exp_low,
    kv_low,
    bands,
    mixed,
    normed_two,
    cot_low,
    act,
    dpre,
    dn_two,
    dnum,
    dden,
    bias_part,
    bias_recv_y,
    bias_recv_z,
    bias_hop,
    stats,
    stats_recv,
    recv_core,
    recv_one,
    recv_two,
    recv_z,
    ag_send,
    ag_recv,
    rs_send,
    rs_recv,
    halo_send,
    halo_recv,
    bias_send,
    bias_recv,
    stat_send,
    stat_recv,
):
    tokens, width = x_ref.shape
    window = x_halo.shape[0]
    rows = wu_ref.shape[0]
    chan = width // 4
    ffn = gin_ref
    sig, ratio, rden, expk, val = (
        wide_rows.at[pl.ds(i * tokens, tokens)] for i in range(5)
    )
    group = lax.axis_index("dph")
    inner = lax.axis_index("dpl")
    mp = lax.axis_index("mp")
    z, y = group // YN, group % YN
    x, c = mp // 2, mp % 2

    def device(zs, ys, xs, cs):
        return (zs * YN + ys, inner, xs * 2 + cs)

    def z_at(k):
        return (z + k) % ZN

    core_peer = device(z, y, x, 1 - c)
    x_peer = device(z, y, 1 - x, c)
    y_peer = device(z, 1 - y, x, c)
    diag_peer = device(z, y, 1 - x, 1 - c)
    z_peers = [device(z_at(k), y, x, c) for k in range(1, ZN)]

    out = Copies()

    half = 2 * chan
    gather_pieces = [
        (mix_w, 0, half, True),
        (mix_w, half, half, False),
        (None, 0, 0, True),
        (up_w, 0, up_w.shape[2], True),
        (down_w, 0, down_w.shape[2], False),
    ]

    def place(piece, zs, ys, xs, cs):
        buf, start, size, _ = gather_pieces[piece]
        if buf is None:
            return band_rows.at[(zs * YN + ys) * 4 + xs * 2 + cs]
        at = pl.multiple_of((zs * YN + ys) * rows, 32)
        return buf.at[xs * 2 + cs, pl.ds(at, rows), pl.ds(start, size)]

    def ag(piece, loc, peer, slot):
        ref = place(piece, *loc)
        return pltpu.make_async_remote_copy(
            src_ref=ref,
            dst_ref=ref,
            send_sem=ag_send.at[piece, slot],
            recv_sem=ag_recv.at[piece, slot],
            device_id=peer,
            device_id_type=MESH,
        )

    own = (z, y, x, c)

    def behind(k):
        return (z + ZN - k) % ZN

    def spot(kind, k):
        return (behind(k), y if kind in (0, 2) else 1 - y, x if kind in (0, 1) else 1 - x, c)

    def forward(piece, kind, k, peer, slot):
        tag = "mix" if piece < 3 else ("near" if kind < 2 else "far")
        out.go(ag(piece, spot(kind, k), peer, slot), tag)

    def to_core(piece, kind, k):
        forward(piece, kind, k, core_peer, 15 + kind * 4 + k)

    def arrived(piece, slot):
        ag(piece, own, core_peer, slot).wait_recv()

    def turns_y(piece):
        return gather_pieces[piece][3]

    def start_z(piece):
        for k in (1, 3, 2):
            forward(piece, 0, 0, z_peers[k - 1], k - 1)

    def start_side(piece):
        forward(piece, 0, 0, y_peer, 3)
        forward(piece, 0, 0, x_peer, 7)
        to_core(piece, 0, 0)

    def gather_z(piece, k):
        arrived(piece, k - 1)
        forward(piece, 0, k, y_peer, 3 + k)
        forward(piece, 0, k, x_peer, 7 + k)
        to_core(piece, 0, k)

    def gather_turn(piece, k):
        if turns_y(piece):
            arrived(piece, 3 + k)
            forward(piece, 1, k, x_peer, 11 + k)
            to_core(piece, 1, k)
        else:
            arrived(piece, 7 + k)
            forward(piece, 2, k, y_peer, 11 + k)
            to_core(piece, 2, k)

    def gather_side(piece, k):
        if turns_y(piece):
            arrived(piece, 7 + k)
            to_core(piece, 2, k)
        else:
            arrived(piece, 3 + k)
            to_core(piece, 1, k)

    def gather_last(piece, k):
        arrived(piece, 11 + k)
        to_core(piece, 3, k)

    def gather_core(piece, kinds=(0, 1, 2, 3)):
        for kind in kinds:
            for k in range(ZN):
                arrived(piece, 15 + kind * 4 + k)

    home = pl.ds(pl.multiple_of(group * rows, 32), rows)
    mix_w[mp, home, :] = jnp.concatenate(
        [wq_ref[0], wq_ref[1], wq_ref[2], wo_ref[...].T], axis=1
    ).astype(BF)
    flip = (
        lax.broadcasted_iota(jnp.int32, (window, window), 0)
        + lax.broadcasted_iota(jnp.int32, (window, window), 1)
        == window - 1
    ).astype(F32)
    band_rows[group * 4 + mp] = dot_nn(
        jnp.exp(bias_ref[...]).astype(BF), flip.astype(BF)
    ).astype(BF)

    barrier = pltpu.get_barrier_semaphore()
    friends = [core_peer, x_peer, y_peer, diag_peer] + z_peers
    for friend in friends:
        pl.semaphore_signal(barrier, inc=1, device_id=friend, device_id_type=MESH)
    here = group * 4 + mp
    moves = here != mp * GROUPS + group
    if last_hop:

        @pl.when(moves)
        def _():
            pl.semaphore_signal(
                barrier,
                inc=1,
                device_id=(here % GROUPS, inner, here // GROUPS),
                device_id_type=MESH,
            )
            pl.semaphore_wait(barrier, len(friends) + 1)

        @pl.when(jnp.logical_not(moves))
        def _():
            pl.semaphore_wait(barrier, len(friends))

    else:
        pl.semaphore_wait(barrier, len(friends))

    halo_copy = pltpu.make_async_remote_copy(
        src_ref=x_ref.at[pl.ds(tokens - window, window)],
        dst_ref=x_halo,
        send_sem=halo_send.at[0],
        recv_sem=halo_recv.at[0],
        device_id=(group, inner, (mp + 1) % 4),
        device_id_type=MESH,
    )

    stats[0] = jnp.zeros(stats.shape[1:], F32)

    def add_stat(row, value):
        stats[0, row : row + 1, :] += jnp.sum(value, axis=0, keepdims=True)

    def rms(value):
        return lax.rsqrt(jnp.mean(value * value, axis=-1, keepdims=True) + EPS)

    def mask_at(at):
        spots = lax.broadcasted_iota(jnp.int32, (CHUNK, width), 0) + (at + mp * tokens)
        return (spots < len_ref[0]).astype(F32)

    def norm_own(at):
        part = pl.ds(at, CHUNK)
        xf = x_ref[part].astype(F32)
        normed[pl.ds(at + window, CHUNK)] = (xf * rms(xf) * gains_ref[0:1]).astype(BF)
        mask = mask_at(at)
        add_stat(2, mask * xf * xf)
        add_stat(5, mask)
        cot_low[part] = (cot_ref[part].astype(F32) * mask).astype(BF)

    def norm_halo(at):
        part = pl.ds(at, CHUNK)
        xf = x_halo[part].astype(F32)
        normed[part] = (xf * rms(xf) * gains_ref[0:1]).astype(BF)

    def repack(at):
        part = pl.ds(at, rows)
        for kind in range(4):
            full_w[kind, part] = jnp.concatenate(
                [mix_w[m, part, kind * chan : (kind + 1) * chan] for m in range(4)], axis=1
            )

    def project_halo(at):
        part = pl.ds(at, CHUNK)
        a = normed[part]
        ek = jnp.where(mp > 0, jnp.exp(dot_nn(a, full_w[1])), 0.0)
        exp_low[part] = ek.astype(BF)
        kv_low[part] = (ek * dot_nn(a, full_w[2])).astype(BF)

    def project_own(at):
        part = pl.ds(at, CHUNK)
        shifted = pl.ds(at + window, CHUNK)
        a = normed[shifted]
        ek = jnp.exp(dot_nn(a, full_w[1]))
        v = dot_nn(a, full_w[2])
        exp_low[shifted] = ek.astype(BF)
        kv_low[shifted] = (ek * v).astype(BF)
        expk[part] = ek
        val[part] = v
        sig[part] = jax.nn.sigmoid(dot_nn(a, full_w[0]))

    def build_bands():
        for i in range(3):
            raw = band_rows[pl.ds(mp * 8 + i * 4, 4)].reshape(window, window).astype(F32)
            wide = jnp.concatenate([raw, jnp.zeros_like(raw)], axis=1)
            bands[i] = pltpu.roll(wide, 1, 1, stride=1, stride_axis=0).astype(BF)

    def mix_rows(i):
        part = slice(i * window, (i + 1) * window)
        near = slice(i * window, (i + 2) * window)
        num = dot_nn(bands[i], kv_low[near])
        den = dot_nn(bands[i], exp_low[near])
        ratio[part] = num / den
        rden[part] = 1.0 / den

    def attend(at):
        part = pl.ds(at, CHUNK)
        low = (sig[part] * ratio[part]).astype(BF)
        mixed[part] = low
        attn = dot_nt(low, full_w[3])
        add_stat(3, mask_at(at) * attn * attn)
        total = x_ref[part].astype(F32) + attn
        resid[part] = total
        normed_two[part] = (total * rms(total) * gains_ref[1:2]).astype(BF)

    def hidden_rows(m, first):
        def body(at):
            part = pl.ds(at, CHUNK)
            p = dot_nn(normed_two[part], up_w[m])
            da = dot_nn(cot_low[part], down_w[m])
            t = jnp.tanh(GELU_C * (p + GELU_A * (p * p * p)))
            low = (0.5 * p * (1.0 + t)).astype(BF)
            slope = 0.5 * (1.0 + t) + 0.5 * p * (1.0 - t * t) * (
                GELU_C * (1.0 + 3.0 * GELU_A * (p * p))
            )
            dlow = (da * slope).astype(BF)
            act[part] = low
            dpre[part] = dlow
            f = dot_nt(low, down_w[m])
            d = dot_nt(dlow, up_w[m])
            if first:
                ffn[part] = f
                dn_two[part] = d
            else:
                ffn[part] += f
                dn_two[part] += d

        return body

    def weight_grad(result, left, right):
        for at in range(0, result.shape[1], 256):
            part = slice(at, at + 256)
            result[:, part] = dot_tn(left[...], right[:, part]).astype(result.dtype)

    def close_hidden(at):
        part = pl.ds(at, CHUNK)
        mask = mask_at(at)
        f = ffn[part]
        res = resid[part]
        add_stat(4, mask * f * f)
        blk_ref[part] = (res + f).astype(BF)
        d = dn_two[part]
        r = rms(res)
        u = gains_ref[1:2] * d
        grad = (
            cot_ref[part].astype(F32) * mask
            + r * u
            - res * (r * r * r) * jnp.mean(u * res, axis=-1, keepdims=True)
        )
        add_stat(1, d * res * r)
        ffn[part] = grad
        act[part] = grad.astype(BF)

    def back_attend(at):
        part = pl.ds(at, CHUNK)
        dm = dot_nn(act[part], full_w[3])
        sg = sig[part]
        rt = ratio[part]
        scaled = dm * sg
        normed_two[part] = (scaled * rt * (1.0 - sg)).astype(BF)
        dn = scaled * rden[part]
        dnum[part] = dn.astype(BF)
        dden[part] = (-dn * rt).astype(BF)

    def halo_back(slot, buf):
        return pltpu.make_async_remote_copy(
            src_ref=buf.at[pl.ds(0, window)],
            dst_ref=buf.at[pl.ds(tokens, window)],
            send_sem=halo_send.at[slot],
            recv_sem=halo_recv.at[slot],
            device_id=(group, inner, (mp + 3) % 4),
            device_id_type=MESH,
        )

    def band_grad(i):
        part = slice(i * window, (i + 1) * window)
        near = slice(i * window, (i + 2) * window)
        dn_two[part, 0 : 2 * window] = dot_nt(dnum[part], kv_low[near]) + dot_nt(dden[part], exp_low[near])

    def unskew(j):
        wide = 2 * window
        count = bias_part.shape[1]
        line = lax.broadcasted_iota(jnp.int32, (count, wide), 0)
        v = dn_two[j * count : (j + 1) * count, 0:wide]
        v = pltpu.roll(v, wide - 1 - (j * count) % window, 1)
        bit = 1
        while bit < count:
            v = jnp.where((line & bit) != 0, pltpu.roll(v, wide - bit, 1), v)
            bit *= 2
        bias_part[j] = v[:, 0:window].astype(BF)

    def back_keys(j):
        here = slice(j * window, (j + 1) * window)
        then = slice((j + 1) * window, (j + 2) * window)
        right = bands[j, :, window:]
        left = bands[j + 1, :, :window]
        dkv = dot_tn(right, dnum[here]) + dot_tn(left, dnum[then])
        de = dot_tn(right, dden[here]) + dot_tn(left, dden[then])
        ek = expk[here]
        cot_low[here] = (dkv * ek).astype(BF)
        dpre[here] = ((de + dkv * val[here]) * ek).astype(BF)

    def back_input(at):
        part = pl.ds(at, CHUNK)
        d = (
            dot_nt(normed_two[part], full_w[0])
            + dot_nt(dpre[part], full_w[1])
            + dot_nt(cot_low[part], full_w[2])
        )
        xf = x_ref[part].astype(F32)
        r = rms(xf)
        u = gains_ref[0:1] * d
        gin_ref[part] = (
            ffn[part] + r * u - xf * (r * r * r) * jnp.mean(u * xf, axis=-1, keepdims=True)
        )
        add_stat(0, d * xf * r)

    def mix_grad(kind):
        grad = (normed_two, dpre, cot_low)[kind]
        result = wide_rows.at[pl.ds(kind * GROUPS * rows, GROUPS * rows)]
        weight_grad(result, normed.at[pl.ds(window, tokens)], grad)

    def unpack(kinds):
        def body(at):
            part = pl.ds(at, rows)
            for m in range(4):
                mine = slice(m * chan, (m + 1) * chan)
                pair = [
                    full_w[3, part, mine]
                    if kind == 3
                    else wide_rows[pl.ds(at + kind * GROUPS * rows, rows), mine].astype(BF)
                    for kind in kinds
                ]
                span = slice(kinds[0] * chan, (kinds[-1] + 1) * chan)
                mix_w[m, part, span] = jnp.concatenate(pair, axis=1)

        return body

    scatter_pieces = [
        (mix_w, 0, half, True, None, 0),
        (mix_w, half, half, False, None, half),
        (up_w, 0, up_w.shape[2], False, gu_ref, 2 * half),
        (down_w, 0, down_w.shape[2], False, gd_ref, 2 * half + up_w.shape[2]),
    ]

    def rs(piece, src, dst, peer, slot):
        return pltpu.make_async_remote_copy(
            src_ref=src,
            dst_ref=dst,
            send_sem=rs_send.at[piece, slot],
            recv_sem=rs_recv.at[piece, slot],
            device_id=peer,
            device_id_type=MESH,
        )

    def x_of(far):
        return 1 - x if far else x

    def block(piece, xs, zs, ys):
        buf, start, size = scatter_pieces[piece][:3]
        at = pl.multiple_of((zs * YN + ys) * rows, 32)
        return buf.at[xs * 2 + c, pl.ds(at, rows), pl.ds(start, size)]

    def lanes(piece):
        return pl.ds(scatter_pieces[piece][5], scatter_pieces[piece][2])

    def core_copy(p, far):
        buf, start, size = scatter_pieces[p][:3]
        src = buf.at[x_of(far) * 2 + 1 - c, :, pl.ds(start, size)]
        return rs(p, src, recv_core.at[far, :, lanes(p)], core_peer, far)

    def core_send(p, far):
        out.go(core_copy(p, far))

    def core_sum(p, far):
        buf, start, size = scatter_pieces[p][:3]
        core_copy(p, far).wait_recv()

        def body(at):
            part = pl.ds(at, rows)
            buf[x_of(far) * 2 + c, part, pl.ds(start, size)] += recv_core[far, part, lanes(p)]

        loop_rows(GROUPS * rows, rows, body)

    def y_copy(p, far, k):
        src = block(p, x_of(far), behind(k), 1 - y)
        return rs(p, src, recv_one.at[far * ZN + k, :, lanes(p)], y_peer, 2 + far * ZN + k)

    def y_send(p, far):
        for k in (1, 2, 3, 0):
            out.go(y_copy(p, far, k))

    def y_take(p, far, k):
        y_copy(p, far, k).wait_recv()
        spot_ref = block(p, x_of(far), behind(k), y)
        spot_ref[...] += recv_one[far * ZN + k, :, lanes(p)]

    def x_copy(p, k):
        src = block(p, 1 - x, behind(k), y)
        return rs(p, src, recv_two.at[k, :, lanes(p)], x_peer, 10 + k)

    def x_take(p, k):
        x_copy(p, k).wait_recv()
        spot_ref = block(p, x, behind(k), y)
        spot_ref[...] += recv_two[k, :, lanes(p)]

    def z_copy(p, k):
        src = block(p, x, behind(k), y)
        return rs(p, src, recv_z.at[k - 1, :, lanes(p)], z_peers[ZN - 1 - k], 13 + k)

    def z_take(p):
        total = block(p, x, z, y)[...].astype(F32)
        for k in range(1, ZN):
            z_copy(p, k).wait_recv()
            total = total + recv_z[k - 1, :, lanes(p)].astype(F32)
        if p == 0:
            gq_ref[0] = total[:, :chan]
            gq_ref[1] = total[:, chan:]
        elif p == 1:
            gq_ref[2] = total[:, :chan]
            go_ref[...] = total[:, chan:].T
        else:
            scatter_pieces[p][4][...] = total

    def y_turn(p, k):
        y_take(p, 1, k)
        out.go(x_copy(p, k))

    def x_end(p, k):
        x_take(p, k)
        if k:
            out.go(z_copy(p, k))

    def wide_copy(p, k, ys):
        src = block(p, 1 - x, behind(k), ys)
        slot = k if ys is y else ZN + k
        return rs(p, src, recv_one.at[slot, :, lanes(p)], x_peer, 2 + slot)

    def wide_send(p):
        for k in (1, 2, 3, 0):
            out.go(wide_copy(p, k, other_y))
        for k in (1, 2, 3, 0):
            out.go(wide_copy(p, k, y))

    def wide_take(p, k, ys):
        wide_copy(p, k, ys).wait_recv()
        slot = k if ys is y else ZN + k
        spot_ref = block(p, x, behind(k), ys)
        spot_ref[...] += recv_one[slot, :, lanes(p)]

    def late_copy(p, k):
        src = block(p, x, behind(k), 1 - y)
        return rs(p, src, recv_two.at[k, :, lanes(p)], y_peer, 10 + k)

    def wide_turn(p, k):
        wide_take(p, k, other_y)
        out.go(late_copy(p, k))

    def late_end(p, k):
        wide_take(p, k, y)
        late_copy(p, k).wait_recv()
        spot_ref = block(p, x, behind(k), y)
        spot_ref[...] += recv_two[k, :, lanes(p)]
        if k:
            out.go(z_copy(p, k))

    other_y = 1 - y

    def bias_copy(src, dst, peer, slot):
        return pltpu.make_async_remote_copy(
            src_ref=src,
            dst_ref=dst,
            send_sem=bias_send.at[slot],
            recv_sem=bias_recv.at[slot],
            device_id=peer,
            device_id_type=MESH,
        )

    def bias_y(k):
        return bias_copy(
            bias_part.at[behind(k) * YN + 1 - y], bias_recv_y.at[k], y_peer, k
        )

    def bias_z(k):
        return bias_copy(
            bias_part.at[behind(k) * YN + y], bias_recv_z.at[k - 1], z_peers[ZN - 1 - k], 3 + k
        )

    def bias_turn():
        for k in (1, 2, 3, 0):
            bias_y(k).wait_recv()
            bias_part[behind(k) * YN + y] += bias_recv_y[k]
            if k:
                out.go(bias_z(k))

    def close_bias():
        total = bias_part[z * YN + y].astype(F32)
        for k in range(1, ZN):
            bias_z(k).wait_recv()
            total = total + bias_recv_z[k - 1].astype(F32)
        bias_hop[0] = jnp.dot(
            total, flip, precision=lax.Precision.HIGHEST, preferred_element_type=F32
        )

    def hop_copy():
        owner = mp * GROUPS + group
        return pltpu.make_async_remote_copy(
            src_ref=bias_hop.at[0],
            dst_ref=bias_hop.at[1],
            send_sem=bias_send.at[7],
            recv_sem=bias_recv.at[7],
            device_id=(owner // 4, inner, owner % 4),
            device_id_type=MESH,
        )

    def reduce_stats():
        def copy(step, slot, peer):
            return pltpu.make_async_remote_copy(
                src_ref=stats.at[step],
                dst_ref=stats_recv.at[slot],
                send_sem=stat_send.at[slot],
                recv_sem=stat_recv.at[slot],
                device_id=peer,
                device_id_type=MESH,
            )

        return copy

    def stats_step(step):
        copy = reduce_stats()
        peer = (core_peer, x_peer, y_peer)[step]
        copy(step, step, peer).wait_recv()
        stats[step + 1] = stats[step] + stats_recv[step]

    def stats_send(step):
        copy = reduce_stats()
        if step < 3:
            out.go(copy(step, step, (core_peer, x_peer, y_peer)[step]))
        else:
            for k in range(1, ZN):
                out.go(copy(3, 2 + k, z_peers[k - 1]))

    def stats_end():
        copy = reduce_stats()
        total = stats[3]
        for k in range(1, ZN):
            copy(3, 2 + k, z_peers[k - 1]).wait_recv()
            total = total + stats_recv[2 + k]
        stat_ref[...] = total

    steps = (0, 1, 3, 2)
    early, late = (0, 1, 2), (3, 4)

    @pl.when(mp < 3)
    def _():
        halo_copy.start()

    band_rows[4 * GROUPS : 4 * GROUPS + 4] = jnp.zeros((4, *bias_ref.shape), BF)
    for p in early:
        start_z(p)
    for p in early:
        start_side(p)
    up_w[mp, home, :] = wu_ref[...].astype(BF)
    down_w[mp, home, :] = wd_ref[...].astype(BF)
    loop_rows(tokens, CHUNK, norm_own)
    for k in steps[1:]:
        for p in early:
            gather_z(p, k)
    for p in late:
        start_z(p)
    for step in (gather_turn, gather_side):
        for k in steps:
            for p in early:
                step(p, k)
    for p in late:
        start_side(p)
    for k in steps:
        for p in early:
            gather_last(p, k)

    @pl.when(mp > 0)
    def _():
        halo_copy.wait_recv()

    @pl.when(mp == 0)
    def _():
        x_halo[...] = jnp.zeros_like(x_halo)

    loop_rows(window, CHUNK, norm_halo)
    for k in steps[1:]:
        for p in late:
            gather_z(p, k)
    for p in early:
        gather_core(p)
    tasks = [
        functools.partial(step, p, k)
        for step in (gather_turn, gather_side, gather_last)
        for k in steps
        for p in late
    ]

    def beside(count):
        for _ in range(min(count, len(tasks))):
            tasks.pop(0)()

    loop_rows(GROUPS * rows, rows, repack)
    build_bands()
    for at in range(0, window, CHUNK):
        project_halo(at)
        beside(1)
    for at in range(0, tokens, CHUNK):
        project_own(at)
        beside(1)
    for i in range(2):
        mix_rows(i)
        beside(2)
    for at in range(0, tokens, CHUNK):
        attend(at)
        beside(2)

    def slab(r):
        return x_of(r // 2) * 2 + (1 - c if r % 2 else c)

    beside(len(tasks) - 2 * ZN)
    for r in (1, 0, 3, 2):
        if r % 2:
            if r == 3:
                beside(len(tasks))
            for p in late:
                gather_core(p, (r - 1, r))
        loop_rows(tokens, CHUNK, hidden_rows(slab(r), r == 1))
        beside(2)
        if r % 2 == 0:
            out.drain("far" if r else "near")
        weight_grad(up_w.at[slab(r)], normed_two, dpre)
        if r % 2:
            core_send(2, r // 2)
        else:
            core_sum(2, r // 2)
            y_send(2, r // 2)
        beside(2)
        weight_grad(down_w.at[slab(r)], cot_low, act)
        if r % 2:
            core_send(3, r // 2)
        else:
            core_sum(3, r // 2)
            y_send(3, r // 2)
    for k in steps:
        y_take(2, 0, k)
        y_take(3, 0, k)
    loop_rows(tokens, CHUNK, close_hidden)
    loop_rows(tokens, CHUNK, back_attend)

    backs = [halo_back(1, dnum), halo_back(2, dden)]

    @pl.when(mp > 0)
    def _():
        for item in backs:
            item.start()

    weight_grad(full_w.at[3], act, mixed)
    mix_grad(0)
    for k in (1, 2, 3, 0):
        y_turn(2, k)
    for i in range(2):
        band_grad(i)
    for j in range(GROUPS):
        unskew(j)
    for k in (1, 2, 3, 0):
        out.go(bias_y(k))

    @pl.when(mp < 3)
    def _():
        for item in backs:
            item.wait_recv()

    @pl.when(mp == 3)
    def _():
        dnum[pl.ds(tokens, window)] = jnp.zeros((window, width), BF)
        dden[pl.ds(tokens, window)] = jnp.zeros((window, width), BF)

    for j in range(2):
        back_keys(j)
    mix_grad(1)
    out.drain("mix")
    loop_rows(GROUPS * rows, rows, unpack((0, 1)))
    core_send(0, 1)
    core_send(0, 0)
    mix_grad(2)
    loop_rows(GROUPS * rows, rows, unpack((2, 3)))
    core_send(1, 1)
    core_send(1, 0)
    for k in (1, 2, 3, 0):
        y_turn(3, k)
    core_sum(0, 1)
    wide_send(0)
    core_sum(1, 1)
    y_send(1, 1)
    core_sum(1, 0)
    y_send(1, 0)
    core_sum(0, 0)
    bias_turn()
    for at, k in zip(range(0, tokens, CHUNK), (1, 2, 3, 0), strict=True):
        back_input(at)
        x_end(2, k)
    stats_send(0)
    close_bias()
    if last_hop:

        @pl.when(moves)
        def _():
            hop_copy().start()

    for k in (1, 2, 3, 0):
        x_end(3, k)
    stats_step(0)
    stats_send(1)
    for k in (1, 2, 3, 0):
        wide_turn(0, k)
        y_turn(1, k)
    stats_step(1)
    stats_send(2)
    z_take(2)
    for k in (1, 2, 3, 0):
        y_take(1, 0, k)
        late_end(0, k)
        x_end(1, k)
    stats_step(2)
    stats_send(3)
    z_take(3)
    if last_hop:

        @pl.when(moves)
        def _():
            hop_copy().wait_recv()
            gb_ref[...] = bias_hop[1]

        @pl.when(jnp.logical_not(moves))
        def _():
            gb_ref[...] = bias_hop[0]

    else:
        gb_ref[...] = bias_hop[0]
    stats_end()
    z_take(0)
    z_take(1)

    @pl.when(mp < 3)
    def _():
        halo_copy.wait_send()

    @pl.when(mp > 0)
    def _():
        for item in backs:
            item.wait_send()

    if last_hop:

        @pl.when(moves)
        def _():
            hop_copy().wait_send()

    out.drain()


def run_block(lengths, x, cot, gains, wq, wo, wu, wd, bias, last_hop):
    tokens, width = x.shape
    window = bias.shape[1]
    rows = wu.shape[0]
    full = rows * GROUPS
    mix_width = 4 * wq.shape[2]
    hidden = wu.shape[1]
    lanes = mix_width + 2 * hidden
    vmem = pl.BlockSpec(memory_space=pltpu.VMEM)

    def shape(*dims, kind=F32):
        return jax.ShapeDtypeStruct(dims, kind)

    def buf(*dims):
        return pltpu.VMEM(dims, F32)

    def low(*dims):
        return pltpu.VMEM(dims, BF)

    dma = pltpu.SemaphoreType.DMA
    return pl.pallas_call(
        functools.partial(block_kernel, last_hop),
        out_shape=(
            shape(tokens, width, kind=BF),
            shape(tokens, width),
            shape(*wq.shape),
            shape(*wo.shape),
            shape(*wu.shape),
            shape(*wd.shape),
            shape(*bias.shape),
            shape(8, width),
        ),
        in_specs=[pl.BlockSpec(memory_space=pltpu.SMEM)] + [vmem] * 8,
        out_specs=(vmem,) * 8,
        scratch_shapes=[
            low(4, full, mix_width),
            low(4, full, hidden),
            low(4, full, hidden),
            low(4 * GROUPS + 4, *bias.shape),
            low(window, width),
            low(4, full, width),
            low(window + tokens, width),
            buf(5 * tokens, width),
            buf(tokens, width),
            low(window + tokens, width),
            low(window + tokens, width),
            low(3, window, 2 * window),
            low(tokens, width),
            low(tokens, width),
            low(tokens, width),
            low(tokens, hidden),
            low(tokens, hidden),
            buf(tokens, width),
            low(tokens + window, width),
            low(tokens + window, width),
            low(GROUPS, *bias.shape),
            low(ZN, *bias.shape),
            low(ZN - 1, *bias.shape),
            buf(2, *bias.shape),
            buf(4, 8, width),
            buf(6, 8, width),
            low(2, full, lanes),
            low(GROUPS, rows, lanes),
            low(ZN, rows, lanes),
            low(ZN - 1, rows, lanes),
            dma((5, 31)),
            dma((5, 31)),
            dma((4, 17)),
            dma((4, 17)),
            dma((3,)),
            dma((3,)),
            dma((8,)),
            dma((8,)),
            dma((6,)),
            dma((6,)),
        ],
        compiler_params=pltpu.CompilerParams(
            collective_id=0, has_side_effects=True, vmem_limit_bytes=63 * 1024 * 1024
        ),
    )(lengths, x, cot, gains, wq, wo, wu, wd, bias)


MESH = pl.DeviceIdType.MESH


def adam_kernel(scale, *refs):
    grads, refs = refs[:6], refs[6:]
    params, refs = refs[:6], refs[6:]
    firsts, refs = refs[:6], refs[6:]
    seconds, refs = refs[:6], refs[6:]
    out_grads, out_firsts, out_seconds, out_updates = (
        refs[6 * i : 6 * i + 6] for i in range(4)
    )
    rms_ref = refs[24]
    one = 1.0 / (1.0 - BETA_ONE**ADAM_STEP)
    two = 1.0 / (1.0 - BETA_TWO**ADAM_STEP)
    for i in range(6):
        if i == 4:
            grad = grads[4][...] * jnp.exp(params[4][...])
        elif i == 5:
            grad = grads[5][0:2]
        else:
            grad = grads[i][...]
        grad = grad * scale
        first = BETA_ONE * firsts[i][...] + (1.0 - BETA_ONE) * grad
        second = BETA_TWO * seconds[i][...] + (1.0 - BETA_TWO) * (grad * grad)
        step = (first * one) / (jnp.sqrt(second * two) + ADAM_EPS)
        if i < 4:
            step = step + WEIGHT_DECAY * params[i][...]
        out_grads[i][...] = grad
        out_firsts[i][...] = first
        out_seconds[i][...] = second
        out_updates[i][...] = -LEARN_RATE * step
    sums = jnp.sum(grads[5][...], axis=1, keepdims=True)
    rms_ref[...] = jnp.sqrt(sums[2:5] / sums[5:6])


def run_adam(scale, grads, params, firsts, seconds):
    vmem = pl.BlockSpec(memory_space=pltpu.VMEM)
    kinds = [jax.ShapeDtypeStruct(param.shape, F32) for param in params]
    return pl.pallas_call(
        functools.partial(adam_kernel, scale),
        out_shape=(*(kinds * 4), jax.ShapeDtypeStruct((3, 1), F32)),
        in_specs=[vmem] * 24,
        out_specs=(vmem,) * 25,
        compiler_params=pltpu.CompilerParams(vmem_limit_bytes=62 * 1024 * 1024),
    )(*grads, *params, *firsts, *seconds)


def stored(items):
    qkv, mix, up, down, bias, gains = items
    return [qkv.transpose(1, 0, 2), mix, up, down.T, bias, gains]


def shards(inner, block_input, out_cotangent, lengths, *rest):
    params, firsts, seconds = (stored(rest[6 * i : 6 * i + 6]) for i in range(3))
    held = params
    if inner > 1:
        axes = (1, 1, 0, 0)
        held = [
            lax.all_gather(item.astype(BF), "dpl", axis=axis, tiled=True).astype(F32)
            for item, axis in zip(params[:4], axes, strict=True)
        ]
        count = params[4].shape[0]
        every = lax.all_gather(params[4], ("dpl", "mp"), axis=0, tiled=True)
        at = lax.axis_index("mp") * inner * count
        held += [lax.dynamic_slice_in_dim(every, at, inner * count, 0), params[5]]
    block_low, grad_input, *grads = run_block(
        lengths,
        block_input[0],
        out_cotangent[0],
        held[5],
        *held[:5],
        inner == 1,
    )
    if inner > 1:
        for i, axis in enumerate(axes):
            grads[i] = lax.psum_scatter(grads[i], "dpl", scatter_dimension=axis, tiled=True)
        grads[4], grads[5] = lax.psum((grads[4], grads[5]), "dpl")
        every = lax.all_gather(grads[4], ("mp", "dph"), axis=0, tiled=True)
        place = lax.axis_index(("dph", "dpl", "mp"))
        grads[4] = lax.dynamic_slice_in_dim(every, place * count, count, 0)
    scale = float(lax.axis_size("dph") * inner * LEN) ** (-0.5)
    *results, rms_stats = run_adam(scale, grads, params, firsts, seconds)
    outs = []
    for i in range(4):
        qkv, mix, up, down, bias, gains = results[6 * i : 6 * i + 6]
        outs += [qkv.transpose(1, 0, 2), mix, up, down.T, bias, gains]
    return (block_low[None], grad_input[None], *outs, rms_stats[:, 0])


def solution(mesh):
    inner = mesh.shape["dp"] // GROUPS
    fine = Mesh(
        mesh.devices.reshape(GROUPS, inner, mesh.shape["mp"]),
        ("dph", "dpl", "mp"),
    )
    dp = ("dph", "dpl")
    weights = (
        P(dp, None, "mp"),
        P("mp", dp),
        P(dp, "mp"),
        P("mp", dp),
        P((*dp, "mp"), None),
        P(),
    )
    acts = P(dp, "mp", None)
    return jax.shard_map(
        functools.partial(shards, inner),
        mesh=fine,
        in_specs=(acts, acts, P(dp), *weights, *weights, *weights),
        out_specs=(acts, acts, *weights, *weights, *weights, *weights, P()),
        check_vma=False,
    )
```

time: 319 us -> 204 us (0.64)
  Pallas kernels: 282 us -> 197 us
  other arithmetic: 16.1 us -> 1.43 us
  local copies, waits for them, and re-layouts: 13.7 us -> 2.03 us
    pallas_call x1 -> x2, Pallas kernels: 282 us -> 197 us  [the longest x1 192 us: run_block(): pl.pallas_call(functools.partial(block_kernel, last_hop), out_shape=(shap...]
    mul x8 -> x0, other arithmetic: 10.1 us -> none  [the longest x6 7.43 us: adam_step(): -LEARN_RATE]
    unnamed x64 -> x6, local copies, waits for them, and re-layouts: 10.6 us -> 2.03 us
    convert_element_type x4 -> x0, other arithmetic: 3.26 us -> none  [the longest x1 0.98 us: shards(): w_qkv.reshape(w_qkv.shape[0], 3 * chan).astype(BF)]
  transfers between devices with their start and end apart: 1 -> 0, of which waited for: 0 -> 0; matrix products, arithmetic and copies ran while one was open for 6% -> 0% of each run, Pallas kernels for 0% -> 0%
where the time goes in v2:
time: 204 us; the launch traced here: 202 us
  Pallas kernels  197 us (97%)
    pallas_call x1, Pallas kernels, run_block(): pl.pallas_call(functools.partial(block_kernel, last_hop), out_shape=(shap...  192 us
    pallas_call x1, Pallas kernels, run_adam(): pl.pallas_call(functools.partial(adam_kernel, scale), out_shape=(*kinds *...  5.34 us

profile of v2, /device:TPU:4, one launch (start us, length us, event | category | flops | bytes accessed | tf_op | source)
XLA Modules:
  0.0 201.8 jit_solution(12184755687908824021)
XLA Ops:
  1.3 191.6 %shard_map.412 = (bf16[512,768]{1,0:T(8,128)(2,1)}, f32[512,768]{1,0:T(8,128)}, f32[3,96,192]{2,1,0:T(8,128)}, f32[192,96]{1,0:T(8,128)}, f32[96,768]{1,0:T(8,12...) custom-call(s32[1]{0:T(128)S(6)} %copy.50.len_ref, bf16[512,768]{1,0:T(8,128)(2,1)} %bitcast.24, ...), custom_call_target="tpu_custom_call" | custom-call | tf_op jit(solution)/shard_map/pallas_call | solution.py:942
  193.0 0.0 copy-start.1
  193.0 5.3 %shard_map.413 = (f32[3,96,192]{2,1,0:T(8,128)}, f32[192,96]{1,0:T(8,128)}, f32[96,768]{1,0:T(8,128)}, f32[96,768]{1,0:T(8,128)}, f32[64,256]{1,0:T(8,128)}, /*i...) custom-call(f32[3,96,192]{2,1,0:T(8,128)} %get-tuple-element.62.refs, ...), custom_call_target="tpu_custom_call" | custom-call | tf_op jit(solution)/shard_map/pallas_call | solution.py:1042
  198.3 0.0 copy-start
  198.3 1.4 reduce
  199.8 0.0 copy-done.1
  199.8 0.9 copy.51
  200.6 0.0 copy-done
  200.6 1.1 copy.52
Async XLA Ops:
  193.0 6.8 %copy-start.1 = (bf16[512,768]{1,0:T(8,128)(2,1)S(1)}, bf16[512,768]{1,0:T(8,128)(2,1)}, u32[]{:S(2)}) copy-start(bf16[512,768]{1,0:T(8,128)(2,1)} %get-tuple-element.60) | copy-start | bytes 2359300
  198.3 2.3 %copy-start = (f32[512,768]{1,0:T(8,128)S(1)}, f32[512,768]{1,0:T(8,128)}, u32[]{:S(2)}) copy-start(f32[512,768]{1,0:T(8,128)} %get-tuple-element.61) | copy-start | bytes 4718596

commit v3 on v2

--- a/solution.py
+++ b/solution.py
@@ -21,9 +21,48 @@
 BF = jnp.bfloat16
 ZN, YN = 4, 2
 GROUPS = ZN * YN
-CHUNK = 128
+CHUNK = 256
 GELU_C = 0.7978845608028654
 GELU_A = 0.044715
+
+
+ROUTES = ((True, False), (False, False), (True, True), (True, False), (False, True))
+LINE_SUMS = (False, True, False, True)
+SCHEDULE = (
+    ("send_x", 2), ("send_x", 0), ("send_z", 2), ("send_x", 1), ("send_y", 0), ("send_y", 1),
+    ("send_z", 1), ("send_z", 0), ("send_y", 2), ("y", 0, 0), ("z", 2, 1), ("z", 2, 2),
+    ("z", 1, 1), ("x", 1, 0), ("send_c", 1), ("z", 0, 1), ("y", 2, 0), ("norm",), ("z", 0, 2),
+    ("send_z", 3), ("send_x", 3), ("z", 0, 3), ("z", 2, 3), ("x", 2, 0), ("x", 2, 1),
+    ("z", 1, 2), ("x", 2, 2), ("y", 0, 1), ("send_y", 3), ("y", 0, 2), ("y", 0, 3), ("y", 1, 0),
+    ("d", 2, 0), ("send_y", 4), ("d", 2, 1), ("d", 1, 0), ("y", 2, 1), ("y", 2, 2), ("z", 1, 3),
+    ("z", 3, 1), ("z", 3, 2), ("x", 3, 0), ("send_c", 2), ("x", 0, 0), ("x", 0, 1), ("y", 1, 1),
+    ("x", 1, 1), ("x", 1, 2), ("d", 0, 0), ("d", 0, 1), ("y", 2, 3), ("send_x", 4), ("x", 1, 3),
+    ("halo",), ("z", 3, 3), ("d", 2, 2), ("d", 2, 3), ("send_z", 4), ("d", 1, 1), ("y", 1, 2),
+    ("y", 1, 3), ("x", 0, 2), ("x", 0, 3), ("send_c", 0), ("z", 4, 1), ("x", 2, 3), ("bands",),
+    ("d", 1, 2), ("d", 1, 3), ("y", 3, 0), ("y", 3, 1), ("send_c", 4), ("d", 0, 2), ("d", 0, 3),
+    ("x", 4, 0), ("send_c", 3), ("y", 3, 2), ("y", 3, 3), ("z", 4, 2), ("z", 4, 3), ("repack",),
+    ("y", 4, 0), ("d", 4, 0), ("proj", 0), ("proj", 1), ("y", 4, 1), ("y", 4, 2), ("halow",),
+    ("mix", 0), ("mix", 1), ("att", 0), ("att", 1), ("y", 4, 3), ("x", 4, 1), ("d", 3, 0),
+    ("x", 3, 1), ("x", 3, 2), ("x", 3, 3), ("h", 1, 0), ("d", 4, 1), ("h", 1, 1), ("g", 1, 0),
+    ("cs", 2, 0), ("d", 3, 1), ("d", 4, 2), ("g", 1, 1), ("h", 0, 0), ("d", 3, 2), ("cs", 3, 0),
+    ("h", 0, 1), ("g", 0, 0), ("d", 4, 3), ("sum", 2, 0), ("x", 4, 2), ("g", 0, 1), ("x", 4, 3),
+    ("d", 3, 3), ("h", 3, 0), ("h", 3, 1), ("g", 3, 0), ("g", 3, 1), ("yt", 2, 1),
+    ("sum", 3, 0), ("cs", 3, 1), ("h", 2, 0), ("h", 2, 1), ("g", 2, 0), ("g", 2, 1),
+    ("sum", 3, 1), ("close", 0), ("close", 1), ("cs", 2, 1), ("ba", 0), ("sum", 2, 1),
+    ("yt", 2, 2), ("yt", 2, 3), ("hb",), ("ba", 1), ("bg", 0), ("bg", 1), ("yt", 3, 1),
+    ("xe", 3, 1), ("yt", 3, 2), ("yt", 3, 3), ("mg", 0), ("bk", 0), ("yt", 2, 0), ("gout",),
+    ("unpack", 0), ("xe", 3, 2), ("cs", 0, 1), ("unsk",), ("by",), ("cs", 0, 0), ("sum", 0, 0),
+    ("bk", 1), ("yx", 2, 1), ("mg", 1), ("mg", 2), ("unpack", 1), ("cs", 1, 0), ("xe", 3, 3),
+    ("xe", 3, 0), ("sum", 0, 1), ("xe", 2, 1), ("yx", 3, 1), ("yx", 3, 2), ("yx", 2, 2),
+    ("yx", 2, 3), ("yx", 2, 0), ("cs", 1, 1), ("bt",), ("sum", 1, 1), ("yx", 0, 1),
+    ("yx", 3, 3), ("yt", 0, 1), ("sum", 1, 0), ("xe", 2, 2), ("bi", 0), ("bi", 1), ("ss", 0),
+    ("sw", 0), ("xe", 2, 3), ("yx", 3, 0), ("yx", 0, 2), ("yx", 0, 3), ("ss", 1), ("yx", 1, 1),
+    ("yx", 1, 2), ("yx", 1, 3), ("yx", 0, 0), ("xe", 0, 1), ("yt", 0, 2), ("yt", 0, 3),
+    ("yt", 0, 0), ("xe", 0, 2), ("yt", 3, 0), ("yt", 1, 1), ("xe", 1, 1), ("sw", 1),
+    ("yt", 1, 2), ("yt", 1, 3), ("xe", 1, 2), ("xe", 2, 0), ("xe", 1, 3), ("xe", 1, 0),
+    ("xe", 0, 3), ("ss", 2), ("sw", 2), ("ss", 3), ("bc",), ("yx", 1, 0), ("yt", 1, 0),
+    ("zt", 1), ("xe", 0, 0), ("hopw",), ("zt", 2), ("zt", 0), ("zt", 3), ("se",),
+)
 
 
 def dot_nn(a, b):
@@ -52,10 +91,17 @@
         copy.start()
         self.started.setdefault(tag, []).append(copy)
 
+    def go_if(self, when, copy, tag=None):
+        pl.when(when)(copy.start)
+        self.started.setdefault(tag, []).append((when, copy))
+
     def drain(self, *tags):
         for tag in tags or list(self.started):
             for copy in self.started.pop(tag, []):
-                copy.wait_send()
+                if isinstance(copy, tuple):
+                    pl.when(copy[0])(copy[1].wait_send)
+                else:
+                    copy.wait_send()
 
 
 def block_kernel(
@@ -148,15 +194,15 @@
 
     half = 2 * chan
     gather_pieces = [
-        (mix_w, 0, half, True),
-        (mix_w, half, half, False),
-        (None, 0, 0, True),
-        (up_w, 0, up_w.shape[2], True),
-        (down_w, 0, down_w.shape[2], False),
+        (mix_w, 0, half),
+        (mix_w, half, half),
+        (None, 0, 0),
+        (up_w, 0, up_w.shape[2]),
+        (down_w, 0, down_w.shape[2]),
     ]
 
     def place(piece, zs, ys, xs, cs):
-        buf, start, size, _ = gather_pieces[piece]
+        buf, start, size = gather_pieces[piece]
         if buf is None:
             return band_rows.at[(zs * YN + ys) * 4 + xs * 2 + cs]
         at = pl.multiple_of((zs * YN + ys) * rows, 32)
@@ -175,70 +221,99 @@
 
     own = (z, y, x, c)
 
-    def behind(k):
-        return (z + ZN - k) % ZN
-
-    def spot(kind, k):
-        return (behind(k), y if kind in (0, 2) else 1 - y, x if kind in (0, 1) else 1 - x, c)
-
-    def forward(piece, kind, k, peer, slot):
-        tag = "mix" if piece < 3 else ("near" if kind < 2 else "far")
-        out.go(ag(piece, spot(kind, k), peer, slot), tag)
-
-    def to_core(piece, kind, k):
-        forward(piece, kind, k, core_peer, 15 + kind * 4 + k)
+    def along(i):
+        edge = jnp.where(z == 0, i, ZN - 1 - i)
+        inside = jnp.where(z == 1, (1, 0, 2, 3)[i], (2, 1, 3, 0)[i])
+        return jnp.where((z == 0) | (z == ZN - 1), edge, inside)
+
+    order = [along(i) for i in range(ZN)]
+
+    def spot(kind, zs):
+        return (zs, y if kind in (0, 2) else 1 - y, x if kind in (0, 1) else 1 - x, c)
+
+    def tag_of(piece, kind):
+        return "mix" if piece < 3 else ("near" if kind < 2 else "far")
+
+    def forward(piece, kind, zs, peer, slot):
+        out.go(ag(piece, spot(kind, zs), peer, slot), tag_of(piece, kind))
+
+    def to_core(piece, kind, i):
+        forward(piece, kind, order[i], core_peer, 16 + kind * 4 + order[i])
 
     def arrived(piece, slot):
         ag(piece, own, core_peer, slot).wait_recv()
 
     def turns_y(piece):
-        return gather_pieces[piece][3]
+        return ROUTES[piece][0]
+
+    def pass_z(piece, kind, zs, step, when):
+        peer = device(jnp.clip(z + step, 0, ZN - 1), y, x, c)
+        copy = ag(piece, spot(kind, zs), peer, kind * 4 + zs)
+        out.go_if(when, copy, tag_of(piece, kind))
+
+    def start_line(piece, kind):
+        pass_z(piece, kind, z, 1, z < ZN - 1)
+        pass_z(piece, kind, z, -1, z > 0)
+
+    def pass_line(piece, kind, zs):
+        up = zs < z
+        pass_z(piece, kind, zs, jnp.where(up, 1, -1), jnp.where(up, z < ZN - 1, z > 0))
 
     def start_z(piece):
-        for k in (1, 3, 2):
-            forward(piece, 0, 0, z_peers[k - 1], k - 1)
-
-    def start_side(piece):
-        forward(piece, 0, 0, y_peer, 3)
-        forward(piece, 0, 0, x_peer, 7)
+        start_line(piece, 0)
+
+    def start_y(piece):
+        forward(piece, 0, z, y_peer, 4 + z)
+
+    def start_x(piece):
+        forward(piece, 0, z, x_peer, 8 + z)
+
+    def start_core(piece):
         to_core(piece, 0, 0)
 
-    def gather_z(piece, k):
-        arrived(piece, k - 1)
-        forward(piece, 0, k, y_peer, 3 + k)
-        forward(piece, 0, k, x_peer, 7 + k)
-        to_core(piece, 0, k)
-
-    def gather_turn(piece, k):
-        if turns_y(piece):
-            arrived(piece, 3 + k)
-            forward(piece, 1, k, x_peer, 11 + k)
-            to_core(piece, 1, k)
-        else:
-            arrived(piece, 7 + k)
-            forward(piece, 2, k, y_peer, 11 + k)
-            to_core(piece, 2, k)
-
-    def gather_side(piece, k):
-        if turns_y(piece):
-            arrived(piece, 7 + k)
-            to_core(piece, 2, k)
-        else:
-            arrived(piece, 3 + k)
-            to_core(piece, 1, k)
-
-    def gather_last(piece, k):
-        arrived(piece, 11 + k)
-        to_core(piece, 3, k)
+    def gather_z(piece, i):
+        zs = order[i]
+        arrived(piece, zs)
+        pass_line(piece, 0, zs)
+        forward(piece, 0, zs, y_peer, 4 + zs)
+        forward(piece, 0, zs, x_peer, 8 + zs)
+        to_core(piece, 0, i)
+
+    def turns(piece, i):
+        return not ROUTES[piece][1] or i == 0
+
+    def gather_y(piece, i):
+        zs = order[i]
+        arrived(piece, 4 + zs)
+        if turns_y(piece) and turns(piece, i):
+            forward(piece, 1, zs, x_peer, 12 + zs)
+        to_core(piece, 1, i)
+
+    def gather_x(piece, i):
+        zs = order[i]
+        arrived(piece, 8 + zs)
+        if not turns_y(piece) and turns(piece, i):
+            forward(piece, 2, zs, y_peer, 12 + zs)
+        to_core(piece, 2, i)
+
+    def gather_last(piece, i):
+        zs = order[i]
+        arrived(piece, 12 + zs)
+        if ROUTES[piece][1]:
+            if i:
+                pass_line(piece, 3, zs)
+            else:
+                start_line(piece, 3)
+        to_core(piece, 3, i)
 
     def gather_core(piece, kinds=(0, 1, 2, 3)):
         for kind in kinds:
-            for k in range(ZN):
-                arrived(piece, 15 + kind * 4 + k)
+            for i in range(ZN):
+                arrived(piece, 16 + kind * 4 + order[i])
 
     home = pl.ds(pl.multiple_of(group * rows, 32), rows)
     mix_w[mp, home, :] = jnp.concatenate(
-        [wq_ref[0], wq_ref[1], wq_ref[2], wo_ref[...].T], axis=1
+        [wq_ref[0], wo_ref[...].T, wq_ref[1], wq_ref[2]], axis=1
     ).astype(BF)
     flip = (
         lax.broadcasted_iota(jnp.int32, (window, window), 0)
@@ -311,9 +386,9 @@
 
     def repack(at):
         part = pl.ds(at, rows)
-        for kind in range(4):
+        for kind, at in ((0, 0), (3, 1), (1, 2), (2, 3)):
             full_w[kind, part] = jnp.concatenate(
-                [mix_w[m, part, kind * chan : (kind + 1) * chan] for m in range(4)], axis=1
+                [mix_w[m, part, at * chan : (at + 1) * chan] for m in range(4)], axis=1
             )
 
     def project_halo(at):
@@ -364,11 +439,14 @@
             part = pl.ds(at, CHUNK)
             p = dot_nn(normed_two[part], up_w[m])
             da = dot_nn(cot_low[part], down_w[m])
-            t = jnp.tanh(GELU_C * (p + GELU_A * (p * p * p)))
-            low = (0.5 * p * (1.0 + t)).astype(BF)
-            slope = 0.5 * (1.0 + t) + 0.5 * p * (1.0 - t * t) * (
-                GELU_C * (1.0 + 3.0 * GELU_A * (p * p))
+            square = p * p
+            t = jnp.tanh(p * (GELU_C + GELU_C * GELU_A * square))
+            gate = 0.5 + 0.5 * t
+            value = p * gate
+            slope = gate + value * (1.0 - gate) * (
+                2.0 * GELU_C + 6.0 * GELU_C * GELU_A * square
             )
+            low = value.astype(BF)
             dlow = (da * slope).astype(BF)
             act[part] = low
             dpre[part] = dlow
@@ -476,7 +554,7 @@
         result = wide_rows.at[pl.ds(kind * GROUPS * rows, GROUPS * rows)]
         weight_grad(result, normed.at[pl.ds(window, tokens)], grad)
 
-    def unpack(kinds):
+    def unpack(kinds, first):
         def body(at):
             part = pl.ds(at, rows)
             for m in range(4):
@@ -487,16 +565,16 @@
                     else wide_rows[pl.ds(at + kind * GROUPS * rows, rows), mine].astype(BF)
                     for kind in kinds
                 ]
-                span = slice(kinds[0] * chan, (kinds[-1] + 1) * chan)
+                span = slice(first * chan, (first + 2) * chan)
                 mix_w[m, part, span] = jnp.concatenate(pair, axis=1)
 
         return body
 
     scatter_pieces = [
-        (mix_w, 0, half, True, None, 0),
-        (mix_w, half, half, False, None, half),
-        (up_w, 0, up_w.shape[2], False, gu_ref, 2 * half),
-        (down_w, 0, down_w.shape[2], False, gd_ref, 2 * half + up_w.shape[2]),
+        (mix_w, 0, half, None, 0),
+        (mix_w, half, half, None, half),
+        (up_w, 0, up_w.shape[2], gu_ref, 2 * half),
+        (down_w, 0, down_w.shape[2], gd_ref, 2 * half + up_w.shape[2]),
     ]
 
     def rs(piece, src, dst, peer, slot):
@@ -518,12 +596,17 @@
         return buf.at[xs * 2 + c, pl.ds(at, rows), pl.ds(start, size)]
 
     def lanes(piece):
-        return pl.ds(scatter_pieces[piece][5], scatter_pieces[piece][2])
+        return pl.ds(scatter_pieces[piece][4], scatter_pieces[piece][2])
+
+    def core_landing(p, far):
+        if p < 2:
+            return recv_core.at[0, :, pl.ds((far * 2 + p) * half, half)]
+        return recv_core.at[far, :, pl.ds((p - 2) * up_w.shape[2], up_w.shape[2])]
 
     def core_copy(p, far):
         buf, start, size = scatter_pieces[p][:3]
         src = buf.at[x_of(far) * 2 + 1 - c, :, pl.ds(start, size)]
-        return rs(p, src, recv_core.at[far, :, lanes(p)], core_peer, far)
+        return rs(p, src, core_landing(p, far), core_peer, far)
 
     def core_send(p, far):
         out.go(core_copy(p, far))
@@ -531,20 +614,55 @@
     def core_sum(p, far):
         buf, start, size = scatter_pieces[p][:3]
         core_copy(p, far).wait_recv()
+        landed = core_landing(p, far)
 
         def body(at):
             part = pl.ds(at, rows)
-            buf[x_of(far) * 2 + c, part, pl.ds(start, size)] += recv_core[far, part, lanes(p)]
+            buf[x_of(far) * 2 + c, part, pl.ds(start, size)] += landed[part]
 
         loop_rows(GROUPS * rows, rows, body)
+
+    def behind(k):
+        return (z + ZN - k) % ZN
 
     def y_copy(p, far, k):
         src = block(p, x_of(far), behind(k), 1 - y)
         return rs(p, src, recv_one.at[far * ZN + k, :, lanes(p)], y_peer, 2 + far * ZN + k)
 
+    def line_copy(p, k):
+        src = block(p, 1 - x, behind(k), 1 - y)
+        landing = recv_one.at[ZN + k, :, lanes(p)]
+        return rs(p, src, landing, z_peers[ZN - 1 - k], 2 + ZN + k)
+
+    def cross_copy(p):
+        src = block(p, 1 - x, z, 1 - y)
+        return rs(p, src, recv_one.at[ZN, :, lanes(p)], x_peer, 2 + ZN)
+
     def y_send(p, far):
-        for k in (1, 2, 3, 0):
-            out.go(y_copy(p, far, k))
+        if not LINE_SUMS[p]:
+            for k in (1, 2, 3, 0):
+                out.go(y_copy(p, far, k))
+        elif far:
+            for k in (1, 2, 3):
+                out.go(line_copy(p, k))
+            for k in (1, 2, 3, 0):
+                out.go(x_copy(p, k))
+        else:
+            for k in (1, 2, 3):
+                out.go(y_copy(p, far, k))
+
+    def line_take(p, k):
+        if k:
+            line_copy(p, k).wait_recv()
+            spot_ref = block(p, 1 - x, z, 1 - y)
+            spot_ref[...] += recv_one[ZN + k, :, lanes(p)]
+            if k == 3:
+                out.go(cross_copy(p))
+        else:
+            cross_copy(p).wait_recv()
+            spot_ref = block(p, x, z, 1 - y)
+            spot_ref[...] += recv_one[ZN, :, lanes(p)]
+            out.go(y_copy(p, 0, 0))
 
     def y_take(p, far, k):
         y_copy(p, far, k).wait_recv()
@@ -571,56 +689,24 @@
             total = total + recv_z[k - 1, :, lanes(p)].astype(F32)
         if p == 0:
             gq_ref[0] = total[:, :chan]
-            gq_ref[1] = total[:, chan:]
+            go_ref[...] = total[:, chan:].T
         elif p == 1:
-            gq_ref[2] = total[:, :chan]
-            go_ref[...] = total[:, chan:].T
+            gq_ref[1] = total[:, :chan]
+            gq_ref[2] = total[:, chan:]
         else:
-            scatter_pieces[p][4][...] = total
+            scatter_pieces[p][3][...] = total
 
     def y_turn(p, k):
-        y_take(p, 1, k)
-        out.go(x_copy(p, k))
+        if LINE_SUMS[p]:
+            line_take(p, k)
+        else:
+            y_take(p, 1, k)
+            out.go(x_copy(p, k))
 
     def x_end(p, k):
         x_take(p, k)
         if k:
             out.go(z_copy(p, k))
-
-    def wide_copy(p, k, ys):
-        src = block(p, 1 - x, behind(k), ys)
-        slot = k if ys is y else ZN + k
-        return rs(p, src, recv_one.at[slot, :, lanes(p)], x_peer, 2 + slot)
-
-    def wide_send(p):
-        for k in (1, 2, 3, 0):
-            out.go(wide_copy(p, k, other_y))
-        for k in (1, 2, 3, 0):
-            out.go(wide_copy(p, k, y))
-
-    def wide_take(p, k, ys):
-        wide_copy(p, k, ys).wait_recv()
-        slot = k if ys is y else ZN + k
-        spot_ref = block(p, x, behind(k), ys)
-        spot_ref[...] += recv_one[slot, :, lanes(p)]
-
-    def late_copy(p, k):
-        src = block(p, x, behind(k), 1 - y)
-        return rs(p, src, recv_two.at[k, :, lanes(p)], y_peer, 10 + k)
-
-    def wide_turn(p, k):
-        wide_take(p, k, other_y)
-        out.go(late_copy(p, k))
-
-    def late_end(p, k):
-        wide_take(p, k, y)
-        late_copy(p, k).wait_recv()
-        spot_ref = block(p, x, behind(k), y)
-        spot_ref[...] += recv_two[k, :, lanes(p)]
-        if k:
-            out.go(z_copy(p, k))
-
-    other_y = 1 - y
 
     def bias_copy(src, dst, peer, slot):
         return pltpu.make_async_remote_copy(
@@ -704,202 +790,155 @@
             total = total + stats_recv[2 + k]
         stat_ref[...] = total
 
-    steps = (0, 1, 3, 2)
-    early, late = (0, 1, 2), (3, 4)
-
-    @pl.when(mp < 3)
-    def _():
-        halo_copy.start()
-
+    backs = [halo_back(1, dnum), halo_back(2, dden)]
+
+    def halo_start():
+        pl.when(mp < 3)(halo_copy.start)
+
+    def repack_all():
+        for p in (0, 1):
+            gather_core(p)
+        loop_rows(GROUPS * rows, rows, repack)
+
+    def halo_work():
+        pl.when(mp > 0)(halo_copy.wait_recv)
+
+        @pl.when(mp == 0)
+        def _():
+            x_halo[...] = jnp.zeros_like(x_halo)
+
+        norm_halo(0)
+        project_halo(0)
+
+    def bands_work():
+        gather_core(2)
+        build_bands()
+
+    def slab(r):
+        return x_of(r // 2) * 2 + (1 - c if r % 2 else c)
+
+    def hidden(r, part):
+        if r % 2 and part == 0:
+            for p in (3, 4):
+                gather_core(p, (r - 1, r))
+        hidden_rows(slab(r), r == 1)(part * CHUNK)
+
+    def hidden_grad(r, part):
+        if part == 0:
+            if r % 2 == 0:
+                out.drain("far" if r else "near")
+            weight_grad(up_w.at[slab(r)], normed_two, dpre)
+        else:
+            weight_grad(down_w.at[slab(r)], cot_low, act)
+
+    def back_start():
+        @pl.when(mp > 0)
+        def _():
+            for item in backs:
+                item.start()
+
+    def unpack_pair(part):
+        out.drain("mix")
+        loop_rows(GROUPS * rows, rows, unpack(((0, 3), (1, 2))[part], 2 * part))
+
+    def keys_back(j):
+        if j:
+
+            @pl.when(mp < 3)
+            def _():
+                for item in backs:
+                    item.wait_recv()
+
+            @pl.when(mp == 3)
+            def _():
+                dnum[pl.ds(tokens, window)] = jnp.zeros((window, width), BF)
+                dden[pl.ds(tokens, window)] = jnp.zeros((window, width), BF)
+
+        back_keys(j)
+
+    def sum_send(p, far):
+        core_sum(p, far)
+        y_send(p, far)
+
+    def unskew_all():
+        for j in range(GROUPS):
+            unskew(j)
+
+    def bias_start():
+        for k in (1, 2, 3, 0):
+            out.go(bias_y(k))
+
+    def bias_close():
+        close_bias()
+        if last_hop:
+
+            @pl.when(moves)
+            def _():
+                hop_copy().start()
+
+    def bias_end():
+        if last_hop:
+
+            @pl.when(moves)
+            def _():
+                hop_copy().wait_recv()
+                gb_ref[...] = bias_hop[1]
+
+            @pl.when(jnp.logical_not(moves))
+            def _():
+                gb_ref[...] = bias_hop[0]
+
+        else:
+            gb_ref[...] = bias_hop[0]
+
+    actions = {
+        "send_z": start_z,
+        "send_y": start_y,
+        "send_x": start_x,
+        "send_c": start_core,
+        "z": gather_z,
+        "y": gather_y,
+        "x": gather_x,
+        "d": gather_last,
+        "halo": halo_start,
+        "norm": lambda: loop_rows(tokens, CHUNK, norm_own),
+        "repack": repack_all,
+        "proj": lambda q: project_own(q * CHUNK),
+        "halow": halo_work,
+        "bands": bands_work,
+        "mix": mix_rows,
+        "att": lambda q: attend(q * CHUNK),
+        "h": hidden,
+        "g": hidden_grad,
+        "close": lambda q: close_hidden(q * CHUNK),
+        "ba": lambda q: back_attend(q * CHUNK),
+        "hb": back_start,
+        "gout": lambda: weight_grad(full_w.at[3], act, mixed),
+        "mg": mix_grad,
+        "unpack": unpack_pair,
+        "bk": keys_back,
+        "bg": band_grad,
+        "unsk": unskew_all,
+        "bi": lambda q: back_input(q * CHUNK),
+        "cs": core_send,
+        "sum": sum_send,
+        "yt": lambda p, k: y_take(p, 0, k),
+        "yx": y_turn,
+        "xe": x_end,
+        "zt": z_take,
+        "by": bias_start,
+        "bt": bias_turn,
+        "bc": bias_close,
+        "hopw": bias_end,
+        "ss": stats_send,
+        "sw": stats_step,
+        "se": stats_end,
+    }
     band_rows[4 * GROUPS : 4 * GROUPS + 4] = jnp.zeros((4, *bias_ref.shape), BF)
-    for p in early:
-        start_z(p)
-    for p in early:
-        start_side(p)
     up_w[mp, home, :] = wu_ref[...].astype(BF)
     down_w[mp, home, :] = wd_ref[...].astype(BF)
-    loop_rows(tokens, CHUNK, norm_own)
-    for k in steps[1:]:
-        for p in early:
-            gather_z(p, k)
-    for p in late:
-        start_z(p)
-    for step in (gather_turn, gather_side):
-        for k in steps:
-            for p in early:
-                step(p, k)
-    for p in late:
-        start_side(p)
-    for k in steps:
-        for p in early:
-            gather_last(p, k)
-
-    @pl.when(mp > 0)
-    def _():
-        halo_copy.wait_recv()
-
-    @pl.when(mp == 0)
-    def _():
-        x_halo[...] = jnp.zeros_like(x_halo)
-
-    loop_rows(window, CHUNK, norm_halo)
-    for k in steps[1:]:
-        for p in late:
-            gather_z(p, k)
-    for p in early:
-        gather_core(p)
-    tasks = [
-        functools.partial(step, p, k)
-        for step in (gather_turn, gather_side, gather_last)
-        for k in steps
-        for p in late
-    ]
-
-    def beside(count):
-        for _ in range(min(count, len(tasks))):
-            tasks.pop(0)()
-
-    loop_rows(GROUPS * rows, rows, repack)
-    build_bands()
-    for at in range(0, window, CHUNK):
-        project_halo(at)
-        beside(1)
-    for at in range(0, tokens, CHUNK):
-        project_own(at)
-        beside(1)
-    for i in range(2):
-        mix_rows(i)
-        beside(2)
-    for at in range(0, tokens, CHUNK):
-        attend(at)
-        beside(2)
-
-    def slab(r):
-        return x_of(r // 2) * 2 + (1 - c if r % 2 else c)
-
-    beside(len(tasks) - 2 * ZN)
-    for r in (1, 0, 3, 2):
-        if r % 2:
-            if r == 3:
-                beside(len(tasks))
-            for p in late:
-                gather_core(p, (r - 1, r))
-        loop_rows(tokens, CHUNK, hidden_rows(slab(r), r == 1))
-        beside(2)
-        if r % 2 == 0:
-            out.drain("far" if r else "near")
-        weight_grad(up_w.at[slab(r)], normed_two, dpre)
-        if r % 2:
-            core_send(2, r // 2)
-        else:
-            core_sum(2, r // 2)
-            y_send(2, r // 2)
-        beside(2)
-        weight_grad(down_w.at[slab(r)], cot_low, act)
-        if r % 2:
-            core_send(3, r // 2)
-        else:
-            core_sum(3, r // 2)
-            y_send(3, r // 2)
-    for k in steps:
-        y_take(2, 0, k)
-        y_take(3, 0, k)
-    loop_rows(tokens, CHUNK, close_hidden)
-    loop_rows(tokens, CHUNK, back_attend)
-
-    backs = [halo_back(1, dnum), halo_back(2, dden)]
-
-    @pl.when(mp > 0)
-    def _():
-        for item in backs:
-            item.start()
-
-    weight_grad(full_w.at[3], act, mixed)
-    mix_grad(0)
-    for k in (1, 2, 3, 0):
-        y_turn(2, k)
-    for i in range(2):
-        band_grad(i)
-    for j in range(GROUPS):
-        unskew(j)
-    for k in (1, 2, 3, 0):
-        out.go(bias_y(k))
-
-    @pl.when(mp < 3)
-    def _():
-        for item in backs:
-            item.wait_recv()
-
-    @pl.when(mp == 3)
-    def _():
-        dnum[pl.ds(tokens, window)] = jnp.zeros((window, width), BF)
-        dden[pl.ds(tokens, window)] = jnp.zeros((window, width), BF)
-
-    for j in range(2):
-        back_keys(j)
-    mix_grad(1)
-    out.drain("mix")
-    loop_rows(GROUPS * rows, rows, unpack((0, 1)))
-    core_send(0, 1)
-    core_send(0, 0)
-    mix_grad(2)
-    loop_rows(GROUPS * rows, rows, unpack((2, 3)))
-    core_send(1, 1)
-    core_send(1, 0)
-    for k in (1, 2, 3, 0):
-        y_turn(3, k)
-    core_sum(0, 1)
-    wide_send(0)
-    core_sum(1, 1)
-    y_send(1, 1)
-    core_sum(1, 0)
-    y_send(1, 0)
-    core_sum(0, 0)
-    bias_turn()
-    for at, k in zip(range(0, tokens, CHUNK), (1, 2, 3, 0), strict=True):
-        back_input(at)
-        x_end(2, k)
-    stats_send(0)
-    close_bias()
-    if last_hop:
-
-        @pl.when(moves)
-        def _():
-            hop_copy().start()
-
-    for k in (1, 2, 3, 0):
-        x_end(3, k)
-    stats_step(0)
-    stats_send(1)
-    for k in (1, 2, 3, 0):
-        wide_turn(0, k)
-        y_turn(1, k)
-    stats_step(1)
-    stats_send(2)
-    z_take(2)
-    for k in (1, 2, 3, 0):
-        y_take(1, 0, k)
-        late_end(0, k)
-        x_end(1, k)
-    stats_step(2)
-    stats_send(3)
-    z_take(3)
-    if last_hop:
-
-        @pl.when(moves)
-        def _():
-            hop_copy().wait_recv()
-            gb_ref[...] = bias_hop[1]
-
-        @pl.when(jnp.logical_not(moves))
-        def _():
-            gb_ref[...] = bias_hop[0]
-
-    else:
-        gb_ref[...] = bias_hop[0]
-    stats_end()
-    z_take(0)
-    z_take(1)
+    for name, *args in SCHEDULE:
+        actions[name](*args)
 
     @pl.when(mp < 3)
     def _():
@@ -980,12 +1019,12 @@
             buf(2, *bias.shape),
             buf(4, 8, width),
             buf(6, 8, width),
-            low(2, full, lanes),
+            low(2, full, 2 * hidden),
             low(GROUPS, rows, lanes),
             low(ZN, rows, lanes),
             low(ZN - 1, rows, lanes),
-            dma((5, 31)),
-            dma((5, 31)),
+            dma((5, 32)),
+            dma((5, 32)),
             dma((4, 17)),
             dma((4, 17)),
             dma((3,)),
@@ -1015,7 +1054,8 @@
     rms_ref = refs[24]
     one = 1.0 / (1.0 - BETA_ONE**ADAM_STEP)
     two = 1.0 / (1.0 - BETA_TWO**ADAM_STEP)
-    for i in range(6):
+
+    def step(i):
         if i == 4:
             grad = grads[4][...] * jnp.exp(params[4][...])
         elif i == 5:
@@ -1025,25 +1065,47 @@
         grad = grad * scale
         first = BETA_ONE * firsts[i][...] + (1.0 - BETA_ONE) * grad
         second = BETA_TWO * seconds[i][...] + (1.0 - BETA_TWO) * (grad * grad)
-        step = (first * one) / (jnp.sqrt(second * two) + ADAM_EPS)
+        change = (first * one) / (jnp.sqrt(second * two) + ADAM_EPS)
         if i < 4:
-            step = step + WEIGHT_DECAY * params[i][...]
+            change = change + WEIGHT_DECAY * params[i][...]
         out_grads[i][...] = grad
         out_firsts[i][...] = first
         out_seconds[i][...] = second
-        out_updates[i][...] = -LEARN_RATE * step
-    sums = jnp.sum(grads[5][...], axis=1, keepdims=True)
-    rms_ref[...] = jnp.sqrt(sums[2:5] / sums[5:6])
+        out_updates[i][...] = -LEARN_RATE * change
+
+    for i in range(4):
+        step(i)
+
+    @pl.when(pl.program_id(0) == 0)
+    def _():
+        for i in (4, 5):
+            step(i)
+        sums = jnp.sum(grads[5][...], axis=1, keepdims=True)
+        rms = jnp.sqrt(sums[2:5] / sums[5:6])
+        for i in range(3):
+            rms_ref[i] = jnp.sum(rms[i : i + 1, :])
 
 
 def run_adam(scale, grads, params, firsts, seconds):
-    vmem = pl.BlockSpec(memory_space=pltpu.VMEM)
     kinds = [jax.ShapeDtypeStruct(param.shape, F32) for param in params]
+    parts = 1
+
+    def cut(item):
+        block = (item.shape[0] // parts, *item.shape[1:])
+        return pl.BlockSpec(block, lambda i: (i, *[0] * (len(item.shape) - 1)))
+
+    def whole(item):
+        return pl.BlockSpec(item.shape, lambda i: (0,) * len(item.shape))
+
+    def specs(items):
+        return [cut(item) for item in items[:4]] + [whole(item) for item in items[4:]]
+
     return pl.pallas_call(
         functools.partial(adam_kernel, scale),
-        out_shape=(*(kinds * 4), jax.ShapeDtypeStruct((3, 1), F32)),
-        in_specs=[vmem] * 24,
-        out_specs=(vmem,) * 25,
+        grid=(parts,),
+        out_shape=(*(kinds * 4), jax.ShapeDtypeStruct((3,), F32)),
+        in_specs=specs(grads) + specs(params) * 3,
+        out_specs=(*specs(kinds) * 4, pl.BlockSpec(memory_space=pltpu.SMEM)),
         compiler_params=pltpu.CompilerParams(vmem_limit_bytes=62 * 1024 * 1024),
     )(*grads, *params, *firsts, *seconds)
 
@@ -1087,7 +1149,7 @@
     for i in range(4):
         qkv, mix, up, down, bias, gains = results[6 * i : 6 * i + 6]
         outs += [qkv.transpose(1, 0, 2), mix, up, down.T, bias, gains]
-    return (block_low[None], grad_input[None], *outs, rms_stats[:, 0])
+    return (block_low[None], grad_input[None], *outs, rms_stats)
 
 
 def solution(mesh):

time: 204 us -> 173 us (0.85)
  Pallas kernels: 197 us -> 165 us
    pallas_call x1, Pallas kernels: 192 us -> 160 us  [run_block(): pl.pallas_call(functools.partial(block_kernel, last_hop), out_shape=(shap...]
where the time goes in v3:
time: 173 us; the launch traced here: 169 us
  Pallas kernels  165 us (95%)
  local copies, waits for them, and re-layouts  2.82 us (2%)
    pallas_call x1, Pallas kernels, run_block(): pl.pallas_call(functools.partial(block_kernel, last_hop), out_shape=(shap...  160 us
    pallas_call x1, Pallas kernels, run_adam(): pl.pallas_call(functools.partial(adam_kernel, scale), grid=(parts,), out_...  5.37 us

profile of v3, /device:TPU:4, one launch (start us, length us, event | category | flops | bytes accessed | tf_op | source)
XLA Modules:
  0.0 169.3 jit_solution(4814989554952898417)
XLA Ops:
  1.3 159.5 %shard_map.412 = (bf16[512,768]{1,0:T(8,128)(2,1)}, f32[512,768]{1,0:T(8,128)}, f32[3,96,192]{2,1,0:T(8,128)}, f32[192,96]{1,0:T(8,128)}, f32[96,768]{1,0:T(8,12...) custom-call(s32[1]{0:T(128)S(6)} %copy.50.len_ref, bf16[512,768]{1,0:T(8,128)(2,1)} %bitcast.24, ...), custom_call_target="tpu_custom_call" | custom-call | tf_op jit(solution)/shard_map/pallas_call | solution.py:981
  160.9 0.0 copy-start.1
  160.9 5.4 %shard_map.413 = (f32[3,96,192]{2,1,0:T(8,128)}, f32[192,96]{1,0:T(8,128)}, f32[96,768]{1,0:T(8,128)}, f32[96,768]{1,0:T(8,128)}, f32[64,256]{1,0:T(8,128)}, /*i...) custom-call(f32[3,96,192]{2,1,0:T(8,128)} %get-tuple-element.62.refs, ...), custom_call_target="tpu_custom_call" | custom-call | tf_op jit(solution)/shard_map/pallas_call | solution.py:1103
  166.2 0.0 copy-start
  166.3 0.0 copy-done.1
  166.3 0.9 copy.51
  167.1 0.8 copy-done
  167.9 1.1 copy.52
Async XLA Ops:
  160.9 5.4 %copy-start.1 = (bf16[512,768]{1,0:T(8,128)(2,1)S(1)}, bf16[512,768]{1,0:T(8,128)(2,1)}, u32[]{:S(2)}) copy-start(bf16[512,768]{1,0:T(8,128)(2,1)} %get-tuple-element.60) | copy-start | bytes 2359300
  166.2 1.7 copy-start

commit v4 on v3

--- a/solution.py
+++ b/solution.py
@@ -26,42 +26,43 @@
 GELU_A = 0.044715
 
 
-ROUTES = ((True, False), (False, False), (True, True), (True, False), (False, True))
-LINE_SUMS = (False, True, False, True)
+ROUTES = ((True, False), (False, False), (False, False), (True, False), (False, True))
+LINE_SUMS = (False, False, True, False)
 SCHEDULE = (
-    ("send_x", 2), ("send_x", 0), ("send_z", 2), ("send_x", 1), ("send_y", 0), ("send_y", 1),
-    ("send_z", 1), ("send_z", 0), ("send_y", 2), ("y", 0, 0), ("z", 2, 1), ("z", 2, 2),
-    ("z", 1, 1), ("x", 1, 0), ("send_c", 1), ("z", 0, 1), ("y", 2, 0), ("norm",), ("z", 0, 2),
-    ("send_z", 3), ("send_x", 3), ("z", 0, 3), ("z", 2, 3), ("x", 2, 0), ("x", 2, 1),
-    ("z", 1, 2), ("x", 2, 2), ("y", 0, 1), ("send_y", 3), ("y", 0, 2), ("y", 0, 3), ("y", 1, 0),
-    ("d", 2, 0), ("send_y", 4), ("d", 2, 1), ("d", 1, 0), ("y", 2, 1), ("y", 2, 2), ("z", 1, 3),
-    ("z", 3, 1), ("z", 3, 2), ("x", 3, 0), ("send_c", 2), ("x", 0, 0), ("x", 0, 1), ("y", 1, 1),
-    ("x", 1, 1), ("x", 1, 2), ("d", 0, 0), ("d", 0, 1), ("y", 2, 3), ("send_x", 4), ("x", 1, 3),
-    ("halo",), ("z", 3, 3), ("d", 2, 2), ("d", 2, 3), ("send_z", 4), ("d", 1, 1), ("y", 1, 2),
-    ("y", 1, 3), ("x", 0, 2), ("x", 0, 3), ("send_c", 0), ("z", 4, 1), ("x", 2, 3), ("bands",),
-    ("d", 1, 2), ("d", 1, 3), ("y", 3, 0), ("y", 3, 1), ("send_c", 4), ("d", 0, 2), ("d", 0, 3),
-    ("x", 4, 0), ("send_c", 3), ("y", 3, 2), ("y", 3, 3), ("z", 4, 2), ("z", 4, 3), ("repack",),
-    ("y", 4, 0), ("d", 4, 0), ("proj", 0), ("proj", 1), ("y", 4, 1), ("y", 4, 2), ("halow",),
-    ("mix", 0), ("mix", 1), ("att", 0), ("att", 1), ("y", 4, 3), ("x", 4, 1), ("d", 3, 0),
-    ("x", 3, 1), ("x", 3, 2), ("x", 3, 3), ("h", 1, 0), ("d", 4, 1), ("h", 1, 1), ("g", 1, 0),
-    ("cs", 2, 0), ("d", 3, 1), ("d", 4, 2), ("g", 1, 1), ("h", 0, 0), ("d", 3, 2), ("cs", 3, 0),
-    ("h", 0, 1), ("g", 0, 0), ("d", 4, 3), ("sum", 2, 0), ("x", 4, 2), ("g", 0, 1), ("x", 4, 3),
-    ("d", 3, 3), ("h", 3, 0), ("h", 3, 1), ("g", 3, 0), ("g", 3, 1), ("yt", 2, 1),
-    ("sum", 3, 0), ("cs", 3, 1), ("h", 2, 0), ("h", 2, 1), ("g", 2, 0), ("g", 2, 1),
-    ("sum", 3, 1), ("close", 0), ("close", 1), ("cs", 2, 1), ("ba", 0), ("sum", 2, 1),
-    ("yt", 2, 2), ("yt", 2, 3), ("hb",), ("ba", 1), ("bg", 0), ("bg", 1), ("yt", 3, 1),
-    ("xe", 3, 1), ("yt", 3, 2), ("yt", 3, 3), ("mg", 0), ("bk", 0), ("yt", 2, 0), ("gout",),
-    ("unpack", 0), ("xe", 3, 2), ("cs", 0, 1), ("unsk",), ("by",), ("cs", 0, 0), ("sum", 0, 0),
-    ("bk", 1), ("yx", 2, 1), ("mg", 1), ("mg", 2), ("unpack", 1), ("cs", 1, 0), ("xe", 3, 3),
-    ("xe", 3, 0), ("sum", 0, 1), ("xe", 2, 1), ("yx", 3, 1), ("yx", 3, 2), ("yx", 2, 2),
-    ("yx", 2, 3), ("yx", 2, 0), ("cs", 1, 1), ("bt",), ("sum", 1, 1), ("yx", 0, 1),
-    ("yx", 3, 3), ("yt", 0, 1), ("sum", 1, 0), ("xe", 2, 2), ("bi", 0), ("bi", 1), ("ss", 0),
-    ("sw", 0), ("xe", 2, 3), ("yx", 3, 0), ("yx", 0, 2), ("yx", 0, 3), ("ss", 1), ("yx", 1, 1),
-    ("yx", 1, 2), ("yx", 1, 3), ("yx", 0, 0), ("xe", 0, 1), ("yt", 0, 2), ("yt", 0, 3),
-    ("yt", 0, 0), ("xe", 0, 2), ("yt", 3, 0), ("yt", 1, 1), ("xe", 1, 1), ("sw", 1),
-    ("yt", 1, 2), ("yt", 1, 3), ("xe", 1, 2), ("xe", 2, 0), ("xe", 1, 3), ("xe", 1, 0),
-    ("xe", 0, 3), ("ss", 2), ("sw", 2), ("ss", 3), ("bc",), ("yx", 1, 0), ("yt", 1, 0),
-    ("zt", 1), ("xe", 0, 0), ("hopw",), ("zt", 2), ("zt", 0), ("zt", 3), ("se",),
+    ("send_y", 1), ("send_x", 2), ("send_c", 3), ("send_c", 0), ("send_x", 0), ("send_x", 1),
+    ("send_c", 1), ("send_z", 0), ("send_y", 0), ("send_z", 1), ("norm",), ("x", 2, 0),
+    ("send_c", 2), ("y", 1, 0), ("send_z", 3), ("z", 0, 1), ("x", 0, 0), ("y", 0, 0),
+    ("x", 1, 0), ("z", 0, 2), ("y", 0, 1), ("x", 0, 1), ("z", 1, 1), ("send_z", 2), ("d", 1, 0),
+    ("d", 0, 0), ("z", 1, 2), ("z", 3, 1), ("z", 3, 2), ("x", 1, 1), ("y", 0, 2), ("z", 2, 1),
+    ("send_y", 2), ("z", 0, 3), ("z", 2, 2), ("x", 0, 2), ("z", 1, 3), ("z", 3, 3), ("y", 0, 3),
+    ("z", 2, 3), ("send_y", 3), ("halo",), ("d", 1, 1), ("y", 2, 0), ("y", 1, 1), ("y", 1, 2),
+    ("d", 0, 1), ("d", 0, 2), ("x", 2, 1), ("y", 1, 3), ("x", 1, 2), ("send_z", 4), ("d", 1, 2),
+    ("send_x", 3), ("x", 1, 3), ("z", 4, 1), ("y", 2, 1), ("y", 2, 2), ("z", 4, 2), ("y", 2, 3),
+    ("x", 2, 2), ("x", 2, 3), ("send_x", 4), ("d", 0, 3), ("d", 2, 0), ("d", 2, 1), ("x", 0, 3),
+    ("send_y", 4), ("x", 3, 0), ("y", 3, 0), ("y", 3, 1), ("z", 4, 3), ("send_c", 4),
+    ("d", 1, 3), ("y", 3, 2), ("y", 3, 3), ("x", 3, 1), ("repack",), ("proj", 0), ("proj", 1),
+    ("d", 2, 2), ("d", 2, 3), ("bands",), ("halow",), ("y", 4, 0), ("y", 4, 1), ("y", 4, 2),
+    ("x", 4, 0), ("x", 4, 1), ("mix", 0), ("mix", 1), ("y", 4, 3), ("x", 4, 2), ("att", 0),
+    ("att", 1), ("d", 4, 0), ("d", 3, 0), ("h", 1, 0), ("h", 1, 1), ("g", 1, 0), ("g", 1, 1),
+    ("cs", 2, 0), ("cs", 3, 0), ("d", 3, 1), ("h", 0, 0), ("h", 0, 1), ("d", 4, 1), ("g", 0, 0),
+    ("sum", 2, 0), ("g", 0, 1), ("d", 3, 2), ("x", 3, 2), ("x", 4, 3), ("x", 3, 3), ("d", 4, 2),
+    ("d", 4, 3), ("sum", 3, 0), ("d", 3, 3), ("h", 3, 0), ("h", 3, 1), ("g", 3, 0),
+    ("cs", 2, 1), ("g", 3, 1), ("cs", 3, 1), ("yt", 2, 1), ("yt", 2, 2), ("h", 2, 0),
+    ("h", 2, 1), ("g", 2, 0), ("sum", 2, 1), ("g", 2, 1), ("close", 0), ("close", 1),
+    ("sum", 3, 1), ("yt", 3, 1), ("yt", 3, 2), ("xe", 2, 1), ("ba", 0), ("ba", 1), ("bh",),
+    ("hb",), ("xe", 2, 2), ("bg", 0), ("bg", 1), ("unsk",), ("yt", 3, 3), ("yx", 3, 1),
+    ("mg", 0), ("gout",), ("unpack", 0), ("bk", 0), ("cs", 0, 1), ("by",), ("bk", 1), ("mg", 1),
+    ("bi", 0), ("yt", 3, 0), ("yt", 2, 3), ("cs", 0, 0), ("yx", 2, 1), ("yx", 2, 2),
+    ("xe", 2, 3), ("yx", 2, 3), ("sum", 0, 1), ("mg", 2), ("unpack", 1), ("cs", 1, 0),
+    ("bi", 1), ("ss", 0), ("sum", 0, 0), ("bt",), ("yx", 3, 2), ("yx", 3, 3), ("yx", 3, 0),
+    ("sw", 0), ("xe", 3, 1), ("xe", 3, 2), ("yx", 0, 1), ("yt", 0, 1), ("sum", 1, 0),
+    ("yt", 0, 2), ("cs", 1, 1), ("sum", 1, 1), ("yx", 2, 0), ("yx", 0, 2), ("xe", 3, 3),
+    ("xe", 3, 0), ("yx", 0, 3), ("xe", 0, 1), ("yt", 1, 1), ("yt", 0, 3), ("yx", 0, 0),
+    ("ss", 1), ("xe", 0, 2), ("xe", 0, 3), ("yt", 1, 2), ("yt", 1, 3), ("yx", 1, 1),
+    ("yt", 0, 0), ("sw", 1), ("ss", 2), ("yx", 1, 2), ("yx", 1, 3), ("xe", 1, 1), ("xe", 1, 2),
+    ("yx", 1, 0), ("xe", 1, 3), ("yt", 2, 0), ("xe", 0, 0), ("zt", 0), ("sw", 2), ("xe", 2, 0),
+    ("zt", 2), ("yt", 1, 0), ("ss", 3), ("zt", 3), ("xe", 1, 0), ("bc",), ("hopw",), ("zt", 1),
+    ("se",),
 )
 
 
@@ -143,6 +144,9 @@
     dn_two,
     dnum,
     dden,
+    dkey_halo,
+    dval_halo,
+    dnorm_recv,
     bias_part,
     bias_recv_y,
     bias_recv_z,
@@ -234,14 +238,27 @@
     def tag_of(piece, kind):
         return "mix" if piece < 3 else ("near" if kind < 2 else "far")
 
-    def forward(piece, kind, zs, peer, slot):
-        out.go(ag(piece, spot(kind, zs), peer, slot), tag_of(piece, kind))
+    def forward(piece, kind, zs, peer, slot, when=None):
+        copy = ag(piece, spot(kind, zs), peer, slot)
+        if piece == 2 and when is not None:
+            out.go_if(when, copy, tag_of(piece, kind))
+        else:
+            out.go(copy, tag_of(piece, kind))
+
+    def used_here(zs):
+        return zs // 2 == x
 
     def to_core(piece, kind, i):
-        forward(piece, kind, order[i], core_peer, 16 + kind * 4 + order[i])
-
-    def arrived(piece, slot):
-        ag(piece, own, core_peer, slot).wait_recv()
+        zs = order[i]
+        when = used_here(zs) & (zs % 2 != c)
+        forward(piece, kind, zs, core_peer, 16 + kind * 4 + zs, when)
+
+    def arrived(piece, slot, when=None):
+        wait = ag(piece, own, core_peer, slot).wait_recv
+        if piece == 2 and when is not None:
+            pl.when(when)(wait)
+        else:
+            wait()
 
     def turns_y(piece):
         return ROUTES[piece][0]
@@ -263,10 +280,10 @@
         start_line(piece, 0)
 
     def start_y(piece):
-        forward(piece, 0, z, y_peer, 4 + z)
+        forward(piece, 0, z, y_peer, 4 + z, used_here(z))
 
     def start_x(piece):
-        forward(piece, 0, z, x_peer, 8 + z)
+        forward(piece, 0, z, x_peer, 8 + z, jnp.logical_not(used_here(z)))
 
     def start_core(piece):
         to_core(piece, 0, 0)
@@ -275,8 +292,8 @@
         zs = order[i]
         arrived(piece, zs)
         pass_line(piece, 0, zs)
-        forward(piece, 0, zs, y_peer, 4 + zs)
-        forward(piece, 0, zs, x_peer, 8 + zs)
+        forward(piece, 0, zs, y_peer, 4 + zs, used_here(zs))
+        forward(piece, 0, zs, x_peer, 8 + zs, jnp.logical_not(used_here(zs)))
         to_core(piece, 0, i)
 
     def turns(piece, i):
@@ -284,21 +301,21 @@
 
     def gather_y(piece, i):
         zs = order[i]
-        arrived(piece, 4 + zs)
+        arrived(piece, 4 + zs, used_here(zs))
         if turns_y(piece) and turns(piece, i):
             forward(piece, 1, zs, x_peer, 12 + zs)
         to_core(piece, 1, i)
 
     def gather_x(piece, i):
         zs = order[i]
-        arrived(piece, 8 + zs)
+        arrived(piece, 8 + zs, used_here(zs))
         if not turns_y(piece) and turns(piece, i):
-            forward(piece, 2, zs, y_peer, 12 + zs)
+            forward(piece, 2, zs, y_peer, 12 + zs, used_here(zs))
         to_core(piece, 2, i)
 
     def gather_last(piece, i):
         zs = order[i]
-        arrived(piece, 12 + zs)
+        arrived(piece, 12 + zs, used_here(zs))
         if ROUTES[piece][1]:
             if i:
                 pass_line(piece, 3, zs)
@@ -309,7 +326,25 @@
     def gather_core(piece, kinds=(0, 1, 2, 3)):
         for kind in kinds:
             for i in range(ZN):
-                arrived(piece, 16 + kind * 4 + order[i])
+                zs = order[i]
+                arrived(piece, 16 + kind * 4 + zs, used_here(zs) & (zs % 2 == c))
+
+    barrier = pltpu.get_barrier_semaphore()
+    friends = [core_peer, x_peer, y_peer, diag_peer] + z_peers
+    for friend in friends:
+        pl.semaphore_signal(barrier, inc=1, device_id=friend, device_id_type=MESH)
+    here = group * 4 + mp
+    moves = here != mp * GROUPS + group
+    if last_hop:
+
+        @pl.when(moves)
+        def _():
+            pl.semaphore_signal(
+                barrier,
+                inc=1,
+                device_id=(here % GROUPS, inner, here // GROUPS),
+                device_id_type=MESH,
+            )
 
     home = pl.ds(pl.multiple_of(group * rows, 32), rows)
     mix_w[mp, home, :] = jnp.concatenate(
@@ -324,22 +359,13 @@
         jnp.exp(bias_ref[...]).astype(BF), flip.astype(BF)
     ).astype(BF)
 
-    barrier = pltpu.get_barrier_semaphore()
-    friends = [core_peer, x_peer, y_peer, diag_peer] + z_peers
-    for friend in friends:
-        pl.semaphore_signal(barrier, inc=1, device_id=friend, device_id_type=MESH)
-    here = group * 4 + mp
-    moves = here != mp * GROUPS + group
+    up_w[mp, home, :] = wu_ref[...].astype(BF)
+    down_w[mp, home, :] = wd_ref[...].astype(BF)
+    stats[0] = jnp.zeros(stats.shape[1:], F32)
     if last_hop:
 
         @pl.when(moves)
         def _():
-            pl.semaphore_signal(
-                barrier,
-                inc=1,
-                device_id=(here % GROUPS, inner, here // GROUPS),
-                device_id_type=MESH,
-            )
             pl.semaphore_wait(barrier, len(friends) + 1)
 
         @pl.when(jnp.logical_not(moves))
@@ -358,7 +384,6 @@
         device_id_type=MESH,
     )
 
-    stats[0] = jnp.zeros(stats.shape[1:], F32)
 
     def add_stat(row, value):
         stats[0, row : row + 1, :] += jnp.sum(value, axis=0, keepdims=True)
@@ -411,7 +436,7 @@
         sig[part] = jax.nn.sigmoid(dot_nn(a, full_w[0]))
 
     def build_bands():
-        for i in range(3):
+        for i in range(2):
             raw = band_rows[pl.ds(mp * 8 + i * 4, 4)].reshape(window, window).astype(F32)
             wide = jnp.concatenate([raw, jnp.zeros_like(raw)], axis=1)
             bands[i] = pltpu.roll(wide, 1, 1, stride=1, stride_axis=0).astype(BF)
@@ -461,10 +486,13 @@
 
         return body
 
-    def weight_grad(result, left, right):
+    def weight_grad(result, left, right, left_more=None, right_more=None):
         for at in range(0, result.shape[1], 256):
             part = slice(at, at + 256)
-            result[:, part] = dot_tn(left[...], right[:, part]).astype(result.dtype)
+            total = dot_tn(left[...], right[:, part])
+            if right_more is not None:
+                total = total + dot_tn(left_more[0:window], right_more[:, part])
+            result[:, part] = total.astype(result.dtype)
 
     def close_hidden(at):
         part = pl.ds(at, CHUNK)
@@ -496,12 +524,12 @@
         dnum[part] = dn.astype(BF)
         dden[part] = (-dn * rt).astype(BF)
 
-    def halo_back(slot, buf):
+    def halo_back():
         return pltpu.make_async_remote_copy(
-            src_ref=buf.at[pl.ds(0, window)],
-            dst_ref=buf.at[pl.ds(tokens, window)],
-            send_sem=halo_send.at[slot],
-            recv_sem=halo_recv.at[slot],
+            src_ref=x_halo,
+            dst_ref=dnorm_recv,
+            send_sem=halo_send.at[1],
+            recv_sem=halo_recv.at[1],
             device_id=(group, inner, (mp + 3) % 4),
             device_id_type=MESH,
         )
@@ -525,14 +553,32 @@
 
     def back_keys(j):
         here = slice(j * window, (j + 1) * window)
-        then = slice((j + 1) * window, (j + 2) * window)
         right = bands[j, :, window:]
-        left = bands[j + 1, :, :window]
-        dkv = dot_tn(right, dnum[here]) + dot_tn(left, dnum[then])
-        de = dot_tn(right, dden[here]) + dot_tn(left, dden[then])
+        dkv = dot_tn(right, dnum[here])
+        de = dot_tn(right, dden[here])
+        if j == 0:
+            then = slice(window, 2 * window)
+            left = bands[1, :, :window]
+            dkv = dkv + dot_tn(left, dnum[then])
+            de = de + dot_tn(left, dden[then])
         ek = expk[here]
         cot_low[here] = (dkv * ek).astype(BF)
         dpre[here] = ((de + dkv * val[here]) * ek).astype(BF)
+
+    def back_halo():
+        before = slice(0, window)
+        left = bands[0, :, :window]
+        dkv = dot_tn(left, dnum[before])
+        de = dot_tn(left, dden[before])
+        ek = exp_low[before].astype(F32)
+        dval_halo[...] = (dkv * ek).astype(BF)
+        dkey_halo[...] = (de * ek + dkv * kv_low[before].astype(F32)).astype(BF)
+
+    def halo_return():
+        x_halo[...] = (
+            dot_nt(dkey_halo[...], full_w[1]) + dot_nt(dval_halo[...], full_w[2])
+        ).astype(BF)
+        pl.when(mp > 0)(halo_back().start)
 
     def back_input(at):
         part = pl.ds(at, CHUNK)
@@ -541,6 +587,14 @@
             + dot_nt(dpre[part], full_w[1])
             + dot_nt(cot_low[part], full_w[2])
         )
+        if at:
+            pl.when(mp < 3)(halo_back().wait_recv)
+
+            @pl.when(mp == 3)
+            def _():
+                dnorm_recv[...] = jnp.zeros_like(dnorm_recv)
+
+            d = d + dnorm_recv[...].astype(F32)
         xf = x_ref[part].astype(F32)
         r = rms(xf)
         u = gains_ref[0:1] * d
@@ -552,7 +606,11 @@
     def mix_grad(kind):
         grad = (normed_two, dpre, cot_low)[kind]
         result = wide_rows.at[pl.ds(kind * GROUPS * rows, GROUPS * rows)]
-        weight_grad(result, normed.at[pl.ds(window, tokens)], grad)
+        left = normed.at[pl.ds(window, tokens)]
+        if kind == 0:
+            weight_grad(result, left, grad)
+        else:
+            weight_grad(result, left, grad, normed, (dkey_halo, dval_halo)[kind - 1])
 
     def unpack(kinds, first):
         def body(at):
@@ -790,8 +848,6 @@
             total = total + stats_recv[2 + k]
         stat_ref[...] = total
 
-    backs = [halo_back(1, dnum), halo_back(2, dden)]
-
     def halo_start():
         pl.when(mp < 3)(halo_copy.start)
 
@@ -831,30 +887,9 @@
         else:
             weight_grad(down_w.at[slab(r)], cot_low, act)
 
-    def back_start():
-        @pl.when(mp > 0)
-        def _():
-            for item in backs:
-                item.start()
-
     def unpack_pair(part):
         out.drain("mix")
         loop_rows(GROUPS * rows, rows, unpack(((0, 3), (1, 2))[part], 2 * part))
-
-    def keys_back(j):
-        if j:
-
-            @pl.when(mp < 3)
-            def _():
-                for item in backs:
-                    item.wait_recv()
-
-            @pl.when(mp == 3)
-            def _():
-                dnum[pl.ds(tokens, window)] = jnp.zeros((window, width), BF)
-                dden[pl.ds(tokens, window)] = jnp.zeros((window, width), BF)
-
-        back_keys(j)
 
     def sum_send(p, far):
         core_sum(p, far)
@@ -912,11 +947,12 @@
         "g": hidden_grad,
         "close": lambda q: close_hidden(q * CHUNK),
         "ba": lambda q: back_attend(q * CHUNK),
-        "hb": back_start,
+        "hb": halo_return,
+        "bh": back_halo,
         "gout": lambda: weight_grad(full_w.at[3], act, mixed),
         "mg": mix_grad,
         "unpack": unpack_pair,
-        "bk": keys_back,
+        "bk": back_keys,
         "bg": band_grad,
         "unsk": unskew_all,
         "bi": lambda q: back_input(q * CHUNK),
@@ -934,9 +970,6 @@
         "sw": stats_step,
         "se": stats_end,
     }
-    band_rows[4 * GROUPS : 4 * GROUPS + 4] = jnp.zeros((4, *bias_ref.shape), BF)
-    up_w[mp, home, :] = wu_ref[...].astype(BF)
-    down_w[mp, home, :] = wd_ref[...].astype(BF)
     for name, *args in SCHEDULE:
         actions[name](*args)
 
@@ -944,10 +977,7 @@
     def _():
         halo_copy.wait_send()
 
-    @pl.when(mp > 0)
-    def _():
-        for item in backs:
-            item.wait_send()
+    pl.when(mp > 0)(halo_back().wait_send)
 
     if last_hop:
 
@@ -996,7 +1026,7 @@
             low(4, full, mix_width),
             low(4, full, hidden),
             low(4, full, hidden),
-            low(4 * GROUPS + 4, *bias.shape),
+            low(4 * GROUPS, *bias.shape),
             low(window, width),
             low(4, full, width),
             low(window + tokens, width),
@@ -1004,15 +1034,18 @@
             buf(tokens, width),
             low(window + tokens, width),
             low(window + tokens, width),
-            low(3, window, 2 * window),
+            low(2, window, 2 * window),
             low(tokens, width),
             low(tokens, width),
             low(tokens, width),
             low(tokens, hidden),
             low(tokens, hidden),
             buf(tokens, width),
-            low(tokens + window, width),
-            low(tokens + window, width),
+            low(tokens, width),
+            low(tokens, width),
+            low(window, width),
+            low(window, width),
+            low(window, width),
             low(GROUPS, *bias.shape),
             low(ZN, *bias.shape),
             low(ZN - 1, *bias.shape),
@@ -1027,8 +1060,8 @@
             dma((5, 32)),
             dma((4, 17)),
             dma((4, 17)),
-            dma((3,)),
-            dma((3,)),
+            dma((2,)),
+            dma((2,)),
             dma((8,)),
             dma((8,)),
             dma((6,)),
@@ -1043,7 +1076,18 @@
 MESH = pl.DeviceIdType.MESH
 
 
-def adam_kernel(scale, *refs):
+def adam_kernel(scale, blk_ref, gin_ref, *refs):
+    *refs, blk_out, gin_out, blk_held, gin_held, copied = refs
+    taken = [
+        pltpu.make_async_copy(blk_ref, blk_held, copied.at[0]),
+        pltpu.make_async_copy(gin_ref, gin_held, copied.at[1]),
+    ]
+    given = [
+        pltpu.make_async_copy(blk_held, blk_out, copied.at[2]),
+        pltpu.make_async_copy(gin_held, gin_out, copied.at[3]),
+    ]
+    for item in taken:
+        item.start()
     grads, refs = refs[:6], refs[6:]
     params, refs = refs[:6], refs[6:]
     firsts, refs = refs[:6], refs[6:]
@@ -1073,41 +1117,38 @@
         out_seconds[i][...] = second
         out_updates[i][...] = -LEARN_RATE * change
 
-    for i in range(4):
+    for i in range(6):
+        if i == 2:
+            for item, onward in zip(taken, given, strict=True):
+                item.wait()
+                onward.start()
         step(i)
-
-    @pl.when(pl.program_id(0) == 0)
-    def _():
-        for i in (4, 5):
-            step(i)
-        sums = jnp.sum(grads[5][...], axis=1, keepdims=True)
-        rms = jnp.sqrt(sums[2:5] / sums[5:6])
-        for i in range(3):
-            rms_ref[i] = jnp.sum(rms[i : i + 1, :])
-
-
-def run_adam(scale, grads, params, firsts, seconds):
+    sums = jnp.sum(grads[5][...], axis=1, keepdims=True)
+    rms = jnp.sqrt(sums[2:5] / sums[5:6])
+    for i in range(3):
+        rms_ref[i] = jnp.sum(rms[i : i + 1, :])
+
+    for item in given:
+        item.wait()
+
+
+def run_adam(scale, blk, gin, grads, params, firsts, seconds):
     kinds = [jax.ShapeDtypeStruct(param.shape, F32) for param in params]
-    parts = 1
-
-    def cut(item):
-        block = (item.shape[0] // parts, *item.shape[1:])
-        return pl.BlockSpec(block, lambda i: (i, *[0] * (len(item.shape) - 1)))
-
-    def whole(item):
-        return pl.BlockSpec(item.shape, lambda i: (0,) * len(item.shape))
-
-    def specs(items):
-        return [cut(item) for item in items[:4]] + [whole(item) for item in items[4:]]
-
+    vmem = pl.BlockSpec(memory_space=pltpu.VMEM)
+    anywhere = pl.BlockSpec(memory_space=pl.ANY)
+    passed = [jax.ShapeDtypeStruct(item.shape, item.dtype) for item in (blk, gin)]
     return pl.pallas_call(
         functools.partial(adam_kernel, scale),
-        grid=(parts,),
-        out_shape=(*(kinds * 4), jax.ShapeDtypeStruct((3,), F32)),
-        in_specs=specs(grads) + specs(params) * 3,
-        out_specs=(*specs(kinds) * 4, pl.BlockSpec(memory_space=pltpu.SMEM)),
+        out_shape=(*(kinds * 4), jax.ShapeDtypeStruct((3,), F32), *passed),
+        in_specs=[anywhere] * 2 + [vmem] * 24,
+        out_specs=(*[vmem] * 24, pl.BlockSpec(memory_space=pltpu.SMEM), anywhere, anywhere),
+        scratch_shapes=[
+            pltpu.VMEM(blk.shape, blk.dtype),
+            pltpu.VMEM(gin.shape, gin.dtype),
+            pltpu.SemaphoreType.DMA((4,)),
+        ],
         compiler_params=pltpu.CompilerParams(vmem_limit_bytes=62 * 1024 * 1024),
-    )(*grads, *params, *firsts, *seconds)
+    )(blk, gin, *grads, *params, *firsts, *seconds)
 
 
 def stored(items):
@@ -1144,7 +1185,9 @@
         place = lax.axis_index(("dph", "dpl", "mp"))
         grads[4] = lax.dynamic_slice_in_dim(every, place * count, count, 0)
     scale = float(lax.axis_size("dph") * inner * LEN) ** (-0.5)
-    *results, rms_stats = run_adam(scale, grads, params, firsts, seconds)
+    *results, rms_stats, block_low, grad_input = run_adam(
+        scale, block_low, grad_input, grads, params, firsts, seconds
+    )
     outs = []
     for i in range(4):
         qkv, mix, up, down, bias, gains = results[6 * i : 6 * i + 6]

time: 173 us -> 165 us (0.954)
  Pallas kernels: 165 us -> 160 us
  local copies, waits for them, and re-layouts: 2.82 us -> 0 us
    pallas_call x1, Pallas kernels: 160 us -> 153 us  [run_block(): pl.pallas_call(functools.partial(block_kernel, last_hop), out_shape=(shap...]
    unnamed x6 -> x0, local copies, waits for them, and re-layouts: 2.82 us -> none
    pallas_call x1, Pallas kernels: 5.37 us -> 7.19 us  [run_adam(): pl.pallas_call(functools.partial(adam_kernel, scale), out_shape=(*kinds *...]
where the time goes in v4:
time: 165 us; the launch traced here: 162 us
  Pallas kernels  160 us (97%)
    pallas_call x1, Pallas kernels, run_block(): pl.pallas_call(functools.partial(block_kernel, last_hop), out_shape=(shap...  153 us
    pallas_call x1, Pallas kernels, run_adam(): pl.pallas_call(functools.partial(adam_kernel, scale), out_shape=(*kinds *...  7.19 us

profile of v4, /device:TPU:4, one launch (start us, length us, event | category | flops | bytes accessed | tf_op | source)
XLA Modules:
  0.0 161.5 jit_solution(2227159624654002425)
XLA Ops:
  1.3 152.7 %shard_map.412 = (bf16[512,768]{1,0:T(8,128)(2,1)}, f32[512,768]{1,0:T(8,128)}, f32[3,96,192]{2,1,0:T(8,128)}, f32[192,96]{1,0:T(8,128)}, f32[96,768]{1,0:T(8,12...) custom-call(s32[1]{0:T(128)S(6)} %copy.48.len_ref, bf16[512,768]{1,0:T(8,128)(2,1)} %bitcast.22, ...), custom_call_target="tpu_custom_call" | custom-call | tf_op jit(solution)/shard_map/pallas_call | solution.py:1011
  154.1 7.2 %shard_map.413 = (f32[3,96,192]{2,1,0:T(8,128)}, f32[192,96]{1,0:T(8,128)}, f32[96,768]{1,0:T(8,128)}, f32[96,768]{1,0:T(8,128)}, f32[64,256]{1,0:T(8,128)}, /*i...) custom-call(bf16[512,768]{1,0:T(8,128)(2,1)} %get-tuple-element.62.b, ...), custom_call_target="tpu_custom_call" | custom-call | tf_op jit(solution)/shard_map/pallas_call | solution.py:1140

commit v5 on v4

--- a/solution.py
+++ b/solution.py
@@ -27,41 +27,41 @@
 
 
 ROUTES = ((True, False), (False, False), (False, False), (True, False), (False, True))
-LINE_SUMS = (False, False, True, False)
+LINE_SUMS = (False, False, False, True)
 SCHEDULE = (
-    ("send_y", 1), ("send_x", 2), ("send_c", 3), ("send_c", 0), ("send_x", 0), ("send_x", 1),
-    ("send_c", 1), ("send_z", 0), ("send_y", 0), ("send_z", 1), ("norm",), ("x", 2, 0),
-    ("send_c", 2), ("y", 1, 0), ("send_z", 3), ("z", 0, 1), ("x", 0, 0), ("y", 0, 0),
-    ("x", 1, 0), ("z", 0, 2), ("y", 0, 1), ("x", 0, 1), ("z", 1, 1), ("send_z", 2), ("d", 1, 0),
-    ("d", 0, 0), ("z", 1, 2), ("z", 3, 1), ("z", 3, 2), ("x", 1, 1), ("y", 0, 2), ("z", 2, 1),
-    ("send_y", 2), ("z", 0, 3), ("z", 2, 2), ("x", 0, 2), ("z", 1, 3), ("z", 3, 3), ("y", 0, 3),
-    ("z", 2, 3), ("send_y", 3), ("halo",), ("d", 1, 1), ("y", 2, 0), ("y", 1, 1), ("y", 1, 2),
-    ("d", 0, 1), ("d", 0, 2), ("x", 2, 1), ("y", 1, 3), ("x", 1, 2), ("send_z", 4), ("d", 1, 2),
-    ("send_x", 3), ("x", 1, 3), ("z", 4, 1), ("y", 2, 1), ("y", 2, 2), ("z", 4, 2), ("y", 2, 3),
-    ("x", 2, 2), ("x", 2, 3), ("send_x", 4), ("d", 0, 3), ("d", 2, 0), ("d", 2, 1), ("x", 0, 3),
-    ("send_y", 4), ("x", 3, 0), ("y", 3, 0), ("y", 3, 1), ("z", 4, 3), ("send_c", 4),
-    ("d", 1, 3), ("y", 3, 2), ("y", 3, 3), ("x", 3, 1), ("repack",), ("proj", 0), ("proj", 1),
-    ("d", 2, 2), ("d", 2, 3), ("bands",), ("halow",), ("y", 4, 0), ("y", 4, 1), ("y", 4, 2),
-    ("x", 4, 0), ("x", 4, 1), ("mix", 0), ("mix", 1), ("y", 4, 3), ("x", 4, 2), ("att", 0),
-    ("att", 1), ("d", 4, 0), ("d", 3, 0), ("h", 1, 0), ("h", 1, 1), ("g", 1, 0), ("g", 1, 1),
-    ("cs", 2, 0), ("cs", 3, 0), ("d", 3, 1), ("h", 0, 0), ("h", 0, 1), ("d", 4, 1), ("g", 0, 0),
-    ("sum", 2, 0), ("g", 0, 1), ("d", 3, 2), ("x", 3, 2), ("x", 4, 3), ("x", 3, 3), ("d", 4, 2),
-    ("d", 4, 3), ("sum", 3, 0), ("d", 3, 3), ("h", 3, 0), ("h", 3, 1), ("g", 3, 0),
-    ("cs", 2, 1), ("g", 3, 1), ("cs", 3, 1), ("yt", 2, 1), ("yt", 2, 2), ("h", 2, 0),
-    ("h", 2, 1), ("g", 2, 0), ("sum", 2, 1), ("g", 2, 1), ("close", 0), ("close", 1),
-    ("sum", 3, 1), ("yt", 3, 1), ("yt", 3, 2), ("xe", 2, 1), ("ba", 0), ("ba", 1), ("bh",),
-    ("hb",), ("xe", 2, 2), ("bg", 0), ("bg", 1), ("unsk",), ("yt", 3, 3), ("yx", 3, 1),
-    ("mg", 0), ("gout",), ("unpack", 0), ("bk", 0), ("cs", 0, 1), ("by",), ("bk", 1), ("mg", 1),
-    ("bi", 0), ("yt", 3, 0), ("yt", 2, 3), ("cs", 0, 0), ("yx", 2, 1), ("yx", 2, 2),
-    ("xe", 2, 3), ("yx", 2, 3), ("sum", 0, 1), ("mg", 2), ("unpack", 1), ("cs", 1, 0),
-    ("bi", 1), ("ss", 0), ("sum", 0, 0), ("bt",), ("yx", 3, 2), ("yx", 3, 3), ("yx", 3, 0),
-    ("sw", 0), ("xe", 3, 1), ("xe", 3, 2), ("yx", 0, 1), ("yt", 0, 1), ("sum", 1, 0),
-    ("yt", 0, 2), ("cs", 1, 1), ("sum", 1, 1), ("yx", 2, 0), ("yx", 0, 2), ("xe", 3, 3),
-    ("xe", 3, 0), ("yx", 0, 3), ("xe", 0, 1), ("yt", 1, 1), ("yt", 0, 3), ("yx", 0, 0),
-    ("ss", 1), ("xe", 0, 2), ("xe", 0, 3), ("yt", 1, 2), ("yt", 1, 3), ("yx", 1, 1),
-    ("yt", 0, 0), ("sw", 1), ("ss", 2), ("yx", 1, 2), ("yx", 1, 3), ("xe", 1, 1), ("xe", 1, 2),
-    ("yx", 1, 0), ("xe", 1, 3), ("yt", 2, 0), ("xe", 0, 0), ("zt", 0), ("sw", 2), ("xe", 2, 0),
-    ("zt", 2), ("yt", 1, 0), ("ss", 3), ("zt", 3), ("xe", 1, 0), ("bc",), ("hopw",), ("zt", 1),
+    ("send_z", 0), ("send_c", 1), ("send_x", 0), ("send_x", 1), ("send_y", 2), ("send_z", 1),
+    ("send_x", 3), ("send_y", 0), ("send_x", 2), ("send_y", 3), ("x", 0, 0), ("y", 0, 0),
+    ("z", 1, 1), ("send_y", 1), ("x", 1, 0), ("send_z", 2), ("z", 0, 1), ("z", 0, 2),
+    ("z", 0, 3), ("z", 1, 2), ("z", 1, 3), ("send_z", 4), ("y", 3, 0), ("x", 1, 1), ("norm",),
+    ("y", 2, 0), ("z", 2, 1), ("send_c", 0), ("send_y", 4), ("x", 3, 0), ("z", 2, 2),
+    ("y", 1, 0), ("y", 1, 1), ("x", 1, 2), ("send_c", 3), ("d", 0, 0), ("send_z", 3),
+    ("x", 0, 1), ("y", 0, 1), ("y", 0, 2), ("y", 1, 2), ("x", 0, 2), ("z", 2, 3), ("send_x", 4),
+    ("z", 3, 1), ("d", 3, 0), ("z", 4, 1), ("x", 0, 3), ("d", 1, 0), ("d", 1, 1), ("send_c", 4),
+    ("y", 2, 1), ("y", 2, 2), ("y", 0, 3), ("halo",), ("y", 4, 0), ("x", 2, 0), ("x", 2, 1),
+    ("x", 1, 3), ("z", 3, 2), ("x", 2, 2), ("x", 2, 3), ("y", 2, 3), ("y", 1, 3), ("d", 1, 2),
+    ("d", 0, 1), ("d", 0, 2), ("z", 4, 2), ("z", 4, 3), ("y", 3, 1), ("z", 3, 3), ("y", 3, 2),
+    ("send_c", 2), ("d", 2, 0), ("d", 2, 1), ("d", 1, 3), ("d", 2, 2), ("d", 2, 3), ("d", 0, 3),
+    ("x", 3, 1), ("bands",), ("repack",), ("proj", 0), ("proj", 1), ("x", 4, 0), ("y", 4, 1),
+    ("y", 4, 2), ("halow",), ("y", 4, 3), ("x", 4, 1), ("mix", 0), ("mix", 1), ("att", 0),
+    ("x", 3, 2), ("y", 3, 3), ("att", 1), ("h", 1, 0), ("h", 1, 1), ("d", 4, 0), ("g", 1, 0),
+    ("g", 1, 1), ("cs", 2, 0), ("cs", 3, 0), ("h", 0, 0), ("h", 0, 1), ("g", 0, 0), ("d", 4, 1),
+    ("sum", 2, 0), ("d", 4, 2), ("g", 0, 1), ("x", 4, 2), ("x", 4, 3), ("d", 3, 1), ("d", 3, 2),
+    ("d", 3, 3), ("sum", 3, 0), ("x", 3, 3), ("d", 4, 3), ("h", 3, 0), ("h", 3, 1),
+    ("yt", 2, 1), ("g", 3, 0), ("cs", 2, 1), ("g", 3, 1), ("cs", 3, 1), ("h", 2, 0),
+    ("h", 2, 1), ("g", 2, 0), ("g", 2, 1), ("sum", 3, 1), ("close", 0), ("close", 1), ("ba", 0),
+    ("sum", 2, 1), ("ba", 1), ("yt", 2, 2), ("yt", 2, 3), ("bh",), ("bg", 0), ("bg", 1),
+    ("yt", 3, 1), ("xe", 3, 1), ("yt", 3, 2), ("xe", 3, 2), ("unsk",), ("hb",), ("by",),
+    ("mg", 0), ("gout",), ("unpack", 0), ("cs", 0, 1), ("bk", 0), ("sum", 0, 1), ("yx", 2, 1),
+    ("bk", 1), ("mg", 1), ("cs", 0, 0), ("yt", 3, 3), ("xe", 3, 3), ("yx", 2, 2), ("mg", 2),
+    ("yx", 2, 3), ("unpack", 1), ("cs", 1, 1), ("sum", 1, 1), ("yx", 2, 0), ("bt",),
+    ("sum", 0, 0), ("cs", 1, 0), ("yx", 3, 1), ("bi", 0), ("bi", 1), ("ss", 0), ("yx", 3, 2),
+    ("yt", 2, 0), ("xe", 2, 1), ("xe", 2, 2), ("xe", 2, 3), ("sum", 1, 0), ("sw", 0), ("ss", 1),
+    ("yx", 3, 3), ("yx", 3, 0), ("yx", 0, 1), ("yx", 0, 2), ("yx", 0, 3), ("yx", 0, 0),
+    ("yt", 0, 1), ("xe", 0, 1), ("xe", 2, 0), ("yt", 0, 2), ("yt", 0, 3), ("sw", 1),
+    ("yx", 1, 1), ("ss", 2), ("yx", 1, 2), ("yx", 1, 3), ("yt", 0, 0), ("xe", 0, 2),
+    ("xe", 0, 3), ("xe", 0, 0), ("yx", 1, 0), ("bc",), ("yt", 1, 1), ("yt", 1, 2), ("xe", 1, 1),
+    ("xe", 1, 2), ("sw", 2), ("hopw",), ("yt", 1, 3), ("yt", 1, 0), ("xe", 1, 3), ("ss", 3),
+    ("zt", 2), ("yt", 3, 0), ("xe", 3, 0), ("zt", 3), ("zt", 0), ("xe", 1, 0), ("zt", 1),
     ("se",),
 )
 

time: 165 us -> 162 us (0.982)
  the two profiles are of different devices: /device:TPU:4 before, /device:TPU:1 now
where the time goes in v5:
time: 162 us; the launch traced here: 159 us
  Pallas kernels  158 us (98%)
  between operations  1.62 us (1%)
    pallas_call x1, Pallas kernels, run_block(): pl.pallas_call(functools.partial(block_kernel, last_hop), out_shape=(shap...  150 us
    pallas_call x1, Pallas kernels, run_adam(): pl.pallas_call(functools.partial(adam_kernel, scale), out_shape=(*kinds *...  7.19 us

profile of v5, /device:TPU:1, one launch (start us, length us, event | category | flops | bytes accessed | tf_op | source)
XLA Modules:
  0.0 159.3 jit_solution(12214379568288855125)
XLA Ops:
  1.3 150.4 %shard_map.412 = (bf16[512,768]{1,0:T(8,128)(2,1)}, f32[512,768]{1,0:T(8,128)}, f32[3,96,192]{2,1,0:T(8,128)}, f32[192,96]{1,0:T(8,128)}, f32[96,768]{1,0:T(8,12...) custom-call(s32[1]{0:T(128)S(6)} %copy.48.len_ref, bf16[512,768]{1,0:T(8,128)(2,1)} %bitcast.22, ...), custom_call_target="tpu_custom_call" | custom-call | tf_op jit(solution)/shard_map/pallas_call | solution.py:1011
  151.8 7.2 %shard_map.413 = (f32[3,96,192]{2,1,0:T(8,128)}, f32[192,96]{1,0:T(8,128)}, f32[96,768]{1,0:T(8,128)}, f32[96,768]{1,0:T(8,128)}, f32[64,256]{1,0:T(8,128)}, /*i...) custom-call(bf16[512,768]{1,0:T(8,128)(2,1)} %get-tuple-element.62.b, ...), custom_call_target="tpu_custom_call" | custom-call | tf_op jit(solution)/shard_map/pallas_call | solution.py:1140
